TPU v7x, 32 devices: a whole 2x2x4 slice. The times are simulated.
32 devices in a mesh: row: 2 (over core), col: 8 (over z, y), layer: 2 (over x).
Axes of the slice: x: 2, y: 2, z: 4, core: 2. Of those that a mesh axis runs over, the one named last changes fastest.
Arguments:
- flow_cols: int32 [16, 2, 8], P('row', 'layer', 'col'), may hold values from 0 to 64, as said below
- flow_vals: bfloat16 [16, 2, 8, 128, 128], P('row', 'layer', 'col'), may hold values from -22 to 22
- window_flow: bfloat16 [2, 8192, 4096], P('layer', 'row', 'col'), may hold values from -0.396875 to 0.396875
Outputs:
- flow_next: float32 [2048, 4096], P(('row', 'layer'), 'col')
Inputs may be any that keep to these rules, and one draw needn't show every extreme that they name: `flow_cols`: an entry 64 marks an empty slot; the live entries of one block row and layer are distinct; every block row and layer has at least one live slot, and some block row and layer has all 8 slots live.
All inputs are finite; a program needn't handle non-finite values.
Results may differ from a plain program's by a relative error of at most 0.0003.
Values may be sent and summed in bfloat16 or wider, within the bound.
No kernel may reach another device: no remote copies, remote signals or barrier semaphores. Data moves between devices by JAX's collectives and lax.ppermute only.
A program may use at most 128 MiB of HBM per device.

v0:
```python
import jax
import jax.numpy as jnp
from jax import lax
from jax.sharding import PartitionSpec as P


def body(flow_cols, flow_vals, window_flow):
    window_panel = lax.all_gather(window_flow[0], "row", axis=0, tiled=True)
    block_size = flow_vals.shape[-1]
    block_count = window_panel.shape[0] // block_size
    row_blocks = flow_vals.shape[0]
    all_cols, all_vals = (
        lax.all_gather(flow_cols, "col", axis=2, tiled=True),
        lax.all_gather(flow_vals, "col", axis=2, tiled=True),
    )
    slot_cols = all_cols[:, 0, :]
    slot_vals = all_vals[:, 0]
    column_ids = jnp.arange(block_count, dtype=jnp.int32)
    one_hot = (slot_cols[:, :, None] == column_ids[None, None, :]).astype(jnp.bfloat16)
    dense_row = jnp.einsum(
        "isab,isk->iakb", slot_vals, one_hot, preferred_element_type=jnp.bfloat16
    )
    dense_row = dense_row.reshape(row_blocks * block_size, block_count * block_size)
    expanded = jnp.dot(dense_row, window_panel, preferred_element_type=jnp.float32)
    total_rows = row_blocks * block_size * lax.axis_size("row")
    row_share = lax.psum_scatter(expanded, "layer", scatter_dimension=0, tiled=True)
    squares = row_share * row_share
    column_sums = lax.psum(jnp.sum(squares, axis=0), ("row", "layer"))
    return squares / (column_sums / total_rows + 1e-06)


def solution(mesh):
    placed = (
        P("row", "layer", "col"),
        P("row", "layer", "col", None, None),
        P("layer", "row", "col"),
    )
    return jax.shard_map(
        body, mesh=mesh, in_specs=placed, out_specs=P(("row", "layer"), "col"), check_vma=False
    )
```

profile of v0, /device:TPU:0, one launch (start us, length us, event | category | flops | bytes accessed | tf_op | source)
XLA Modules:
  0.0 155.8 jit_solution(2234007701143787164)
XLA Ops:
  6.5 0.0 all-gather.4.cloned.1.call-start
  6.5 0.7 all-gather.4.cloned.1.call-update
  7.3 0.0 all-gather.6.cloned.1.call-start
  7.3 0.7 all-gather.6.cloned.1.call-update
  8.0 0.0 reduce-scatter.2.cloned.1.call-start
  8.1 22.4 %all_gather.9 = s32[8,1,8]{0,1,2:T(1,128)S(1)} all-gather(s32[8,1,1]{0,1,2:T(1,128)} %bitcast.23), channel_id=1, replica_groups=mesh['row'=2,'col'=8,'layer'=2] {'col'}, dimensions={2}, use_global_device_ids=true | all-gather | bytes 288 | tf_op jit(solution)/shard_map/all_gather | solution.py:13
  30.4 0.1 copy.7
  30.5 31.2 %all-gather.4.cloned.1.call-done = bf16[8,1,8,128,128]{4,3,1,0,2:T(8,128)(2,1)} async-done(((bf16[8,1,1,128,128]{4,3,1,0,2:T(8,128)(2,1)}), bf16[8,1,8,128,128]{4,3,1,0,2:T(8,128)(2,1)}) %all-gather.4.cloned.1.call-update) | async-done | bytes 2097168 | tf_op jit(solution)/shard_map/all_gather | solution.py:14
  61.7 14.9 %fusion.4 = bf16[8,64,128,128]{3,1,2,0:T(8,128)(2,1)} fusion(bf16[8,1,8,128,128]{4,3,1,0,2:T(8,128)(2,1)} %all-gather.4.cloned.1.call-done, s32[8,8]{1,0:T(8,128)S(1)} %bitcast.22), kind=kOutput, calls=%fused_computation.4 | convolution fusion | flops 134221824 | bytes 18874624 | tf_op jit(solution)/shard_map/isab,isk->iakb/dot_general | solution.py:20
  76.6 5.0 %all-gather.6.cloned.1.call-done = bf16[1,8192,512]{2,1,0:T(8,128)(2,1)} async-done(((bf16[1,4096,512]{2,1,0:T(8,128)(2,1)}), bf16[1,8192,512]{2,1,0:T(8,128)(2,1)}) %all-gather.6.cloned.1.call-update) | async-done | bytes 8388624 | tf_op jit(solution)/shard_map/all_gather | solution.py:8
  81.6 24.6 %fusion = f32[1024,512]{1,0:T(8,128)} fusion(bf16[128,8,64,128]{3,2,1,0:T(8,128)(2,1)} %bitcast.20, bf16[1,8192,512]{2,1,0:T(8,128)(2,1)} %all-gather.6.cloned.1.call-done), kind=kOutput, calls=%fused_computation | convolution fusion | flops 8589934592 | bytes 27262976 | tf_op jit(solution)/shard_map/dot_general | solution.py:24
  106.1 0.0 reduce-scatter.2.cloned.1.call-update
  106.2 33.2 %reduce-scatter.2.cloned.1.call-done = f32[512,512]{1,0:T(8,128)} async-done(((f32[1024,512]{1,0:T(8,128)}), f32[512,512]{1,0:T(8,128)}) %reduce-scatter.2.cloned.1.call-update) | async-done | bytes 1048592 | tf_op jit(solution)/shard_map/reduce_scatter | solution.py:26
  139.3 1.3 multiply_reduce_fusion
  140.7 6.3 %psum.7 = f32[512]{0:T(512)S(1)} all-reduce(f32[512]{0:T(512)S(1)} %multiply_reduce_fusion), channel_id=1, replica_groups=mesh['row'=2,'col'=8,'layer'=2] {'row','layer'}, use_global_device_ids=true, to_apply=%region_2.0 | all-reduce | flops 512 | bytes 4096 | tf_op jit(solution)/shard_map/psum | solution.py:28
  147.0 2.4 %multiply_divide_fusion = f32[512,512]{1,0:T(8,128)} fusion(f32[512,512]{1,0:T(8,128)} %reduce-scatter.2.cloned.1.call-done, f32[512]{0:T(512)S(1)} %multiply_add_fusion), kind=kLoop, calls=%fused_computation.7 | loop fusion | flops 524288 | bytes 2099200 | tf_op jit(solution)/shard_map/div | solution.py:29
  (1 shorter events, 0.0 us)
Async XLA Ops:
  6.5 55.1 %all-gather.4.cloned.1.call-start = ((), (), s32[]{:S(2)}) async-start(), calls=%async_computation.1 | async-start | bytes 2359296 | tf_op jit(solution)/shard_map/all_gather | solution.py:14
  7.3 74.3 %all-gather.6.cloned.1.call-start = ((), (), s32[]{:S(2)}) async-start(), calls=%async_computation.3 | async-start | bytes 12582912 | tf_op jit(solution)/shard_map/all_gather | solution.py:8
  8.0 131.3 %reduce-scatter.2.cloned.1.call-start = ((), (), s32[]{:S(2)}) async-start(), calls=%async_computation.2 | async-start | bytes 3145728 | tf_op jit(solution)/shard_map/reduce_scatter | solution.py:26
Sparse Core Ops, SparseCore 0:
  9.5 52.1 all-gather.3
  63.2 18.3 all-gather.5
  106.3 32.9 reduce-scatter.1
where the time goes:
time: 156 us
  waiting for transfers between devices  70.7 us (45%)
  matrix products  39.5 us (25%)
  blocking collectives  28.7 us (18%)
  between operations  13.1 us (8%)
  other arithmetic  3.7 us (2%)
    reduce_scatter x1, waiting for transfers between devices, body(): lax.psum_scatter(expanded, 'layer', scatter_dimension=0, tiled=True)  33.2 us
    all_gather x1, waiting for transfers between devices, body(): lax.all_gather(flow_vals, 'col', axis=2, tiled=True)  31.2 us
    dot_general x1, matrix products, body(): jnp.dot(dense_row, window_panel, preferred_element_type=jnp.float32)  24.6 us
    all_gather x1, blocking collectives, body(): lax.all_gather(flow_cols, 'col', axis=2, tiled=True)  22.4 us
    dot_general x1, matrix products, body(): jnp.einsum('isab,isk->iakb', slot_vals, one_hot, preferred_element_type=j...  14.9 us
    psum x1, blocking collectives, body(): column_sums = lax.psum(jnp.sum(squares, axis=0), ('row', 'layer'))  6.3 us
    all_gather x1, waiting for transfers between devices, body(): window_panel = lax.all_gather(window_flow[0], 'row', axis=0, tiled=True)  5 us
  transfers between devices with their start and end apart: 3, of which 3 were waited for; matrix products, arithmetic and copies ran while one was open for 10% of the time, Pallas kernels for 0%

commit v1 on v0

v1 whole, which is shorter than its diff:
```python
import functools

import jax
import jax.numpy as jnp
from jax import lax
from jax.experimental import pallas as pl
from jax.experimental.pallas import tpu as pltpu
from jax.sharding import PartitionSpec as P

CODE_SPAN = 250.0
CODE_MID = 125.0
LOG2E = 1.4426950408889634
ID_ROWS = 16
VMEM_BYTES = 48 * 1024 * 1024


def pack_kernel(cols_ref, layer_ref, vals_ref, send_ref, keep_ref, ids, sems):
    rows = send_ref.shape[0] - ID_ROWS
    block = vals_ref.shape[1]
    count = rows // block
    layer = layer_ref[0]
    copies = []
    for k, (out, part) in enumerate(((send_ref, 1 - layer), (keep_ref, layer))):
        copies.append(
            pltpu.make_async_copy(
                vals_ref.at[pl.ds(pl.multiple_of(part * rows, block), rows)],
                out.at[pl.ds(0, rows)],
                sems.at[2 * k],
            )
        )
        copies[-1].start()
        lanes = lax.broadcasted_iota(jnp.int32, (ID_ROWS, block), 1)
        line = jnp.zeros((ID_ROWS, block), jnp.int32)
        for j in range(count):
            line = jnp.where(lanes == j, cols_ref[part * count + j, 0, 0], line)
        ids[k] = line.astype(jnp.float32).astype(jnp.bfloat16)
        copies.append(
            pltpu.make_async_copy(ids.at[k], out.at[pl.ds(rows, ID_ROWS)], sems.at[2 * k + 1])
        )
        copies[-1].start()
    for copy in copies:
        copy.wait()


def products(items, row, own, other, flat, blocks, ids_v, ids_s, sem_id, sem_a, sem_b, finish):
    block = flat.shape[1] // len(items)
    rows = flat.shape[0]
    count = rows // block
    slots = len(items)
    half = own.shape[0] // block
    for s, item in enumerate(items):
        ids_v[pl.ds(s, 1)] = item[rows : rows + 1, :].astype(jnp.float32).astype(jnp.int32)
    to_scalar = pltpu.make_async_copy(ids_v, ids_s, sem_id)
    to_scalar.start()
    for s, item in enumerate(items):
        flat[:, s * block : (s + 1) * block] = item[0:rows, :]
    to_scalar.wait()
    depth = blocks.shape[0]

    def fetch(j):
        for s in range(slots):
            col = jnp.minimum(ids_s[s, j], 2 * half - 1)
            local = lax.rem(col, half)
            here = lax.div(col, half) == row
            where = pl.ds(pl.multiple_of(local * block, block), block)
            target = blocks.at[j % depth, pl.ds(s * block, block)]

            @pl.when(here)
            def _():
                pltpu.make_async_copy(own.at[where], target, sem_b.at[j % depth]).start()

            @pl.when(jnp.logical_not(here))
            def _():
                pltpu.make_async_copy(other.at[where], target, sem_b.at[j % depth]).start()

    for j in range(min(depth, count)):
        fetch(j)
    for j in range(count):
        pieces = []
        for s in range(slots):
            live = jnp.where(ids_s[s, j] < 2 * half, 1.0, 0.0).astype(jnp.float32)
            piece = flat[j * block : (j + 1) * block, s * block : (s + 1) * block]
            pieces.append((piece.astype(jnp.float32) * live).astype(jnp.bfloat16))
        whole = blocks.at[j % depth]
        pltpu.make_async_copy(whole, whole, sem_b.at[j % depth]).wait()
        left = jnp.concatenate(pieces, axis=1)
        finish(j, jnp.dot(left, blocks[j % depth], preferred_element_type=jnp.float32))
        if j + depth < count:
            fetch(j + depth)


def send_kernel(slots, row_ref, *refs):
    items, (own, other, code_ref, flat, blocks, ids_v, ids_s, total, sem_id, sem_b) = refs[:slots], refs[slots:]
    block = flat.shape[1] // slots
    rows = flat.shape[0]

    def finish(j, value):
        total[j * block : (j + 1) * block, :] = value

    products(items, row_ref[0], own, other, flat, blocks, ids_v, ids_s, sem_id, None, sem_b, finish)
    most = jnp.max(jnp.abs(total[...]), axis=0, keepdims=True)
    scale = (most * 1.01 + 1e-30).astype(jnp.bfloat16)
    inverse = CODE_SPAN / scale.astype(jnp.float32)
    for j in range(rows // block):
        value = total[j * block : (j + 1) * block, :]
        size = jnp.exp((jnp.abs(value) * inverse - CODE_MID) * (1.0 / LOG2E))
        code_ref[j * block : (j + 1) * block, :] = jnp.where(value < 0, -size, size).astype(jnp.bfloat16)
    code_ref[rows : rows + ID_ROWS, :] = jnp.broadcast_to(scale, (ID_ROWS, scale.shape[1]))


def keep_kernel(slots, row_ref, *refs):
    items, rest = refs[:slots], refs[slots:]
    own, other, code_ref, square_ref, sum_ref, flat, blocks, ids_v, ids_s, sem_id, sem_b = rest
    block = flat.shape[1] // slots
    rows = flat.shape[0]
    scale = code_ref[rows : rows + 1, :].astype(jnp.float32) * (1.0 / CODE_SPAN)
    sums = []

    def finish(j, value):
        code = code_ref[j * block : (j + 1) * block, :].astype(jnp.float32)
        size = (jnp.log(jnp.abs(code)) * LOG2E + CODE_MID) * scale
        full = value + jnp.where(code < 0, -size, size)
        square = full * full
        square_ref[j * block : (j + 1) * block, :] = square
        sums.append(jnp.sum(square, axis=0, keepdims=True))

    products(items, row_ref[0], own, other, flat, blocks, ids_v, ids_s, sem_id, None, sem_b, finish)
    sum_ref[...] = functools.reduce(jnp.add, sums)


def ring_of(mesh):
    size = mesh.shape["col"]
    if size != 8:
        return list(range(size))
    return [0, 2, 4, 6, 7, 5, 3, 1]


def solution(mesh):
    size = mesh.shape["col"]
    order = ring_of(mesh)
    ahead = [(order[i], order[(i + 1) % size]) for i in range(size)]
    back = [(b, a) for a, b in ahead]
    swap = [(0, 1), (1, 0)]
    vmem = pl.BlockSpec(memory_space=pltpu.VMEM)
    smem = pl.BlockSpec(memory_space=pltpu.SMEM)
    anywhere = pl.BlockSpec(memory_space=pl.ANY)

    def gather(item, last_ahead):
        items = [item]
        front = rear = item
        for step in range(1, size // 2 + 1):
            if step < size // 2 or last_ahead:
                front = lax.ppermute(front, "col", ahead)
                items.append(front)
            if step < size // 2 or not last_ahead:
                rear = lax.ppermute(rear, "col", back)
                items.append(rear)
        return items

    def gather_all(item):
        stacked = lax.all_gather(item, "col", axis=0)
        return [stacked[i] for i in range(size)]

    def body(flow_cols, flow_vals, window_flow):
        block = flow_vals.shape[-1]
        count = flow_vals.shape[0] // 2
        rows = count * block
        own = window_flow[0]
        columns = own.shape[1]
        other = lax.ppermute(own, "row", swap)
        row = lax.axis_index("row").astype(jnp.int32).reshape(1)
        layer = lax.axis_index("layer").astype(jnp.int32).reshape(1)
        item = jax.ShapeDtypeStruct((rows + ID_ROWS, block), flow_vals.dtype)
        send, keep = pl.pallas_call(
            pack_kernel,
            out_shape=(item, item),
            in_specs=[smem, smem, anywhere],
            out_specs=(anywhere, anywhere),
            scratch_shapes=[pltpu.VMEM((2, ID_ROWS, block), flow_vals.dtype), pltpu.SemaphoreType.DMA((4,))],
        )(flow_cols, layer, flow_vals.reshape(2 * rows, block))
        if size == 8:
            sends, keeps = gather(send, True), gather(keep, False)
        else:
            sends, keeps = gather_all(send), gather_all(keep)
        depth = count if size <= 8 else 1
        scratch = [
            pltpu.VMEM((rows, size * block), flow_vals.dtype),
            pltpu.VMEM((depth, size * block, columns), own.dtype),
            pltpu.VMEM((max(size, 8), block), jnp.int32),
            pltpu.SMEM((max(size, 8), block), jnp.int32),
        ]
        sems = [pltpu.SemaphoreType.DMA(()), pltpu.SemaphoreType.DMA((depth,))]
        params = pltpu.CompilerParams(vmem_limit_bytes=VMEM_BYTES)
        code = pl.pallas_call(
            functools.partial(send_kernel, size),
            out_shape=jax.ShapeDtypeStruct((rows + ID_ROWS, columns), jnp.bfloat16),
            in_specs=[smem] + [vmem] * size + [anywhere] * 2,
            out_specs=vmem,
            scratch_shapes=scratch + [pltpu.VMEM((rows, columns), jnp.float32)] + sems,
            compiler_params=params,
        )(row, *sends, own, other)
        code = lax.ppermute(code, "layer", swap)
        square, sums = pl.pallas_call(
            functools.partial(keep_kernel, size),
            out_shape=(
                jax.ShapeDtypeStruct((rows, columns), jnp.float32),
                jax.ShapeDtypeStruct((1, columns), jnp.float32),
            ),
            in_specs=[smem] + [vmem] * size + [anywhere] * 2 + [vmem],
            out_specs=(vmem, vmem),
            scratch_shapes=scratch + sems,
            compiler_params=params,
        )(row, *keeps, own, other, code)
        sums = sums + lax.ppermute(sums, "row", swap)
        sums = sums + lax.ppermute(sums, "layer", swap)
        total_rows = rows * lax.axis_size("row") * lax.axis_size("layer")
        return square * (1.0 / (sums / total_rows + 1e-6))

    placed = (
        P("row", "layer", "col"),
        P("row", "layer", "col", None, None),
        P("layer", "row", "col"),
    )
    return jax.shard_map(body, mesh=mesh, in_specs=placed, out_specs=P(("row", "layer"), "col"), check_vma=False)
```

time: 156 us -> 70.9 us (0.45)
  waiting for transfers between devices: 70.7 us -> 27.9 us
  matrix products: 39.5 us -> 0 us
  blocking collectives: 28.7 us -> 0 us
  starting transfers between devices: 0.08 us -> 18.3 us
  Pallas kernels: 0 us -> 17.8 us
  between operations: 13.1 us -> 0.06 us
  local copies, waits for them, and re-layouts: 0.07 us -> 4.41 us
  other arithmetic: 3.7 us -> 1.11 us
    dot_general x2 -> x0, matrix products: 39.5 us -> none  [the longest x1 24.6 us: body(): jnp.dot(dense_row, window_panel, preferred_element_type=jnp.float32)]
    all_gather x2 -> x0, waiting for transfers between devices: 36.2 us -> none  [the longest x1 31.2 us: body(): lax.all_gather(flow_vals, 'col', axis=2, tiled=True)]
    reduce_scatter x1 -> x0, waiting for transfers between devices: 33.2 us -> none  [body(): lax.psum_scatter(expanded, 'layer', scatter_dimension=0, tiled=True)]
    ppermute x0 -> x18, waiting for transfers between devices: none -> 27.9 us  [the longest x7 22.5 us: gather(): front = lax.ppermute(front, 'col', ahead)]
    all_gather x1 -> x0, blocking collectives: 22.4 us -> none  [body(): lax.all_gather(flow_cols, 'col', axis=2, tiled=True)]
    ppermute x0 -> x18, starting transfers between devices: none -> 18.3 us  [the longest x7 12.1 us: gather(): front = lax.ppermute(front, 'col', ahead)]
    pallas_call x0 -> x3, Pallas kernels: none -> 17.8 us  [the longest x1 9.8 us: body(): pl.pallas_call(pack_kernel, out_shape=(item, item), in_specs=[smem, smem,...]
    psum x1 -> x0, blocking collectives: 6.3 us -> none  [body(): column_sums = lax.psum(jnp.sum(squares, axis=0), ('row', 'layer'))]
  transfers between devices with their start and end apart: 3 -> 18, of which waited for: 3 -> 11; matrix products, arithmetic and copies ran while one was open for 10% -> 2% of each run, Pallas kernels for 0% -> 21%
where the time goes in v1:
time: 70.9 us; the launch traced here: 69.6 us
  waiting for transfers between devices  27.9 us (39%)
  starting transfers between devices  18.3 us (26%)
  Pallas kernels  17.8 us (25%)
  local copies, waits for them, and re-layouts  4.41 us (6%)
  other arithmetic  1.11 us (2%)
    ppermute x7, waiting for transfers between devices, gather(): front = lax.ppermute(front, 'col', ahead)  22.5 us
    ppermute x7, starting transfers between devices, gather(): front = lax.ppermute(front, 'col', ahead)  12.1 us
    pallas_call x1, Pallas kernels, body(): pl.pallas_call(pack_kernel, out_shape=(item, item), in_specs=[smem, smem,...  9.8 us
    pallas_call x1, Pallas kernels, body(): pl.pallas_call(functools.partial(send_kernel, size), out_shape=jax.ShapeD...  4.68 us
    unnamed x7, local copies, waits for them, and re-layouts  4.41 us
    pallas_call x1, Pallas kernels, body(): pl.pallas_call(functools.partial(keep_kernel, size), out_shape=(jax.Shape...  3.34 us
    ppermute x7, starting transfers between devices, gather(): rear = lax.ppermute(rear, 'col', back)  2.69 us
    ppermute x1, waiting for transfers between devices, body(): sums = sums + lax.ppermute(sums, 'layer', swap)  2.15 us
  transfers between devices with their start and end apart: 18, of which 11 were waited for; matrix products, arithmetic and copies ran while one was open for 2% of the time, Pallas kernels for 21%

profile of v1, /device:TPU:0, one launch (start us, length us, event | category | flops | bytes accessed | tf_op | source)
XLA Modules:
  0.0 69.6 jit_solution(14001634643152671849)
XLA Ops:
  0.5 1.3 %copy.4.cols_ref = s32[8,1,1]{2,1,0:T(1,128)} copy(s32[8,1,1]{0,2,1:T(1,128)} %param.3) | data formatting | bytes 64 | tf_op args[0]
  1.8 9.8 %shard_map.37 = (bf16[528,128]{1,0:T(8,128)(2,1)}, bf16[528,128]{1,0:T(8,128)(2,1)}) custom-call(s32[8,1,1]{2,1,0:T(1,128)} %copy.4.cols_ref, s32[1]{0:T(128)} %bitcast.1.layer_ref, bf16[1024,128]{1,0:T(8,128)(2,1)} %bitcast.8), custom_call_target="tpu_custom_call" | custom-call | tf_op jit(solution)/shard_map/pallas_call | solution.py:174
  11.6 2.6 %collective-permute-start.8 = (bf16[528,128]{1,0:T(8,128)(2,1)}, bf16[528,128]{1,0:T(8,128)(2,1)S(1)}, u32[]{:S(2)}, u32[]{:S(2)}) collective-permute-start(bf16[528,128]{1,0:T(8,128)(2,1)} %get-tuple-element.10.refs_0_), channel_id=1, source_target_pairs={{0,4},{4,8},{8,12},{12,14},{14,10},{10,6},{6,2},{2,0},{1,5},{5,9},... | collective-permute-start | bytes 405512 | tf_op jit(solution)/shard_map/ppermute | solution.py:153
  14.2 4.4 %collective-permute-done.8.refs_1_ = bf16[528,128]{1,0:T(8,128)(2,1)S(1)} collective-permute-done((bf16[528,128]{1,0:T(8,128)(2,1)}, bf16[528,128]{1,0:T(8,128)(2,1)S(1)}, u32[]{:S(2)}, u32[]{:S(2)}) %collective-permute-start.8) | collective-permute-done | bytes 135200 | tf_op jit(solution)/shard_map/ppermute | solution.py:153
  18.6 1.8 %collective-permute-start.10 = (bf16[528,128]{1,0:T(8,128)(2,1)S(1)}, bf16[528,128]{1,0:T(8,128)(2,1)S(1)}, u32[]{:S(2)}, u32[]{:S(2)}) collective-permute-start(bf16[528,128]{1,0:T(8,128)(2,1)S(1)} %collective-permute-done.8.refs_1_), channel_id=1, source_target_pairs={{0,4},{4,8},{8,12},{12,14},{14,10},{10,6},{6,2},{2,0},{1,5},{5,9},... | collective-permute-start | bytes 405512 | tf_op jit(solution)/shard_map/ppermute | solution.py:153
  20.6 3.4 %collective-permute-done.10.refs_3_ = bf16[528,128]{1,0:T(8,128)(2,1)S(1)} collective-permute-done((bf16[528,128]{1,0:T(8,128)(2,1)S(1)}, bf16[528,128]{1,0:T(8,128)(2,1)S(1)}, u32[]{:S(2)}, u32[]{:S(2)}) %collective-permute-start.10) | collective-permute-done | bytes 135200 | tf_op jit(solution)/shard_map/ppermute | solution.py:153
  24.0 1.6 %collective-permute-start.12 = (bf16[528,128]{1,0:T(8,128)(2,1)S(1)}, bf16[528,128]{1,0:T(8,128)(2,1)S(1)}, u32[]{:S(2)}, u32[]{:S(2)}) collective-permute-start(bf16[528,128]{1,0:T(8,128)(2,1)S(1)} %collective-permute-done.10.refs_3_), channel_id=1, source_target_pairs={{0,4},{4,8},{8,12},{12,14},{14,10},{10,6},{6,2},{2,0},{1,5},{5,9},... | collective-permute-start | bytes 405512 | tf_op jit(solution)/shard_map/ppermute | solution.py:153
  26.1 3.0 %collective-permute-done.12.refs_5_ = bf16[528,128]{1,0:T(8,128)(2,1)S(1)} collective-permute-done((bf16[528,128]{1,0:T(8,128)(2,1)S(1)}, bf16[528,128]{1,0:T(8,128)(2,1)S(1)}, u32[]{:S(2)}, u32[]{:S(2)}) %collective-permute-start.12) | collective-permute-done | bytes 135200 | tf_op jit(solution)/shard_map/ppermute | solution.py:153
  29.0 1.6 %collective-permute-start.14 = (bf16[528,128]{1,0:T(8,128)(2,1)S(1)}, bf16[528,128]{1,0:T(8,128)(2,1)S(1)}, u32[]{:S(2)}, u32[]{:S(2)}) collective-permute-start(bf16[528,128]{1,0:T(8,128)(2,1)S(1)} %collective-permute-done.12.refs_5_), channel_id=1, source_target_pairs={{0,4},{4,8},{8,12},{12,14},{14,10},{10,6},{6,2},{2,0},{1,5},{5,9},... | collective-permute-start | bytes 405512 | tf_op jit(solution)/shard_map/ppermute | solution.py:153
  31.1 3.0 %collective-permute-done.14.refs_7_ = bf16[528,128]{1,0:T(8,128)(2,1)S(1)} collective-permute-done((bf16[528,128]{1,0:T(8,128)(2,1)S(1)}, bf16[528,128]{1,0:T(8,128)(2,1)S(1)}, u32[]{:S(2)}, u32[]{:S(2)}) %collective-permute-start.14) | collective-permute-done | bytes 135200 | tf_op jit(solution)/shard_map/ppermute | solution.py:153
  34.1 2.2 %copy-done = bf16[1,4096,512]{2,1,0:T(8,128)(2,1)S(1)} copy-done((bf16[1,4096,512]{2,1,0:T(8,128)(2,1)S(1)}, bf16[1,4096,512]{2,1,0:T(8,128)(2,1)}, u32[]{:S(2)}) %copy-start) | copy-done | bytes 4194328
  37.2 4.7 %shard_map.38 = bf16[528,512]{1,0:T(8,128)(2,1)S(1)} custom-call(s32[1]{0:T(128)} %bitcast.row_ref, bf16[528,128]{1,0:T(8,128)(2,1)S(1)} %copy-done.2, bf16[528,128]{1,0:T(8,128)(2,1)S(1)} %collective-permute-done.8.refs_1_, bf16[528,128]{1,0:T(8,128)(2,1)S(1)} %collective-permute-done.9.refs_2_, bf16[528,128]{1,0:T(8,128)(2,1)S(1)} %collective-permute-done.10.refs_3_, ...), custom_call_target="tpu_custom_call" | custom-call | tf_op jit(solution)/shard_map/pallas_call | solution.py:194
  41.9 1.5 %collective-permute-start.15 = (bf16[528,512]{1,0:T(8,128)(2,1)S(1)}, bf16[528,512]{1,0:T(8,128)(2,1)S(1)}, u32[]{:S(2)}, u32[]{:S(2)}) collective-permute-start(bf16[528,512]{1,0:T(8,128)(2,1)S(1)} %shard_map.38), channel_id=1, source_target_pairs={{0,1},{1,0},{2,3},{3,2},{4,5},{5,4},{6,7},{7,6},{8,9},{9,8},{10,11... | collective-permute-start | bytes 1622024 | tf_op jit(solution)/shard_map/ppermute | solution.py:202
  43.4 1.5 %collective-permute-start = (bf16[528,128]{1,0:T(8,128)(2,1)S(1)}, bf16[528,128]{1,0:T(8,128)(2,1)S(1)}, u32[]{:S(2)}, u32[]{:S(2)}) collective-permute-start(bf16[528,128]{1,0:T(8,128)(2,1)S(1)} %copy-done.1), channel_id=1, source_target_pairs={{0,4},{4,8},{8,12},{12,14},{14,10},{10,6},{6,2},{2,0},{1,5},{5,9},... | collective-permute-start | bytes 405512 | tf_op jit(solution)/shard_map/ppermute | solution.py:153
  45.4 3.0 %collective-permute-done.refs_1_ = bf16[528,128]{1,0:T(8,128)(2,1)S(1)} collective-permute-done((bf16[528,128]{1,0:T(8,128)(2,1)S(1)}, bf16[528,128]{1,0:T(8,128)(2,1)S(1)}, u32[]{:S(2)}, u32[]{:S(2)}) %collective-permute-start) | collective-permute-done | bytes 135200 | tf_op jit(solution)/shard_map/ppermute | solution.py:153
  48.4 1.5 %collective-permute-start.2 = (bf16[528,128]{1,0:T(8,128)(2,1)S(1)}, bf16[528,128]{1,0:T(8,128)(2,1)S(1)}, u32[]{:S(2)}, u32[]{:S(2)}) collective-permute-start(bf16[528,128]{1,0:T(8,128)(2,1)S(1)} %collective-permute-done.refs_1_), channel_id=1, source_target_pairs={{0,4},{4,8},{8,12},{12,14},{14,10},{10,6},{6,2},{2,0},{1,5},{5,9},... | collective-permute-start | bytes 405512 | tf_op jit(solution)/shard_map/ppermute | solution.py:153
  50.4 3.1 %collective-permute-done.2.refs_3_ = bf16[528,128]{1,0:T(8,128)(2,1)S(1)} collective-permute-done((bf16[528,128]{1,0:T(8,128)(2,1)S(1)}, bf16[528,128]{1,0:T(8,128)(2,1)S(1)}, u32[]{:S(2)}, u32[]{:S(2)}) %collective-permute-start.2) | collective-permute-done | bytes 135200 | tf_op jit(solution)/shard_map/ppermute | solution.py:153
  53.5 1.5 %collective-permute-start.4 = (bf16[528,128]{1,0:T(8,128)(2,1)S(1)}, bf16[528,128]{1,0:T(8,128)(2,1)S(1)}, u32[]{:S(2)}, u32[]{:S(2)}) collective-permute-start(bf16[528,128]{1,0:T(8,128)(2,1)S(1)} %collective-permute-done.2.refs_3_), channel_id=1, source_target_pairs={{0,4},{4,8},{8,12},{12,14},{14,10},{10,6},{6,2},{2,0},{1,5},{5,9},... | collective-permute-start | bytes 405512 | tf_op jit(solution)/shard_map/ppermute | solution.py:153
  55.9 2.7 %collective-permute-done.4.refs_5_ = bf16[528,128]{1,0:T(8,128)(2,1)S(1)} collective-permute-done((bf16[528,128]{1,0:T(8,128)(2,1)S(1)}, bf16[528,128]{1,0:T(8,128)(2,1)S(1)}, u32[]{:S(2)}, u32[]{:S(2)}) %collective-permute-start.4) | collective-permute-done | bytes 135200 | tf_op jit(solution)/shard_map/ppermute | solution.py:153
  58.6 1.8 %collective-permute-done.6.refs_7_ = bf16[528,128]{1,0:T(8,128)(2,1)S(1)} collective-permute-done((bf16[528,128]{1,0:T(8,128)(2,1)S(1)}, bf16[528,128]{1,0:T(8,128)(2,1)S(1)}, u32[]{:S(2)}, u32[]{:S(2)}) %collective-permute-start.6) | collective-permute-done | bytes 135200 | tf_op jit(solution)/shard_map/ppermute | solution.py:156
  60.3 3.3 %shard_map.39 = (f32[512,512]{1,0:T(8,128)S(1)}, f32[1,512]{1,0:T(1,128)S(1)}) custom-call(s32[1]{0:T(128)} %bitcast.row_ref, bf16[528,128]{1,0:T(8,128)(2,1)S(1)} %copy-done.1, bf16[528,128]{1,0:T(8,128)(2,1)S(1)} %collective-permute-done.refs_1_, bf16[528,128]{1,0:T(8,128)(2,1)S(1)} %collective-permute-done.1.refs_2_, ...), custom_call_target="tpu_custom_call" | custom-call | tf_op jit(solution)/shard_map/pallas_call | solution.py:203
  63.8 1.1 %collective-permute-done.16 = f32[1,512]{1,0:T(1,128)S(1)} collective-permute-done((f32[1,512]{1,0:T(1,128)S(1)}, f32[1,512]{1,0:T(1,128)S(1)}, u32[]{:S(2)}, u32[]{:S(2)}) %collective-permute-start.16) | collective-permute-done | bytes 2080 | tf_op jit(solution)/shard_map/ppermute | solution.py:214
  64.9 1.4 %collective-permute-start.17 = (f32[1,512]{1,0:T(1,128)S(1)}, f32[1,512]{1,0:T(1,128)S(1)}, u32[]{:S(2)}, u32[]{:S(2)}) collective-permute-start(f32[1,512]{1,0:T(1,128)S(1)} %add.12), channel_id=1, source_target_pairs={{0,1},{1,0},{2,3},{3,2},{4,5},{5,4},{6,7},{7,6},{8,9},{9,8},{10,11... | collective-permute-start | bytes 6152 | tf_op jit(solution)/shard_map/ppermute | solution.py:215
  66.3 2.2 %collective-permute-done.17 = f32[1,512]{1,0:T(1,128)S(1)} collective-permute-done((f32[1,512]{1,0:T(1,128)S(1)}, f32[1,512]{1,0:T(1,128)S(1)}, u32[]{:S(2)}, u32[]{:S(2)}) %collective-permute-start.17) | collective-permute-done | bytes 2080 | tf_op jit(solution)/shard_map/ppermute | solution.py:215
  (25 shorter events, 5.6 us)
Async XLA Ops:
  0.0 34.1 %collective-permute-start.7 = (bf16[4096,512]{1,0:T(8,128)(2,1)}, bf16[4096,512]{1,0:T(8,128)(2,1)}, u32[]{:S(2)}, u32[]{:S(2)}) collective-permute-start(bf16[4096,512]{1,0:T(8,128)(2,1)} %bitcast.5), channel_id=1, source_target_pairs={{0,16},{16,0},{1,17},{17,1},{2,18},{18,2},{3,19},{19,3},{4,20},{20... | collective-permute-start | bytes 12582920 | tf_op jit(solution)/shard_map/ppermute | solution.py:170
  11.6 7.0 %collective-permute-start.8 = (bf16[528,128]{1,0:T(8,128)(2,1)}, bf16[528,128]{1,0:T(8,128)(2,1)S(1)}, u32[]{:S(2)}, u32[]{:S(2)}) collective-permute-start(bf16[528,128]{1,0:T(8,128)(2,1)} %get-tuple-element.10.refs_0_), channel_id=1, source_target_pairs={{0,4},{4,8},{8,12},{12,14},{14,10},{10,6},{6,2},{2,0},{1,5},{5,9},... | collective-permute-start | bytes 405512 | tf_op jit(solution)/shard_map/ppermute | solution.py:153
  14.2 6.2 %collective-permute-start.9 = (bf16[528,128]{1,0:T(8,128)(2,1)}, bf16[528,128]{1,0:T(8,128)(2,1)S(1)}, u32[]{:S(2)}, u32[]{:S(2)}) collective-permute-start(bf16[528,128]{1,0:T(8,128)(2,1)} %get-tuple-element.10.refs_0_), channel_id=1, source_target_pairs={{4,0},{8,4},{12,8},{14,12},{10,14},{6,10},{2,6},{0,2},{5,1},{9,5},... | collective-permute-start | bytes 405512 | tf_op jit(solution)/shard_map/ppermute | solution.py:156
  18.6 5.4 %collective-permute-start.10 = (bf16[528,128]{1,0:T(8,128)(2,1)S(1)}, bf16[528,128]{1,0:T(8,128)(2,1)S(1)}, u32[]{:S(2)}, u32[]{:S(2)}) collective-permute-start(bf16[528,128]{1,0:T(8,128)(2,1)S(1)} %collective-permute-done.8.refs_1_), channel_id=1, source_target_pairs={{0,4},{4,8},{8,12},{12,14},{14,10},{10,6},{6,2},{2,0},{1,5},{5,9},... | collective-permute-start | bytes 405512 | tf_op jit(solution)/shard_map/ppermute | solution.py:153
  20.4 5.2 %collective-permute-start.11 = (bf16[528,128]{1,0:T(8,128)(2,1)S(1)}, bf16[528,128]{1,0:T(8,128)(2,1)S(1)}, u32[]{:S(2)}, u32[]{:S(2)}) collective-permute-start(bf16[528,128]{1,0:T(8,128)(2,1)S(1)} %collective-permute-done.9.refs_2_), channel_id=1, source_target_pairs={{4,0},{8,4},{12,8},{14,12},{10,14},{6,10},{2,6},{0,2},{5,1},{9,5},... | collective-permute-start | bytes 405512 | tf_op jit(solution)/shard_map/ppermute | solution.py:156
  24.0 5.0 %collective-permute-start.12 = (bf16[528,128]{1,0:T(8,128)(2,1)S(1)}, bf16[528,128]{1,0:T(8,128)(2,1)S(1)}, u32[]{:S(2)}, u32[]{:S(2)}) collective-permute-start(bf16[528,128]{1,0:T(8,128)(2,1)S(1)} %collective-permute-done.10.refs_3_), channel_id=1, source_target_pairs={{0,4},{4,8},{8,12},{12,14},{14,10},{10,6},{6,2},{2,0},{1,5},{5,9},... | collective-permute-start | bytes 405512 | tf_op jit(solution)/shard_map/ppermute | solution.py:153
  25.6 5.4 %collective-permute-start.13 = (bf16[528,128]{1,0:T(8,128)(2,1)S(1)}, bf16[528,128]{1,0:T(8,128)(2,1)S(1)}, u32[]{:S(2)}, u32[]{:S(2)}) collective-permute-start(bf16[528,128]{1,0:T(8,128)(2,1)S(1)} %collective-permute-done.11.refs_4_), channel_id=1, source_target_pairs={{4,0},{8,4},{12,8},{14,12},{10,14},{6,10},{2,6},{0,2},{5,1},{9,5},... | collective-permute-start | bytes 405512 | tf_op jit(solution)/shard_map/ppermute | solution.py:156
  29.0 5.0 %collective-permute-start.14 = (bf16[528,128]{1,0:T(8,128)(2,1)S(1)}, bf16[528,128]{1,0:T(8,128)(2,1)S(1)}, u32[]{:S(2)}, u32[]{:S(2)}) collective-permute-start(bf16[528,128]{1,0:T(8,128)(2,1)S(1)} %collective-permute-done.12.refs_5_), channel_id=1, source_target_pairs={{0,4},{4,8},{8,12},{12,14},{14,10},{10,6},{6,2},{2,0},{1,5},{5,9},... | collective-permute-start | bytes 405512 | tf_op jit(solution)/shard_map/ppermute | solution.py:153
  30.6 14.3 %collective-permute-start.1 = (bf16[528,128]{1,0:T(8,128)(2,1)}, bf16[528,128]{1,0:T(8,128)(2,1)S(1)}, u32[]{:S(2)}, u32[]{:S(2)}) collective-permute-start(bf16[528,128]{1,0:T(8,128)(2,1)} %get-tuple-element.9.refs_0_), channel_id=1, source_target_pairs={{4,0},{8,4},{12,8},{14,12},{10,14},{6,10},{2,6},{0,2},{5,1},{9,5},... | collective-permute-start | bytes 405512 | tf_op jit(solution)/shard_map/ppermute | solution.py:156
  34.1 2.2 %copy-start = (bf16[1,4096,512]{2,1,0:T(8,128)(2,1)S(1)}, bf16[1,4096,512]{2,1,0:T(8,128)(2,1)}, u32[]{:S(2)}) copy-start(bf16[1,4096,512]{2,1,0:T(8,128)(2,1)} %param.5) | copy-start | bytes 12582916
  36.3 0.9 %copy-start.2 = (bf16[528,128]{1,0:T(8,128)(2,1)S(1)}, bf16[528,128]{1,0:T(8,128)(2,1)}, u32[]{:S(2)}) copy-start(bf16[528,128]{1,0:T(8,128)(2,1)} %get-tuple-element.10.refs_0_) | copy-start | bytes 405508
  37.2 6.2 %copy-start.1 = (bf16[528,128]{1,0:T(8,128)(2,1)S(1)}, bf16[528,128]{1,0:T(8,128)(2,1)}, u32[]{:S(2)}) copy-start(bf16[528,128]{1,0:T(8,128)(2,1)} %get-tuple-element.9.refs_0_) | copy-start | bytes 405508
  41.9 18.5 %collective-permute-start.15 = (bf16[528,512]{1,0:T(8,128)(2,1)S(1)}, bf16[528,512]{1,0:T(8,128)(2,1)S(1)}, u32[]{:S(2)}, u32[]{:S(2)}) collective-permute-start(bf16[528,512]{1,0:T(8,128)(2,1)S(1)} %shard_map.38), channel_id=1, source_target_pairs={{0,1},{1,0},{2,3},{3,2},{4,5},{5,4},{6,7},{7,6},{8,9},{9,8},{10,11... | collective-permute-start | bytes 1622024 | tf_op jit(solution)/shard_map/ppermute | solution.py:202
  43.4 5.0 %collective-permute-start = (bf16[528,128]{1,0:T(8,128)(2,1)S(1)}, bf16[528,128]{1,0:T(8,128)(2,1)S(1)}, u32[]{:S(2)}, u32[]{:S(2)}) collective-permute-start(bf16[528,128]{1,0:T(8,128)(2,1)S(1)} %copy-done.1), channel_id=1, source_target_pairs={{0,4},{4,8},{8,12},{12,14},{14,10},{10,6},{6,2},{2,0},{1,5},{5,9},... | collective-permute-start | bytes 405512 | tf_op jit(solution)/shard_map/ppermute | solution.py:153
  44.9 5.0 %collective-permute-start.3 = (bf16[528,128]{1,0:T(8,128)(2,1)S(1)}, bf16[528,128]{1,0:T(8,128)(2,1)S(1)}, u32[]{:S(2)}, u32[]{:S(2)}) collective-permute-start(bf16[528,128]{1,0:T(8,128)(2,1)S(1)} %collective-permute-done.1.refs_2_), channel_id=1, source_target_pairs={{4,0},{8,4},{12,8},{14,12},{10,14},{6,10},{2,6},{0,2},{5,1},{9,5},... | collective-permute-start | bytes 405512 | tf_op jit(solution)/shard_map/ppermute | solution.py:156
  48.4 5.1 %collective-permute-start.2 = (bf16[528,128]{1,0:T(8,128)(2,1)S(1)}, bf16[528,128]{1,0:T(8,128)(2,1)S(1)}, u32[]{:S(2)}, u32[]{:S(2)}) collective-permute-start(bf16[528,128]{1,0:T(8,128)(2,1)S(1)} %collective-permute-done.refs_1_), channel_id=1, source_target_pairs={{0,4},{4,8},{8,12},{12,14},{14,10},{10,6},{6,2},{2,0},{1,5},{5,9},... | collective-permute-start | bytes 405512 | tf_op jit(solution)/shard_map/ppermute | solution.py:153
  49.9 5.4 %collective-permute-start.5 = (bf16[528,128]{1,0:T(8,128)(2,1)S(1)}, bf16[528,128]{1,0:T(8,128)(2,1)S(1)}, u32[]{:S(2)}, u32[]{:S(2)}) collective-permute-start(bf16[528,128]{1,0:T(8,128)(2,1)S(1)} %collective-permute-done.3.refs_4_), channel_id=1, source_target_pairs={{4,0},{8,4},{12,8},{14,12},{10,14},{6,10},{2,6},{0,2},{5,1},{9,5},... | collective-permute-start | bytes 405512 | tf_op jit(solution)/shard_map/ppermute | solution.py:156
  53.5 5.0 %collective-permute-start.4 = (bf16[528,128]{1,0:T(8,128)(2,1)S(1)}, bf16[528,128]{1,0:T(8,128)(2,1)S(1)}, u32[]{:S(2)}, u32[]{:S(2)}) collective-permute-start(bf16[528,128]{1,0:T(8,128)(2,1)S(1)} %collective-permute-done.2.refs_3_), channel_id=1, source_target_pairs={{0,4},{4,8},{8,12},{12,14},{14,10},{10,6},{6,2},{2,0},{1,5},{5,9},... | collective-permute-start | bytes 405512 | tf_op jit(solution)/shard_map/ppermute | solution.py:153
  55.3 5.0 %collective-permute-start.6 = (bf16[528,128]{1,0:T(8,128)(2,1)S(1)}, bf16[528,128]{1,0:T(8,128)(2,1)S(1)}, u32[]{:S(2)}, u32[]{:S(2)}) collective-permute-start(bf16[528,128]{1,0:T(8,128)(2,1)S(1)} %collective-permute-done.5.refs_6_), channel_id=1, source_target_pairs={{4,0},{8,4},{12,8},{14,12},{10,14},{6,10},{2,6},{0,2},{5,1},{9,5},... | collective-permute-start | bytes 405512 | tf_op jit(solution)/shard_map/ppermute | solution.py:156
  63.7 1.2 %collective-permute-start.16 = (f32[1,512]{1,0:T(1,128)S(1)}, f32[1,512]{1,0:T(1,128)S(1)}, u32[]{:S(2)}, u32[]{:S(2)}) collective-permute-start(f32[1,512]{1,0:T(1,128)S(1)} %get-tuple-element.12), channel_id=1, source_target_pairs={{0,16},{16,0},{1,17},{17,1},{2,18},{18,2},{3,19},{19,3},{4,20},{20... | collective-permute-start | bytes 6152 | tf_op jit(solution)/shard_map/ppermute | solution.py:214
  64.9 3.6 %collective-permute-start.17 = (f32[1,512]{1,0:T(1,128)S(1)}, f32[1,512]{1,0:T(1,128)S(1)}, u32[]{:S(2)}, u32[]{:S(2)}) collective-permute-start(f32[1,512]{1,0:T(1,128)S(1)} %add.12), channel_id=1, source_target_pairs={{0,1},{1,0},{2,3},{3,2},{4,5},{5,4},{6,7},{7,6},{8,9},{9,8},{10,11... | collective-permute-start | bytes 6152 | tf_op jit(solution)/shard_map/ppermute | solution.py:215

commit v2 on v1

v2 whole, which is shorter than its diff:
```python
import functools

import jax
import jax.numpy as jnp
from jax import lax
from jax.experimental import pallas as pl
from jax.experimental.pallas import tpu as pltpu
from jax.sharding import PartitionSpec as P

CODE_SPAN = 250.0
CODE_MID = 125.0
LOG2E = 1.4426950408889634
ID_ROWS = 16
VMEM_BYTES = 24 * 1024 * 1024
AFTER = {5: 3}
JOIN_AT = (2, 3)
PLACE_LIMIT = 24 << 20


def pack_kernel(cols_ref, layer_ref, vals_ref, send_ref, keep_ref, sems):
    rows = send_ref.shape[0] - ID_ROWS
    block = vals_ref.shape[1]
    count = rows // block
    layer = layer_ref[0]
    copies = []
    for k, (out, part) in enumerate(((send_ref, 1 - layer), (keep_ref, layer))):
        copies.append(
            pltpu.make_async_copy(
                vals_ref.at[pl.ds(pl.multiple_of(part * rows, block), rows)],
                out.at[pl.ds(0, rows)],
                sems.at[k],
            )
        )
        copies[-1].start()
        lanes = lax.broadcasted_iota(jnp.int32, (ID_ROWS, block), 1)
        line = jnp.zeros((ID_ROWS, block), jnp.int32)
        for j in range(count):
            line = jnp.where(lanes == j, cols_ref[part * count + j], line)
        out[rows : rows + ID_ROWS, :] = line.astype(jnp.float32).astype(jnp.bfloat16)
    for copy in copies:
        copy.wait()


def place_kernel(at_ref, part_ref, *refs):
    window_ref, sem = refs[-2:]
    half = part_ref.shape[0]
    where = pl.ds(pl.multiple_of(at_ref[0] * half, half), half)
    copy = pltpu.make_async_copy(part_ref, window_ref.at[where], sem)
    copy.start()
    copy.wait()


def products(items, window, first, ids_v, ids_s, sems, finish):
    block = first.shape[1]
    rows = first.shape[0] - ID_ROWS
    live_end = window.shape[0] // block
    fetch = pltpu.make_async_copy(items[0], first, sems.at[0])
    fetch.start()
    for s in range(1, len(items)):
        ids_v[pl.ds(s, 1)] = items[s][rows : rows + 1, :].astype(jnp.float32).astype(jnp.int32)
    fetch.wait()
    ids_v[pl.ds(0, 1)] = first[rows : rows + 1, :].astype(jnp.float32).astype(jnp.int32)
    to_scalar = pltpu.make_async_copy(ids_v, ids_s, sems.at[1])
    to_scalar.start()
    to_scalar.wait()
    for j in range(rows // block):
        left, right = [], []
        for s in range(len(items)):
            col = ids_s[s, j]
            live = jnp.where(col < live_end, 1.0, 0.0).astype(jnp.float32)
            source = first if s == 0 else items[s]
            piece = source[j * block : (j + 1) * block, :]
            left.append((piece.astype(jnp.float32) * live).astype(jnp.bfloat16))
            at = pl.multiple_of(jnp.minimum(col, live_end - 1) * block, block)
            right.append(window[pl.ds(at, block), :])
        finish(
            j,
            jnp.dot(
                jnp.concatenate(left, axis=1),
                jnp.concatenate(right, axis=0),
                preferred_element_type=jnp.float32,
            ),
        )


def send_kernel(slots, *refs):
    items, (window, code_ref, first, ids_v, ids_s, total, sems) = refs[:slots], refs[slots:]
    block = first.shape[1]
    rows = total.shape[0]

    def finish(j, value):
        total[j * block : (j + 1) * block, :] = value

    products(items, window, first, ids_v, ids_s, sems, finish)
    most = jnp.max(jnp.abs(total[...]), axis=0, keepdims=True)
    scale = (most * 1.01 + 1e-30).astype(jnp.bfloat16)
    inverse = CODE_SPAN / scale.astype(jnp.float32)
    for j in range(rows // block):
        value = total[j * block : (j + 1) * block, :]
        size = jnp.exp((jnp.abs(value) * inverse - CODE_MID) * (1.0 / LOG2E))
        code_ref[j * block : (j + 1) * block, :] = jnp.where(value < 0, -size, size).astype(jnp.bfloat16)
    code_ref[rows : rows + ID_ROWS, :] = jnp.broadcast_to(scale, (ID_ROWS, scale.shape[1]))


def keep_kernel(slots, *refs):
    items, (window, code_ref, square_ref, sum_ref, first, ids_v, ids_s, sems) = refs[:slots], refs[slots:]
    block = first.shape[1]
    rows = square_ref.shape[0]
    scale = code_ref[rows : rows + 1, :].astype(jnp.float32) * (1.0 / CODE_SPAN)
    sums = []

    def finish(j, value):
        code = code_ref[j * block : (j + 1) * block, :].astype(jnp.float32)
        size = (jnp.log(jnp.abs(code)) * LOG2E + CODE_MID) * scale
        full = value + jnp.where(code < 0, -size, size)
        square = full * full
        square_ref[j * block : (j + 1) * block, :] = square
        sums.append(jnp.sum(square, axis=0, keepdims=True))

    products(items, window, first, ids_v, ids_s, sems, finish)
    sum_ref[...] = functools.reduce(jnp.add, sums)


def ring_of(mesh):
    size = mesh.shape["col"]
    if size != 8:
        return list(range(size))
    return [0, 2, 4, 6, 7, 5, 3, 1]


def solution(mesh):
    size = mesh.shape["col"]
    order = ring_of(mesh)
    ahead = [(order[i], order[(i + 1) % size]) for i in range(size)]
    back = [(b, a) for a, b in ahead]
    swap = [(0, 1), (1, 0)]
    vmem = pl.BlockSpec(memory_space=pltpu.VMEM)
    smem = pl.BlockSpec(memory_space=pltpu.SMEM)
    anywhere = pl.BlockSpec(memory_space=pl.ANY)

    def step_on(ends, items, forward=True, backward=True):
        front, rear = ends
        if forward:
            front = lax.ppermute(front, "col", ahead)
            items.append(front)
        if backward:
            rear = lax.ppermute(rear, "col", back)
            items.append(rear)
        return front, rear

    def gather_two(send, keep, window, join):
        sends, keeps = [send], [keep]
        at, behind = (send, send), (keep, keep)
        last = size // 2
        done = 0
        for step in range(1, last + 2):
            want = AFTER.get(step, 0)
            while done < want:
                done += 1
                behind = step_on(behind, keeps, done < last, True)
            if want:
                at, behind = lax.optimization_barrier((at, behind))
            if step == JOIN_AT[1]:
                window = join(window)
            if step in JOIN_AT:
                at, window = lax.optimization_barrier((at, window))
            if step <= last:
                at = step_on(at, sends, True, step < last)
        sends[-1] = at[0]
        while done < last:
            done += 1
            behind = step_on(behind, keeps, done < last, True)
        return sends, keeps, window

    def gather_all(item):
        stacked = lax.all_gather(item, "col", axis=0)
        return [stacked[i] for i in range(size)]

    def body(flow_cols, flow_vals, window_flow):
        block = flow_vals.shape[-1]
        count = flow_vals.shape[0] // 2
        rows = count * block
        own = window_flow[0]
        half, columns = own.shape
        other = lax.ppermute(own, "row", swap)
        row = lax.axis_index("row").astype(jnp.int32).reshape(1)
        layer = lax.axis_index("layer").astype(jnp.int32).reshape(1)
        item = jax.ShapeDtypeStruct((rows + ID_ROWS, block), flow_vals.dtype)
        params = pltpu.CompilerParams(vmem_limit_bytes=VMEM_BYTES)
        send, keep = pl.pallas_call(
            pack_kernel,
            out_shape=(item, item),
            in_specs=[smem, smem, anywhere],
            out_specs=(vmem, vmem),
            scratch_shapes=[pltpu.SemaphoreType.DMA((2,))],
        )(flow_cols.reshape(2 * count), layer, flow_vals.reshape(2 * rows, block))
        def place(at, part, window=None):
            given = [] if window is None else [window]
            return pl.pallas_call(
                place_kernel,
                out_shape=jax.ShapeDtypeStruct((2 * half, columns), own.dtype),
                in_specs=[smem, anywhere] + [vmem] * len(given),
                out_specs=vmem,
                scratch_shapes=[pltpu.SemaphoreType.DMA(())],
                input_output_aliases={2: 0} if given else {},
                compiler_params=pltpu.CompilerParams(vmem_limit_bytes=PLACE_LIMIT),
                cost_estimate=pl.CostEstimate(flops=0, bytes_accessed=2 * half * columns * 2, transcendentals=0),
            )(at, part, *given)

        window = place(row, own)
        if size == 8:
            sends, keeps, window = gather_two(send, keep, window, lambda w: place(1 - row, other, w))
        else:
            sends, keeps = gather_all(send), gather_all(keep)
            window = place(1 - row, other, window)
        scratch = [
            pltpu.VMEM((rows + ID_ROWS, block), flow_vals.dtype),
            pltpu.VMEM((max(size, 8), block), jnp.int32),
            pltpu.SMEM((max(size, 8), block), jnp.int32),
        ]
        sems = [pltpu.SemaphoreType.DMA((2,))]
        item_specs = [anywhere] + [vmem] * (size - 1)
        code = pl.pallas_call(
            functools.partial(send_kernel, size),
            out_shape=jax.ShapeDtypeStruct((rows + ID_ROWS, columns), jnp.bfloat16),
            in_specs=item_specs + [vmem],
            out_specs=vmem,
            scratch_shapes=scratch + [pltpu.VMEM((rows, columns), jnp.float32)] + sems,
            compiler_params=params,
        )(*sends, window)
        code = lax.ppermute(code, "layer", swap)
        square, sums = pl.pallas_call(
            functools.partial(keep_kernel, size),
            out_shape=(
                jax.ShapeDtypeStruct((rows, columns), jnp.float32),
                jax.ShapeDtypeStruct((1, columns), jnp.float32),
            ),
            in_specs=item_specs + [vmem, vmem],
            out_specs=(vmem, vmem),
            scratch_shapes=scratch + sems,
            compiler_params=params,
        )(*keeps, window, code)
        sums = sums + lax.ppermute(sums, "row", swap)
        sums = sums + lax.ppermute(sums, "layer", swap)
        total_rows = rows * lax.axis_size("row") * lax.axis_size("layer")
        return square * (1.0 / (sums / total_rows + 1e-6))

    placed = (
        P("row", "layer", "col"),
        P("row", "layer", "col", None, None),
        P("layer", "row", "col"),
    )
    return jax.shard_map(body, mesh=mesh, in_specs=placed, out_specs=P(("row", "layer"), "col"), check_vma=False)
```

time: 70.9 us -> 50.7 us (0.72); the launches traced: 69.6 us -> 50.5 us
  Pallas kernels: 17.8 us -> 8.53 us
  waiting for transfers between devices: 27.9 us -> 20.6 us
  local copies, waits for them, and re-layouts: 4.41 us -> 2.2 us
    ppermute x14, waiting for transfers between devices: 24.6 us -> 13.5 us  [the longest x7 9.91 us: step_on(): rear = lax.ppermute(rear, 'col', back)]
    pallas_call x1, Pallas kernels: 9.8 us -> 2.36 us  [body(): pl.pallas_call(pack_kernel, out_shape=(item, item), in_specs=[smem, smem,...]
    ppermute x1, waiting for transfers between devices: 0.01 us -> 3.85 us  [body(): code = lax.ppermute(code, 'layer', swap)]
    pallas_call x1, Pallas kernels: 4.68 us -> 1.9 us  [body(): pl.pallas_call(functools.partial(send_kernel, size), out_shape=jax.ShapeD...]
    pallas_call x0 -> x2, Pallas kernels: none -> 2.49 us  [place(): pl.pallas_call(place_kernel, out_shape=jax.ShapeDtypeStruct((2 * half, co...]
    unnamed x7 -> x6, local copies, waits for them, and re-layouts: 4.41 us -> 2.2 us
    pallas_call x1, Pallas kernels: 3.34 us -> 1.79 us  [body(): pl.pallas_call(functools.partial(keep_kernel, size), out_shape=(jax.Shape...]
  transfers between devices with their start and end apart: 18 -> 18, of which waited for: 11 -> 12; matrix products, arithmetic and copies ran while one was open for 2% -> 0% of each run, Pallas kernels for 21% -> 10%
where the time goes in v2:
time: 50.7 us; the launch traced here: 50.5 us
  waiting for transfers between devices  20.6 us (41%)
  starting transfers between devices  17.9 us (35%)
  Pallas kernels  8.53 us (17%)
  local copies, waits for them, and re-layouts  2.2 us (4%)
  other arithmetic  1.12 us (2%)
    ppermute x7, starting transfers between devices, step_on(): front = lax.ppermute(front, 'col', ahead)  12.6 us
    ppermute x7, waiting for transfers between devices, step_on(): rear = lax.ppermute(rear, 'col', back)  9.91 us
    ppermute x1, waiting for transfers between devices, body(): code = lax.ppermute(code, 'layer', swap)  3.85 us
    ppermute x7, waiting for transfers between devices, step_on(): front = lax.ppermute(front, 'col', ahead)  3.64 us
    pallas_call x2, Pallas kernels, place(): pl.pallas_call(place_kernel, out_shape=jax.ShapeDtypeStruct((2 * half, co...  2.49 us
    pallas_call x1, Pallas kernels, body(): pl.pallas_call(pack_kernel, out_shape=(item, item), in_specs=[smem, smem,...  2.36 us
    unnamed x6, local copies, waits for them, and re-layouts  2.2 us
    ppermute x1, waiting for transfers between devices, body(): sums = sums + lax.ppermute(sums, 'layer', swap)  2.1 us
  transfers between devices with their start and end apart: 18, of which 12 were waited for; matrix products, arithmetic and copies ran while one was open for 0% of the time, Pallas kernels for 10%

profile of v2, /device:TPU:0, one launch (start us, length us, event | category | flops | bytes accessed | tf_op | source)
XLA Modules:
  0.0 50.5 jit_solution(1724644479405042530)
XLA Ops:
  0.5 2.4 %shard_map.37 = (bf16[528,128]{1,0:T(8,128)(2,1)}, bf16[528,128]{1,0:T(8,128)(2,1)}) custom-call(s32[8]{0:T(128)} %bitcast.10, s32[1]{0:T(128)} %bitcast.1.layer_ref, bf16[1024,128]{1,0:T(8,128)(2,1)} %bitcast.8), custom_call_target="tpu_custom_call" | custom-call | tf_op jit(solution)/shard_map/pallas_call | solution.py:190
  2.8 2.6 %collective-permute-start.6 = (bf16[528,128]{1,0:T(8,128)(2,1)}, bf16[528,128]{1,0:T(8,128)(2,1)S(1)}, u32[]{:S(2)}, u32[]{:S(2)}) collective-permute-start(bf16[528,128]{1,0:T(8,128)(2,1)} %get-tuple-element.18.refs_0_), channel_id=1, source_target_pairs={{0,4},{4,8},{8,12},{12,14},{14,10},{10,6},{6,2},{2,0},{1,5},{5,9},... | collective-permute-start | bytes 405512 | tf_op jit(solution)/shard_map/ppermute | solution.py:144
  5.5 2.0 %collective-permute-start = (bf16[528,128]{1,0:T(8,128)(2,1)}, bf16[528,128]{1,0:T(8,128)(2,1)S(1)}, u32[]{:S(2)}, u32[]{:S(2)}) collective-permute-start(bf16[528,128]{1,0:T(8,128)(2,1)} %get-tuple-element.17.refs_0_), channel_id=1, source_target_pairs={{0,4},{4,8},{8,12},{12,14},{14,10},{10,6},{6,2},{2,0},{1,5},{5,9},... | collective-permute-start | bytes 405512 | tf_op jit(solution)/shard_map/ppermute | solution.py:144
  7.5 2.2 %copy-done = bf16[1,4096,512]{2,1,0:T(8,128)(2,1)S(1)} copy-done((bf16[1,4096,512]{2,1,0:T(8,128)(2,1)S(1)}, bf16[1,4096,512]{2,1,0:T(8,128)(2,1)}, u32[]{:S(2)}) %copy-start) | copy-done | bytes 4194328
  10.0 2.0 %collective-permute-done.7.refs_2_ = bf16[528,128]{1,0:T(8,128)(2,1)S(1)} collective-permute-done((bf16[528,128]{1,0:T(8,128)(2,1)}, bf16[528,128]{1,0:T(8,128)(2,1)S(1)}, u32[]{:S(2)}, u32[]{:S(2)}) %collective-permute-start.7) | collective-permute-done | bytes 135200 | tf_op jit(solution)/shard_map/ppermute | solution.py:147
  12.1 1.6 %collective-permute-start.8 = (bf16[528,128]{1,0:T(8,128)(2,1)S(1)}, bf16[528,128]{1,0:T(8,128)(2,1)S(1)}, u32[]{:S(2)}, u32[]{:S(2)}) collective-permute-start(bf16[528,128]{1,0:T(8,128)(2,1)S(1)} %collective-permute-done.6.refs_1_), channel_id=1, source_target_pairs={{0,4},{4,8},{8,12},{12,14},{14,10},{10,6},{6,2},{2,0},{1,5},{5,9},... | collective-permute-start | bytes 405512 | tf_op jit(solution)/shard_map/ppermute | solution.py:144
  14.1 1.6 %collective-permute-start.2 = (bf16[528,128]{1,0:T(8,128)(2,1)S(1)}, bf16[528,128]{1,0:T(8,128)(2,1)S(1)}, u32[]{:S(2)}, u32[]{:S(2)}) collective-permute-start(bf16[528,128]{1,0:T(8,128)(2,1)S(1)} %collective-permute-done.refs_1_), channel_id=1, source_target_pairs={{0,4},{4,8},{8,12},{12,14},{14,10},{10,6},{6,2},{2,0},{1,5},{5,9},... | collective-permute-start | bytes 405512 | tf_op jit(solution)/shard_map/ppermute | solution.py:144
  16.1 2.2 %shard_map.39.refs_8_ = bf16[8192,512]{1,0:T(8,128)(2,1)S(1)} custom-call(s32[1]{0:T(128)S(6)} %sub.3.at_ref, bf16[4096,512]{1,0:T(8,128)(2,1)} %collective-permute-done.10.part_ref, bf16[8192,512]{1,0:T(8,128)(2,1)S(1)} %shard_map.38.refs_0_), custom_call_target="tpu_custom_call", output_to_operand_aliasing={{}: (2, {})} | custom-call | bytes 8388608 | tf_op jit(solution)/shard_map/pallas_call | solution.py:199
  18.4 1.1 %collective-permute-done.9.refs_4_ = bf16[528,128]{1,0:T(8,128)(2,1)S(1)} collective-permute-done((bf16[528,128]{1,0:T(8,128)(2,1)S(1)}, bf16[528,128]{1,0:T(8,128)(2,1)S(1)}, u32[]{:S(2)}, u32[]{:S(2)}) %collective-permute-start.9) | collective-permute-done | bytes 135200 | tf_op jit(solution)/shard_map/ppermute | solution.py:147
  19.5 1.6 %collective-permute-start.11 = (bf16[528,128]{1,0:T(8,128)(2,1)S(1)}, bf16[528,128]{1,0:T(8,128)(2,1)S(1)}, u32[]{:S(2)}, u32[]{:S(2)}) collective-permute-start(bf16[528,128]{1,0:T(8,128)(2,1)S(1)} %collective-permute-done.8.refs_3_), channel_id=1, source_target_pairs={{0,4},{4,8},{8,12},{12,14},{14,10},{10,6},{6,2},{2,0},{1,5},{5,9},... | collective-permute-start | bytes 405512 | tf_op jit(solution)/shard_map/ppermute | solution.py:144
  21.1 1.6 %collective-permute-start.4 = (bf16[528,128]{1,0:T(8,128)(2,1)S(1)}, bf16[528,128]{1,0:T(8,128)(2,1)S(1)}, u32[]{:S(2)}, u32[]{:S(2)}) collective-permute-start(bf16[528,128]{1,0:T(8,128)(2,1)S(1)} %collective-permute-done.2.refs_3_), channel_id=1, source_target_pairs={{0,4},{4,8},{8,12},{12,14},{14,10},{10,6},{6,2},{2,0},{1,5},{5,9},... | collective-permute-start | bytes 405512 | tf_op jit(solution)/shard_map/ppermute | solution.py:144
  23.6 1.9 %collective-permute-done.11.refs_5_ = bf16[528,128]{1,0:T(8,128)(2,1)S(1)} collective-permute-done((bf16[528,128]{1,0:T(8,128)(2,1)S(1)}, bf16[528,128]{1,0:T(8,128)(2,1)S(1)}, u32[]{:S(2)}, u32[]{:S(2)}) %collective-permute-start.11) | collective-permute-done | bytes 135200 | tf_op jit(solution)/shard_map/ppermute | solution.py:144
  25.4 1.6 %collective-permute-start.12 = (bf16[528,128]{1,0:T(8,128)(2,1)S(1)}, bf16[528,128]{1,0:T(8,128)(2,1)S(1)}, u32[]{:S(2)}, u32[]{:S(2)}) collective-permute-start(bf16[528,128]{1,0:T(8,128)(2,1)S(1)} %collective-permute-done.11.refs_5_), channel_id=1, source_target_pairs={{0,4},{4,8},{8,12},{12,14},{14,10},{10,6},{6,2},{2,0},{1,5},{5,9},... | collective-permute-start | bytes 405512 | tf_op jit(solution)/shard_map/ppermute | solution.py:144
  27.7 1.4 %collective-permute-done.13.refs_6_ = bf16[528,128]{1,0:T(8,128)(2,1)S(1)} collective-permute-done((bf16[528,128]{1,0:T(8,128)(2,1)S(1)}, bf16[528,128]{1,0:T(8,128)(2,1)S(1)}, u32[]{:S(2)}, u32[]{:S(2)}) %collective-permute-start.13) | collective-permute-done | bytes 135200 | tf_op jit(solution)/shard_map/ppermute | solution.py:147
  29.1 1.3 %collective-permute-done.12.refs_7_ = bf16[528,128]{1,0:T(8,128)(2,1)S(1)} collective-permute-done((bf16[528,128]{1,0:T(8,128)(2,1)S(1)}, bf16[528,128]{1,0:T(8,128)(2,1)S(1)}, u32[]{:S(2)}, u32[]{:S(2)}) %collective-permute-start.12) | collective-permute-done | bytes 135200 | tf_op jit(solution)/shard_map/ppermute | solution.py:144
  30.4 1.9 %shard_map.40 = bf16[528,512]{1,0:T(8,128)(2,1)S(1)} custom-call(bf16[528,128]{1,0:T(8,128)(2,1)S(1)} %copy-done.2, bf16[528,128]{1,0:T(8,128)(2,1)S(1)} %collective-permute-done.6.refs_1_, bf16[528,128]{1,0:T(8,128)(2,1)S(1)} %collective-permute-done.7.refs_2_, bf16[528,128]{1,0:T(8,128)(2,1)S(1)} %collective-permute-done.8.refs_3_, ...), custom_call_target="tpu_custom_call" | custom-call | tf_op jit(solution)/shard_map/pallas_call | solution.py:223
  32.3 1.6 %collective-permute-start.15 = (bf16[528,512]{1,0:T(8,128)(2,1)S(1)}, bf16[528,512]{1,0:T(8,128)(2,1)S(1)}, u32[]{:S(2)}, u32[]{:S(2)}) collective-permute-start(bf16[528,512]{1,0:T(8,128)(2,1)S(1)} %shard_map.40), channel_id=1, source_target_pairs={{0,1},{1,0},{2,3},{3,2},{4,5},{5,4},{6,7},{7,6},{8,9},{9,8},{10,11... | collective-permute-start | bytes 1622024 | tf_op jit(solution)/shard_map/ppermute | solution.py:231
  33.9 5.0 %collective-permute-done.14.refs_7_ = bf16[528,128]{1,0:T(8,128)(2,1)S(1)} collective-permute-done((bf16[528,128]{1,0:T(8,128)(2,1)S(1)}, bf16[528,128]{1,0:T(8,128)(2,1)S(1)}, u32[]{:S(2)}, u32[]{:S(2)}) %collective-permute-start.14) | collective-permute-done | bytes 135200 | tf_op jit(solution)/shard_map/ppermute | solution.py:147
  38.9 3.9 %collective-permute-done.15.refs_9_ = bf16[528,512]{1,0:T(8,128)(2,1)S(1)} collective-permute-done((bf16[528,512]{1,0:T(8,128)(2,1)S(1)}, bf16[528,512]{1,0:T(8,128)(2,1)S(1)}, u32[]{:S(2)}, u32[]{:S(2)}) %collective-permute-start.15) | collective-permute-done | bytes 540704 | tf_op jit(solution)/shard_map/ppermute | solution.py:231
  42.8 1.8 %shard_map.41 = (f32[512,512]{1,0:T(8,128)S(1)}, f32[1,512]{1,0:T(1,128)S(1)}) custom-call(bf16[528,128]{1,0:T(8,128)(2,1)S(1)} %copy-done.1, bf16[528,128]{1,0:T(8,128)(2,1)S(1)} %collective-permute-done.refs_1_, bf16[528,128]{1,0:T(8,128)(2,1)S(1)} %collective-permute-done.1.refs_2_, bf16[528,128]{1,0:T(8,128)(2,1)S(1)} %collective-permute-done.2.refs_3_, ...), custom_call_target="tpu_custom_call" | custom-call | tf_op jit(solution)/shard_map/pallas_call | solution.py:232
  44.6 1.1 %collective-permute-done.16 = f32[1,512]{1,0:T(1,128)S(1)} collective-permute-done((f32[1,512]{1,0:T(1,128)S(1)}, f32[1,512]{1,0:T(1,128)S(1)}, u32[]{:S(2)}, u32[]{:S(2)}) %collective-permute-start.16) | collective-permute-done | bytes 2080 | tf_op jit(solution)/shard_map/ppermute | solution.py:243
  45.8 1.5 %collective-permute-start.17 = (f32[1,512]{1,0:T(1,128)S(1)}, f32[1,512]{1,0:T(1,128)S(1)}, u32[]{:S(2)}, u32[]{:S(2)}) collective-permute-start(f32[1,512]{1,0:T(1,128)S(1)} %add.12), channel_id=1, source_target_pairs={{0,1},{1,0},{2,3},{3,2},{4,5},{5,4},{6,7},{7,6},{8,9},{9,8},{10,11... | collective-permute-start | bytes 6152 | tf_op jit(solution)/shard_map/ppermute | solution.py:244
  47.3 2.1 %collective-permute-done.17 = f32[1,512]{1,0:T(1,128)S(1)} collective-permute-done((f32[1,512]{1,0:T(1,128)S(1)}, f32[1,512]{1,0:T(1,128)S(1)}, u32[]{:S(2)}, u32[]{:S(2)}) %collective-permute-start.17) | collective-permute-done | bytes 2080 | tf_op jit(solution)/shard_map/ppermute | solution.py:244
  49.4 1.1 %broadcast_multiply_fusion = f32[512,512]{1,0:T(8,128)} fusion(f32[512,512]{1,0:T(8,128)S(1)} %get-tuple-element.27, f32[512]{0:T(512)S(1)} %bitcast.9), kind=kLoop, calls=%fused_computation | loop fusion | flops 262144 | bytes 2099200 | tf_op jit(solution)/shard_map/mul | solution.py:246
  (26 shorter events, 3.4 us)
Async XLA Ops:
  0.0 16.1 %collective-permute-start.10 = (bf16[4096,512]{1,0:T(8,128)(2,1)}, bf16[4096,512]{1,0:T(8,128)(2,1)}, u32[]{:S(2)}, u32[]{:S(2)}) collective-permute-start(bf16[4096,512]{1,0:T(8,128)(2,1)} %bitcast.6), channel_id=1, source_target_pairs={{0,16},{16,0},{1,17},{17,1},{2,18},{18,2},{3,19},{19,3},{4,20},{20... | collective-permute-start | bytes 12582920 | tf_op jit(solution)/shard_map/ppermute | solution.py:185
  2.8 7.2 %collective-permute-start.6 = (bf16[528,128]{1,0:T(8,128)(2,1)}, bf16[528,128]{1,0:T(8,128)(2,1)S(1)}, u32[]{:S(2)}, u32[]{:S(2)}) collective-permute-start(bf16[528,128]{1,0:T(8,128)(2,1)} %get-tuple-element.18.refs_0_), channel_id=1, source_target_pairs={{0,4},{4,8},{8,12},{12,14},{14,10},{10,6},{6,2},{2,0},{1,5},{5,9},... | collective-permute-start | bytes 405512 | tf_op jit(solution)/shard_map/ppermute | solution.py:144
  5.4 6.6 %collective-permute-start.7 = (bf16[528,128]{1,0:T(8,128)(2,1)}, bf16[528,128]{1,0:T(8,128)(2,1)S(1)}, u32[]{:S(2)}, u32[]{:S(2)}) collective-permute-start(bf16[528,128]{1,0:T(8,128)(2,1)} %get-tuple-element.18.refs_0_), channel_id=1, source_target_pairs={{4,0},{8,4},{12,8},{14,12},{10,14},{6,10},{2,6},{0,2},{5,1},{9,5},... | collective-permute-start | bytes 405512 | tf_op jit(solution)/shard_map/ppermute | solution.py:147
  5.5 8.7 %collective-permute-start = (bf16[528,128]{1,0:T(8,128)(2,1)}, bf16[528,128]{1,0:T(8,128)(2,1)S(1)}, u32[]{:S(2)}, u32[]{:S(2)}) collective-permute-start(bf16[528,128]{1,0:T(8,128)(2,1)} %get-tuple-element.17.refs_0_), channel_id=1, source_target_pairs={{0,4},{4,8},{8,12},{12,14},{14,10},{10,6},{6,2},{2,0},{1,5},{5,9},... | collective-permute-start | bytes 405512 | tf_op jit(solution)/shard_map/ppermute | solution.py:144
  7.5 8.2 %collective-permute-start.1 = (bf16[528,128]{1,0:T(8,128)(2,1)}, bf16[528,128]{1,0:T(8,128)(2,1)S(1)}, u32[]{:S(2)}, u32[]{:S(2)}) collective-permute-start(bf16[528,128]{1,0:T(8,128)(2,1)} %get-tuple-element.17.refs_0_), channel_id=1, source_target_pairs={{4,0},{8,4},{12,8},{14,12},{10,14},{6,10},{2,6},{0,2},{5,1},{9,5},... | collective-permute-start | bytes 405512 | tf_op jit(solution)/shard_map/ppermute | solution.py:147
  7.5 2.2 %copy-start = (bf16[1,4096,512]{2,1,0:T(8,128)(2,1)S(1)}, bf16[1,4096,512]{2,1,0:T(8,128)(2,1)}, u32[]{:S(2)}) copy-start(bf16[1,4096,512]{2,1,0:T(8,128)(2,1)} %param.5) | copy-start | bytes 12582916
  12.1 6.3 %collective-permute-start.8 = (bf16[528,128]{1,0:T(8,128)(2,1)S(1)}, bf16[528,128]{1,0:T(8,128)(2,1)S(1)}, u32[]{:S(2)}, u32[]{:S(2)}) collective-permute-start(bf16[528,128]{1,0:T(8,128)(2,1)S(1)} %collective-permute-done.6.refs_1_), channel_id=1, source_target_pairs={{0,4},{4,8},{8,12},{12,14},{14,10},{10,6},{6,2},{2,0},{1,5},{5,9},... | collective-permute-start | bytes 405512 | tf_op jit(solution)/shard_map/ppermute | solution.py:144
  13.7 5.8 %collective-permute-start.9 = (bf16[528,128]{1,0:T(8,128)(2,1)S(1)}, bf16[528,128]{1,0:T(8,128)(2,1)S(1)}, u32[]{:S(2)}, u32[]{:S(2)}) collective-permute-start(bf16[528,128]{1,0:T(8,128)(2,1)S(1)} %collective-permute-done.7.refs_2_), channel_id=1, source_target_pairs={{4,0},{8,4},{12,8},{14,12},{10,14},{6,10},{2,6},{0,2},{5,1},{9,5},... | collective-permute-start | bytes 405512 | tf_op jit(solution)/shard_map/ppermute | solution.py:147
  14.1 16.3 %copy-start.2 = (bf16[528,128]{1,0:T(8,128)(2,1)S(1)}, bf16[528,128]{1,0:T(8,128)(2,1)}, u32[]{:S(2)}) copy-start(bf16[528,128]{1,0:T(8,128)(2,1)} %get-tuple-element.18.refs_0_) | copy-start | bytes 405508
  14.1 7.0 %collective-permute-start.2 = (bf16[528,128]{1,0:T(8,128)(2,1)S(1)}, bf16[528,128]{1,0:T(8,128)(2,1)S(1)}, u32[]{:S(2)}, u32[]{:S(2)}) collective-permute-start(bf16[528,128]{1,0:T(8,128)(2,1)S(1)} %collective-permute-done.refs_1_), channel_id=1, source_target_pairs={{0,4},{4,8},{8,12},{12,14},{14,10},{10,6},{6,2},{2,0},{1,5},{5,9},... | collective-permute-start | bytes 405512 | tf_op jit(solution)/shard_map/ppermute | solution.py:144
  15.7 7.0 %collective-permute-start.3 = (bf16[528,128]{1,0:T(8,128)(2,1)S(1)}, bf16[528,128]{1,0:T(8,128)(2,1)S(1)}, u32[]{:S(2)}, u32[]{:S(2)}) collective-permute-start(bf16[528,128]{1,0:T(8,128)(2,1)S(1)} %collective-permute-done.1.refs_2_), channel_id=1, source_target_pairs={{4,0},{8,4},{12,8},{14,12},{10,14},{6,10},{2,6},{0,2},{5,1},{9,5},... | collective-permute-start | bytes 405512 | tf_op jit(solution)/shard_map/ppermute | solution.py:147
  18.3 24.4 %copy-start.1 = (bf16[528,128]{1,0:T(8,128)(2,1)S(1)}, bf16[528,128]{1,0:T(8,128)(2,1)}, u32[]{:S(2)}) copy-start(bf16[528,128]{1,0:T(8,128)(2,1)} %get-tuple-element.17.refs_0_) | copy-start | bytes 405508
  19.5 5.9 %collective-permute-start.11 = (bf16[528,128]{1,0:T(8,128)(2,1)S(1)}, bf16[528,128]{1,0:T(8,128)(2,1)S(1)}, u32[]{:S(2)}, u32[]{:S(2)}) collective-permute-start(bf16[528,128]{1,0:T(8,128)(2,1)S(1)} %collective-permute-done.8.refs_3_), channel_id=1, source_target_pairs={{0,4},{4,8},{8,12},{12,14},{14,10},{10,6},{6,2},{2,0},{1,5},{5,9},... | collective-permute-start | bytes 405512 | tf_op jit(solution)/shard_map/ppermute | solution.py:144
  21.1 6.3 %collective-permute-start.4 = (bf16[528,128]{1,0:T(8,128)(2,1)S(1)}, bf16[528,128]{1,0:T(8,128)(2,1)S(1)}, u32[]{:S(2)}, u32[]{:S(2)}) collective-permute-start(bf16[528,128]{1,0:T(8,128)(2,1)S(1)} %collective-permute-done.2.refs_3_), channel_id=1, source_target_pairs={{0,4},{4,8},{8,12},{12,14},{14,10},{10,6},{6,2},{2,0},{1,5},{5,9},... | collective-permute-start | bytes 405512 | tf_op jit(solution)/shard_map/ppermute | solution.py:144
  22.7 5.0 %collective-permute-start.5 = (bf16[528,128]{1,0:T(8,128)(2,1)S(1)}, bf16[528,128]{1,0:T(8,128)(2,1)S(1)}, u32[]{:S(2)}, u32[]{:S(2)}) collective-permute-start(bf16[528,128]{1,0:T(8,128)(2,1)S(1)} %collective-permute-done.3.refs_4_), channel_id=1, source_target_pairs={{4,0},{8,4},{12,8},{14,12},{10,14},{6,10},{2,6},{0,2},{5,1},{9,5},... | collective-permute-start | bytes 405512 | tf_op jit(solution)/shard_map/ppermute | solution.py:147
  23.1 6.0 %collective-permute-start.13 = (bf16[528,128]{1,0:T(8,128)(2,1)S(1)}, bf16[528,128]{1,0:T(8,128)(2,1)S(1)}, u32[]{:S(2)}, u32[]{:S(2)}) collective-permute-start(bf16[528,128]{1,0:T(8,128)(2,1)S(1)} %collective-permute-done.9.refs_4_), channel_id=1, source_target_pairs={{4,0},{8,4},{12,8},{14,12},{10,14},{6,10},{2,6},{0,2},{5,1},{9,5},... | collective-permute-start | bytes 405512 | tf_op jit(solution)/shard_map/ppermute | solution.py:147
  25.4 5.0 %collective-permute-start.12 = (bf16[528,128]{1,0:T(8,128)(2,1)S(1)}, bf16[528,128]{1,0:T(8,128)(2,1)S(1)}, u32[]{:S(2)}, u32[]{:S(2)}) collective-permute-start(bf16[528,128]{1,0:T(8,128)(2,1)S(1)} %collective-permute-done.11.refs_5_), channel_id=1, source_target_pairs={{0,4},{4,8},{8,12},{12,14},{14,10},{10,6},{6,2},{2,0},{1,5},{5,9},... | collective-permute-start | bytes 405512 | tf_op jit(solution)/shard_map/ppermute | solution.py:144
  32.3 10.4 %collective-permute-start.15 = (bf16[528,512]{1,0:T(8,128)(2,1)S(1)}, bf16[528,512]{1,0:T(8,128)(2,1)S(1)}, u32[]{:S(2)}, u32[]{:S(2)}) collective-permute-start(bf16[528,512]{1,0:T(8,128)(2,1)S(1)} %shard_map.40), channel_id=1, source_target_pairs={{0,1},{1,0},{2,3},{3,2},{4,5},{5,4},{6,7},{7,6},{8,9},{9,8},{10,11... | collective-permute-start | bytes 1622024 | tf_op jit(solution)/shard_map/ppermute | solution.py:231
  33.9 5.0 %collective-permute-start.14 = (bf16[528,128]{1,0:T(8,128)(2,1)S(1)}, bf16[528,128]{1,0:T(8,128)(2,1)S(1)}, u32[]{:S(2)}, u32[]{:S(2)}) collective-permute-start(bf16[528,128]{1,0:T(8,128)(2,1)S(1)} %collective-permute-done.5.refs_6_), channel_id=1, source_target_pairs={{4,0},{8,4},{12,8},{14,12},{10,14},{6,10},{2,6},{0,2},{5,1},{9,5},... | collective-permute-start | bytes 405512 | tf_op jit(solution)/shard_map/ppermute | solution.py:147
  44.6 1.2 %collective-permute-start.16 = (f32[1,512]{1,0:T(1,128)S(1)}, f32[1,512]{1,0:T(1,128)S(1)}, u32[]{:S(2)}, u32[]{:S(2)}) collective-permute-start(f32[1,512]{1,0:T(1,128)S(1)} %get-tuple-element.28), channel_id=1, source_target_pairs={{0,16},{16,0},{1,17},{17,1},{2,18},{18,2},{3,19},{19,3},{4,20},{20... | collective-permute-start | bytes 6152 | tf_op jit(solution)/shard_map/ppermute | solution.py:243
  45.8 3.6 %collective-permute-start.17 = (f32[1,512]{1,0:T(1,128)S(1)}, f32[1,512]{1,0:T(1,128)S(1)}, u32[]{:S(2)}, u32[]{:S(2)}) collective-permute-start(f32[1,512]{1,0:T(1,128)S(1)} %add.12), channel_id=1, source_target_pairs={{0,1},{1,0},{2,3},{3,2},{4,5},{5,4},{6,7},{7,6},{8,9},{9,8},{10,11... | collective-permute-start | bytes 6152 | tf_op jit(solution)/shard_map/ppermute | solution.py:244

commit v3 on v2

v3 whole, which is shorter than its diff:
```python
import functools

import jax
import jax.numpy as jnp
from jax import lax
from jax.experimental import pallas as pl
from jax.experimental.pallas import tpu as pltpu
from jax.sharding import PartitionSpec as P

CODE_SPAN = 250.0
CODE_MID = 125.0
LOG2E = 1.4426950408889634
ID_ROWS = 16
VMEM_BYTES = 24 * 1024 * 1024
PLAN = ("S1", "K1", "S=W", "S2", "K2", "J", "S=W", "Sf2", "S3", "S=K", "Kf2", "K3")
PLACE_LIMIT = 24 << 20


def pack_kernel(cols_ref, vals_ref, *refs):
    outs, sems = refs[:-1], refs[-1]
    rows = outs[0].shape[0] - ID_ROWS
    block = vals_ref.shape[1]
    layer = lax.axis_index("layer")
    copies = []
    for k, out in enumerate(outs):
        part = 1 - layer if k < len(outs) // 2 else layer
        copies.append(
            pltpu.make_async_copy(
                vals_ref.at[pl.ds(pl.multiple_of(part * rows, block), rows)],
                out.at[pl.ds(0, rows)],
                sems.at[k],
            )
        )
        copies[-1].start()
    line = cols_ref[...].astype(jnp.float32).astype(jnp.bfloat16)
    for out in outs:
        out[rows : rows + ID_ROWS, 0 : line.shape[1]] = jnp.broadcast_to(line, (ID_ROWS, line.shape[1]))
    for copy in copies:
        copy.wait()


def place_kernel(mine, part_ref, *refs):
    window_ref, sem = refs[-2:]
    half = part_ref.shape[0]
    row = lax.axis_index("row")
    where = pl.ds(pl.multiple_of((row if mine else 1 - row) * half, half), half)
    copy = pltpu.make_async_copy(part_ref, window_ref.at[where], sem)
    copy.start()
    copy.wait()


def products(part, items, window, ids_v, ids_s, sem, finish):
    block = items[0].shape[1]
    rows = items[0].shape[0] - ID_ROWS
    live_end = window.shape[0] // block
    for s, item in enumerate(items):
        ids_v[pl.ds(s, 1)] = item[rows : rows + 1, :].astype(jnp.float32).astype(jnp.int32)
    to_scalar = pltpu.make_async_copy(ids_v, ids_s, sem)
    to_scalar.start()
    to_scalar.wait()
    for j in range(rows // block):
        left, right = [], []
        for s in range(len(items)):
            col = ids_s[s, part * (rows // block) + j]
            live = jnp.where(col < live_end, 1.0, 0.0).astype(jnp.float32)
            piece = items[s][j * block : (j + 1) * block, :]
            left.append((piece.astype(jnp.float32) * live).astype(jnp.bfloat16))
            at = pl.multiple_of(jnp.minimum(col, live_end - 1) * block, block)
            right.append(window[pl.ds(at, block), :])
        finish(
            j,
            jnp.dot(
                jnp.concatenate(left, axis=1),
                jnp.concatenate(right, axis=0),
                preferred_element_type=jnp.float32,
            ),
        )


def send_kernel(slots, *refs):
    items, (window, code_ref, ids_v, ids_s, total, sem) = refs[:slots], refs[slots:]
    block = items[0].shape[1]
    rows = total.shape[0]

    def finish(j, value):
        total[j * block : (j + 1) * block, :] = value

    products(1 - lax.axis_index("layer"), items, window, ids_v, ids_s, sem, finish)
    most = jnp.max(jnp.abs(total[...]), axis=0, keepdims=True)
    scale = (most * 1.01 + 1e-30).astype(jnp.bfloat16)
    inverse = CODE_SPAN / scale.astype(jnp.float32)
    for j in range(rows // block):
        value = total[j * block : (j + 1) * block, :]
        size = jnp.exp((jnp.abs(value) * inverse - CODE_MID) * (1.0 / LOG2E))
        code_ref[j * block : (j + 1) * block, :] = jnp.where(value < 0, -size, size).astype(jnp.bfloat16)
    code_ref[rows : rows + ID_ROWS, :] = jnp.broadcast_to(scale, (ID_ROWS, scale.shape[1]))


def keep_kernel(slots, *refs):
    items, (window, code_ref, square_ref, sum_ref, ids_v, ids_s, sem) = refs[:slots], refs[slots:]
    block = items[0].shape[1]
    rows = square_ref.shape[0]
    scale = code_ref[rows : rows + 1, :].astype(jnp.float32) * (1.0 / CODE_SPAN)
    sums = []

    def finish(j, value):
        code = code_ref[j * block : (j + 1) * block, :].astype(jnp.float32)
        size = (jnp.log(jnp.abs(code)) * LOG2E + CODE_MID) * scale
        full = value + jnp.where(code < 0, -size, size)
        square = full * full
        square_ref[j * block : (j + 1) * block, :] = square
        sums.append(jnp.sum(square, axis=0, keepdims=True))

    products(lax.axis_index("layer"), items, window, ids_v, ids_s, sem, finish)
    sum_ref[...] = functools.reduce(jnp.add, sums)


def ring_of(mesh):
    size = mesh.shape["col"]
    if size != 8:
        return list(range(size))
    return [0, 2, 4, 6, 7, 5, 3, 1]


def solution(mesh):
    size = mesh.shape["col"]
    order = ring_of(mesh)
    def shift(hops):
        return [(order[i], order[(i + hops) % size]) for i in range(size)]

    swap = [(0, 1), (1, 0)]
    vmem = pl.BlockSpec(memory_space=pltpu.VMEM)
    anywhere = pl.BlockSpec(memory_space=pl.ANY)

    def gather_two(send, keep, window, join):
        streams = {"S": [send[2]], "K": [keep[2]]}
        ends = {"S": send[:2], "K": keep[:2]}

        def move(name):
            kind = name[0]
            items = streams[kind]
            if name[1] == "f":
                hops = int(name[2])
                front, rear = ends[kind]
                src = front if kind == "S" else rear
                items.append(lax.ppermute(src, "col", shift(hops if kind == "S" else -hops)))
                return
            front, rear = ends[kind]
            front = lax.ppermute(front, "col", shift(1))
            rear = lax.ppermute(rear, "col", shift(-1))
            items.extend((front, rear))
            ends[kind] = (front, rear)

        def tie(*names):
            nonlocal window
            values = lax.optimization_barrier(tuple(window if n == "W" else (ends[n], streams[n][-1]) for n in names))
            for n, v in zip(names, values):
                if n == "W":
                    window = v
                else:
                    ends[n] = v[0]
                    streams[n][-1] = v[1]

        for name in PLAN:
            if name == "J":
                window = join(window)
            elif "=" in name:
                tie(*name.split("="))
            else:
                move(name)
        return streams["S"], streams["K"], window

    def gather_all(item):
        stacked = lax.all_gather(item, "col", axis=0)
        return [stacked[i] for i in range(size)]

    def body(flow_cols, flow_vals, window_flow):
        block = flow_vals.shape[-1]
        count = flow_vals.shape[0] // 2
        rows = count * block
        own = window_flow[0]
        half, columns = own.shape
        other = lax.ppermute(own, "row", swap)
        item = jax.ShapeDtypeStruct((rows + ID_ROWS, block), flow_vals.dtype)
        params = pltpu.CompilerParams(vmem_limit_bytes=VMEM_BYTES)
        items = pl.pallas_call(
            pack_kernel,
            out_shape=(item,) * 2,
            in_specs=[vmem, anywhere],
            out_specs=(vmem,) * 2,
            scratch_shapes=[pltpu.SemaphoreType.DMA((2,))],
            compiler_params=params,
        )(flow_cols.reshape(1, 2 * count), flow_vals.reshape(2 * rows, block))
        send, keep = items[:1] * 3, items[1:] * 3

        def place(mine, part, window=None):
            given = [] if window is None else [window]
            return pl.pallas_call(
                functools.partial(place_kernel, mine),
                out_shape=jax.ShapeDtypeStruct((2 * half, columns), own.dtype),
                in_specs=[anywhere] + [vmem] * len(given),
                out_specs=vmem,
                scratch_shapes=[pltpu.SemaphoreType.DMA(())],
                input_output_aliases={1: 0} if given else {},
                compiler_params=pltpu.CompilerParams(vmem_limit_bytes=PLACE_LIMIT),
                cost_estimate=pl.CostEstimate(flops=0, bytes_accessed=2 * half * columns * 2, transcendentals=0),
            )(part, *given)

        window = place(True, own)
        if size == 8:
            sends, keeps, window = gather_two(send, keep, window, lambda w: place(False, other, w))
        else:
            sends, keeps = gather_all(send[0]), gather_all(keep[0])
            window = place(False, other, window)
        scratch = [
            pltpu.VMEM((max(size, 8), block), jnp.int32),
            pltpu.SMEM((max(size, 8), block), jnp.int32),
        ]
        sems = [pltpu.SemaphoreType.DMA(())]
        item_specs = [vmem] * size
        code = pl.pallas_call(
            functools.partial(send_kernel, size),
            out_shape=jax.ShapeDtypeStruct((rows + ID_ROWS, columns), jnp.bfloat16),
            in_specs=item_specs + [vmem],
            out_specs=vmem,
            scratch_shapes=scratch + [pltpu.VMEM((rows, columns), jnp.float32)] + sems,
            compiler_params=params,
        )(*sends, window)
        code = lax.ppermute(code, "layer", swap)
        square, sums = pl.pallas_call(
            functools.partial(keep_kernel, size),
            out_shape=(
                jax.ShapeDtypeStruct((rows, columns), jnp.float32),
                jax.ShapeDtypeStruct((1, columns), jnp.float32),
            ),
            in_specs=item_specs + [vmem, vmem],
            out_specs=(vmem, vmem),
            scratch_shapes=scratch + sems,
            compiler_params=params,
        )(*keeps, window, code)
        sums = sums + lax.ppermute(sums, "row", swap)
        sums = sums + lax.ppermute(sums, "layer", swap)
        total_rows = rows * lax.axis_size("row") * lax.axis_size("layer")
        return square * (1.0 / (sums / total_rows + 1e-6))

    placed = (
        P("row", "layer", "col"),
        P("row", "layer", "col", None, None),
        P("layer", "row", "col"),
    )
    return jax.shard_map(body, mesh=mesh, in_specs=placed, out_specs=P(("row", "layer"), "col"), check_vma=False)
```

time: 50.7 us -> 48.2 us (0.951)
  the two profiles are of different devices: /device:TPU:0 before, /device:TPU:4 now
where the time goes in v3:
time: 48.2 us; the launch traced here: 48.1 us
  waiting for transfers between devices  20.2 us (42%)
  starting transfers between devices  18.6 us (39%)
  Pallas kernels  4.22 us (9%)
  local copies, waits for them, and re-layouts  3.79 us (8%)
  other arithmetic  1.12 us (2%)
    ppermute x6, starting transfers between devices, move(): rear = lax.ppermute(rear, 'col', shift(-1))  8.31 us
    ppermute x2, waiting for transfers between devices, move(): lax.ppermute(src, 'col', shift(hops if kind == 'S' else -hops))  5.94 us
    ppermute x6, starting transfers between devices, move(): front = lax.ppermute(front, 'col', shift(1))  5.07 us
    unnamed x6, local copies, waits for them, and re-layouts  3.79 us
    ppermute x6, waiting for transfers between devices, move(): rear = lax.ppermute(rear, 'col', shift(-1))  3.7 us
    ppermute x2, starting transfers between devices, move(): lax.ppermute(src, 'col', shift(hops if kind == 'S' else -hops))  3.34 us
    ppermute x1, waiting for transfers between devices, body(): sums = sums + lax.ppermute(sums, 'layer', swap)  3.3 us
    ppermute x1, waiting for transfers between devices, body(): code = lax.ppermute(code, 'layer', swap)  3.13 us
  transfers between devices with their start and end apart: 18, of which 12 were waited for; matrix products, arithmetic and copies ran while one was open for 0% of the time, Pallas kernels for 2%

profile of v3, /device:TPU:4, one launch (start us, length us, event | category | flops | bytes accessed | tf_op | source)
XLA Modules:
  0.0 48.1 jit_solution(6884719156179257597)
XLA Ops:
  0.0 0.9 %copy-done.1 = bf16[8,1,1,128,128]{4,3,2,1,0:T(8,128)(2,1)S(1)} copy-done((bf16[8,1,1,128,128]{4,3,2,1,0:T(8,128)(2,1)S(1)}, bf16[8,1,1,128,128]{4,3,2,1,0:T(8,128)(2,1)}, u32[]{:S(2)}) %copy-start.1) | copy-done | bytes 262168
  2.0 2.0 %collective-permute-start.4 = (bf16[528,128]{1,0:T(8,128)(2,1)S(1)}, bf16[528,128]{1,0:T(8,128)(2,1)S(1)}, u32[]{:S(2)}, u32[]{:S(2)}) collective-permute-start(bf16[528,128]{1,0:T(8,128)(2,1)S(1)} %get-tuple-element.22.refs_0_), channel_id=1, source_target_pairs={{0,2},{4,0},{8,4},{12,8},{14,12},{10,14},{6,10},{2,6},{1,3},{5,1},... | collective-permute-start | bytes 405512 | tf_op jit(solution)/shard_map/ppermute | solution.py:150
  4.1 2.0 %collective-permute-start.1 = (bf16[528,128]{1,0:T(8,128)(2,1)S(1)}, bf16[528,128]{1,0:T(8,128)(2,1)S(1)}, u32[]{:S(2)}, u32[]{:S(2)}) collective-permute-start(bf16[528,128]{1,0:T(8,128)(2,1)S(1)} %get-tuple-element.21.refs_0_), channel_id=1, source_target_pairs={{0,2},{4,0},{8,4},{12,8},{14,12},{10,14},{6,10},{2,6},{1,3},{5,1},... | collective-permute-start | bytes 405512 | tf_op jit(solution)/shard_map/ppermute | solution.py:150
  6.1 2.2 %copy-done = bf16[1,4096,512]{2,1,0:T(8,128)(2,1)S(1)} copy-done((bf16[1,4096,512]{2,1,0:T(8,128)(2,1)S(1)}, bf16[1,4096,512]{2,1,0:T(8,128)(2,1)}, u32[]{:S(2)}) %copy-start) | copy-done | bytes 4194328
  8.6 1.9 %collective-permute-start.5 = (bf16[528,128]{1,0:T(8,128)(2,1)S(1)}, bf16[528,128]{1,0:T(8,128)(2,1)S(1)}, u32[]{:S(2)}, u32[]{:S(2)}) collective-permute-start(bf16[528,128]{1,0:T(8,128)(2,1)S(1)} %collective-permute-done.3.refs_1_), channel_id=1, source_target_pairs={{0,4},{4,8},{8,12},{12,14},{14,10},{10,6},{6,2},{2,0},{1,5},{5,9},... | collective-permute-start | bytes 405512 | tf_op jit(solution)/shard_map/ppermute | solution.py:149
  11.1 1.4 %collective-permute-start.2 = (bf16[528,128]{1,0:T(8,128)(2,1)S(1)}, bf16[528,128]{1,0:T(8,128)(2,1)S(1)}, u32[]{:S(2)}, u32[]{:S(2)}) collective-permute-start(bf16[528,128]{1,0:T(8,128)(2,1)S(1)} %collective-permute-done.refs_1_), channel_id=1, source_target_pairs={{0,4},{4,8},{8,12},{12,14},{14,10},{10,6},{6,2},{2,0},{1,5},{5,9},... | collective-permute-start | bytes 405512 | tf_op jit(solution)/shard_map/ppermute | solution.py:149
  13.5 0.9 %collective-permute-done.5.refs_3_ = bf16[528,128]{1,0:T(8,128)(2,1)S(1)} collective-permute-done((bf16[528,128]{1,0:T(8,128)(2,1)S(1)}, bf16[528,128]{1,0:T(8,128)(2,1)S(1)}, u32[]{:S(2)}, u32[]{:S(2)}) %collective-permute-start.5) | collective-permute-done | bytes 135200 | tf_op jit(solution)/shard_map/ppermute | solution.py:149
  14.4 2.0 %collective-permute-done.6.refs_4_ = bf16[528,128]{1,0:T(8,128)(2,1)S(1)} collective-permute-done((bf16[528,128]{1,0:T(8,128)(2,1)S(1)}, bf16[528,128]{1,0:T(8,128)(2,1)S(1)}, u32[]{:S(2)}, u32[]{:S(2)}) %collective-permute-start.6) | collective-permute-done | bytes 135200 | tf_op jit(solution)/shard_map/ppermute | solution.py:150
  16.3 1.6 %collective-permute-start.8 = (bf16[528,128]{1,0:T(8,128)(2,1)S(1)}, bf16[528,128]{1,0:T(8,128)(2,1)S(1)}, u32[]{:S(2)}, u32[]{:S(2)}) collective-permute-start(bf16[528,128]{1,0:T(8,128)(2,1)S(1)} %collective-permute-done.5.refs_3_), channel_id=1, source_target_pairs={{0,4},{4,8},{8,12},{12,14},{14,10},{10,6},{6,2},{2,0},{1,5},{5,9},... | collective-permute-start | bytes 405512 | tf_op jit(solution)/shard_map/ppermute | solution.py:149
  18.4 2.6 %collective-permute-start.14 = (bf16[528,128]{1,0:T(8,128)(2,1)S(1)}, bf16[528,128]{1,0:T(8,128)(2,1)S(1)}, u32[]{:S(2)}, u32[]{:S(2)}) collective-permute-start(bf16[528,128]{1,0:T(8,128)(2,1)S(1)} %collective-permute-done.5.refs_3_), channel_id=1, source_target_pairs={{0,8},{4,12},{8,14},{12,10},{14,6},{10,2},{6,0},{2,4},{1,9},{5,13}... | collective-permute-start | bytes 405512 | tf_op jit(solution)/shard_map/ppermute | solution.py:146
  21.0 1.0 %collective-permute-done.8.refs_6_ = bf16[528,128]{1,0:T(8,128)(2,1)S(1)} collective-permute-done((bf16[528,128]{1,0:T(8,128)(2,1)S(1)}, bf16[528,128]{1,0:T(8,128)(2,1)S(1)}, u32[]{:S(2)}, u32[]{:S(2)}) %collective-permute-start.8) | collective-permute-done | bytes 135200 | tf_op jit(solution)/shard_map/ppermute | solution.py:149
  22.0 1.0 %collective-permute-done.9.refs_7_ = bf16[528,128]{1,0:T(8,128)(2,1)S(1)} collective-permute-done((bf16[528,128]{1,0:T(8,128)(2,1)S(1)}, bf16[528,128]{1,0:T(8,128)(2,1)S(1)}, u32[]{:S(2)}, u32[]{:S(2)}) %collective-permute-start.9) | collective-permute-done | bytes 135200 | tf_op jit(solution)/shard_map/ppermute | solution.py:150
  22.9 3.6 %collective-permute-done.14.refs_5_ = bf16[528,128]{1,0:T(8,128)(2,1)S(1)} collective-permute-done((bf16[528,128]{1,0:T(8,128)(2,1)S(1)}, bf16[528,128]{1,0:T(8,128)(2,1)S(1)}, u32[]{:S(2)}, u32[]{:S(2)}) %collective-permute-start.14) | collective-permute-done | bytes 135200 | tf_op jit(solution)/shard_map/ppermute | solution.py:146
  26.5 1.7 %shard_map.40 = bf16[528,512]{1,0:T(8,128)(2,1)S(1)} custom-call(bf16[528,128]{1,0:T(8,128)(2,1)S(1)} %get-tuple-element.22.refs_0_, bf16[528,128]{1,0:T(8,128)(2,1)S(1)} %collective-permute-done.3.refs_1_, bf16[528,128]{1,0:T(8,128)(2,1)S(1)} %collective-permute-done.4.refs_2_, bf16[528,128]{1,0:T(8,128)(2,1)S(1)} %collective-permute-done.5.refs_3_, ...), custom_call_target="tpu_custom_call" | custom-call | tf_op jit(solution)/shard_map/pallas_call | solution.py:221
  28.2 1.6 %collective-permute-start.15 = (bf16[528,512]{1,0:T(8,128)(2,1)S(1)}, bf16[528,512]{1,0:T(8,128)(2,1)S(1)}, u32[]{:S(2)}, u32[]{:S(2)}) collective-permute-start(bf16[528,512]{1,0:T(8,128)(2,1)S(1)} %shard_map.40), channel_id=1, source_target_pairs={{0,1},{1,0},{2,3},{3,2},{4,5},{5,4},{6,7},{7,6},{8,9},{9,8},{10,11... | collective-permute-start | bytes 1622024 | tf_op jit(solution)/shard_map/ppermute | solution.py:229
  29.8 0.7 %collective-permute-start.11 = (bf16[528,128]{1,0:T(8,128)(2,1)S(1)}, bf16[528,128]{1,0:T(8,128)(2,1)S(1)}, u32[]{:S(2)}, u32[]{:S(2)}) collective-permute-start(bf16[528,128]{1,0:T(8,128)(2,1)S(1)} %collective-permute-done.10.refs_4_), channel_id=1, source_target_pairs={{0,6},{4,2},{8,0},{12,4},{14,8},{10,12},{6,14},{2,10},{1,7},{5,3},... | collective-permute-start | bytes 405512 | tf_op jit(solution)/shard_map/ppermute | solution.py:146
  30.5 3.2 %collective-permute-start.13 = (bf16[528,128]{1,0:T(8,128)(2,1)S(1)}, bf16[528,128]{1,0:T(8,128)(2,1)S(1)}, u32[]{:S(2)}, u32[]{:S(2)}) collective-permute-start(bf16[528,128]{1,0:T(8,128)(2,1)S(1)} %collective-permute-done.10.refs_4_), channel_id=1, source_target_pairs={{0,2},{4,0},{8,4},{12,8},{14,12},{10,14},{6,10},{2,6},{1,3},{5,1},... | collective-permute-start | bytes 405512 | tf_op jit(solution)/shard_map/ppermute | solution.py:150
  33.7 2.4 %collective-permute-done.11.refs_5_ = bf16[528,128]{1,0:T(8,128)(2,1)S(1)} collective-permute-done((bf16[528,128]{1,0:T(8,128)(2,1)S(1)}, bf16[528,128]{1,0:T(8,128)(2,1)S(1)}, u32[]{:S(2)}, u32[]{:S(2)}) %collective-permute-start.11) | collective-permute-done | bytes 135200 | tf_op jit(solution)/shard_map/ppermute | solution.py:146
  36.6 0.8 %collective-permute-done.13.refs_7_ = bf16[528,128]{1,0:T(8,128)(2,1)S(1)} collective-permute-done((bf16[528,128]{1,0:T(8,128)(2,1)S(1)}, bf16[528,128]{1,0:T(8,128)(2,1)S(1)}, u32[]{:S(2)}, u32[]{:S(2)}) %collective-permute-start.13) | collective-permute-done | bytes 135200 | tf_op jit(solution)/shard_map/ppermute | solution.py:150
  37.4 3.1 %collective-permute-done.15.refs_9_ = bf16[528,512]{1,0:T(8,128)(2,1)S(1)} collective-permute-done((bf16[528,512]{1,0:T(8,128)(2,1)S(1)}, bf16[528,512]{1,0:T(8,128)(2,1)S(1)}, u32[]{:S(2)}, u32[]{:S(2)}) %collective-permute-start.15) | collective-permute-done | bytes 540704 | tf_op jit(solution)/shard_map/ppermute | solution.py:229
  40.5 1.6 %shard_map.41 = (f32[512,512]{1,0:T(8,128)S(1)}, f32[1,512]{1,0:T(1,128)S(1)}) custom-call(bf16[528,128]{1,0:T(8,128)(2,1)S(1)} %get-tuple-element.21.refs_0_, bf16[528,128]{1,0:T(8,128)(2,1)S(1)} %collective-permute-done.refs_1_, bf16[528,128]{1,0:T(8,128)(2,1)S(1)} %collective-permute-done.1.refs_2_, bf16[528,128]{1,0:T(8,128)(2,1)S(1)} %collective-permute-done.2.refs_3_, ...), custom_call_target="tpu_custom_call" | custom-call | tf_op jit(solution)/shard_map/pallas_call | solution.py:230
  42.2 1.1 %collective-permute-done.16 = f32[1,512]{1,0:T(1,128)S(1)} collective-permute-done((f32[1,512]{1,0:T(1,128)S(1)}, f32[1,512]{1,0:T(1,128)S(1)}, u32[]{:S(2)}, u32[]{:S(2)}) %collective-permute-start.16) | collective-permute-done | bytes 2080 | tf_op jit(solution)/shard_map/ppermute | solution.py:241
  43.6 3.3 %collective-permute-done.17 = f32[1,512]{1,0:T(1,128)S(1)} collective-permute-done((f32[1,512]{1,0:T(1,128)S(1)}, f32[1,512]{1,0:T(1,128)S(1)}, u32[]{:S(2)}, u32[]{:S(2)}) %collective-permute-start.17) | collective-permute-done | bytes 2080 | tf_op jit(solution)/shard_map/ppermute | solution.py:242
  47.0 1.1 %broadcast_multiply_fusion = f32[512,512]{1,0:T(8,128)} fusion(f32[512,512]{1,0:T(8,128)S(1)} %get-tuple-element.35, f32[512]{0:T(512)S(1)} %bitcast.8), kind=kLoop, calls=%fused_computation | loop fusion | flops 262144 | bytes 2099200 | tf_op jit(solution)/shard_map/mul | solution.py:244
  (26 shorter events, 4.3 us)
Async XLA Ops:
  0.0 13.2 %collective-permute-start.7 = (bf16[4096,512]{1,0:T(8,128)(2,1)}, bf16[4096,512]{1,0:T(8,128)(2,1)S(1)}, u32[]{:S(2)}, u32[]{:S(2)}) collective-permute-start(bf16[4096,512]{1,0:T(8,128)(2,1)} %bitcast.4), channel_id=1, source_target_pairs={{0,16},{16,0},{1,17},{17,1},{2,18},{18,2},{3,19},{19,3},{4,20},{20... | collective-permute-start | bytes 12582920 | tf_op jit(solution)/shard_map/ppermute | solution.py:183
  0.0 1.0 %copy-start.1 = (bf16[8,1,1,128,128]{4,3,2,1,0:T(8,128)(2,1)S(1)}, bf16[8,1,1,128,128]{4,3,2,1,0:T(8,128)(2,1)}, u32[]{:S(2)}) copy-start(bf16[8,1,1,128,128]{4,3,2,1,0:T(8,128)(2,1)} %param.4) | copy-start | bytes 786436
  1.0 0.7 %copy-start.2 = (s32[8,1,1]{0,2,1:T(1,128)S(1)}, s32[8,1,1]{0,2,1:T(1,128)}, u32[]{:S(2)}) copy-start(s32[8,1,1]{0,2,1:T(1,128)} %param.3) | copy-start | bytes 100
  1.9 6.6 %collective-permute-start.3 = (bf16[528,128]{1,0:T(8,128)(2,1)S(1)}, bf16[528,128]{1,0:T(8,128)(2,1)S(1)}, u32[]{:S(2)}, u32[]{:S(2)}) collective-permute-start(bf16[528,128]{1,0:T(8,128)(2,1)S(1)} %get-tuple-element.22.refs_0_), channel_id=1, source_target_pairs={{0,4},{4,8},{8,12},{12,14},{14,10},{10,6},{6,2},{2,0},{1,5},{5,9},... | collective-permute-start | bytes 405512 | tf_op jit(solution)/shard_map/ppermute | solution.py:149
  2.0 6.5 %collective-permute-start.4 = (bf16[528,128]{1,0:T(8,128)(2,1)S(1)}, bf16[528,128]{1,0:T(8,128)(2,1)S(1)}, u32[]{:S(2)}, u32[]{:S(2)}) collective-permute-start(bf16[528,128]{1,0:T(8,128)(2,1)S(1)} %get-tuple-element.22.refs_0_), channel_id=1, source_target_pairs={{0,2},{4,0},{8,4},{12,8},{14,12},{10,14},{6,10},{2,6},{1,3},{5,1},... | collective-permute-start | bytes 405512 | tf_op jit(solution)/shard_map/ppermute | solution.py:150
  4.0 7.1 %collective-permute-start = (bf16[528,128]{1,0:T(8,128)(2,1)S(1)}, bf16[528,128]{1,0:T(8,128)(2,1)S(1)}, u32[]{:S(2)}, u32[]{:S(2)}) collective-permute-start(bf16[528,128]{1,0:T(8,128)(2,1)S(1)} %get-tuple-element.21.refs_0_), channel_id=1, source_target_pairs={{0,4},{4,8},{8,12},{12,14},{14,10},{10,6},{6,2},{2,0},{1,5},{5,9},... | collective-permute-start | bytes 405512 | tf_op jit(solution)/shard_map/ppermute | solution.py:149
  4.1 8.4 %collective-permute-start.1 = (bf16[528,128]{1,0:T(8,128)(2,1)S(1)}, bf16[528,128]{1,0:T(8,128)(2,1)S(1)}, u32[]{:S(2)}, u32[]{:S(2)}) collective-permute-start(bf16[528,128]{1,0:T(8,128)(2,1)S(1)} %get-tuple-element.21.refs_0_), channel_id=1, source_target_pairs={{0,2},{4,0},{8,4},{12,8},{14,12},{10,14},{6,10},{2,6},{1,3},{5,1},... | collective-permute-start | bytes 405512 | tf_op jit(solution)/shard_map/ppermute | solution.py:150
  6.1 2.2 %copy-start = (bf16[1,4096,512]{2,1,0:T(8,128)(2,1)S(1)}, bf16[1,4096,512]{2,1,0:T(8,128)(2,1)}, u32[]{:S(2)}) copy-start(bf16[1,4096,512]{2,1,0:T(8,128)(2,1)} %param.5) | copy-start | bytes 12582916
  8.6 5.8 %collective-permute-start.5 = (bf16[528,128]{1,0:T(8,128)(2,1)S(1)}, bf16[528,128]{1,0:T(8,128)(2,1)S(1)}, u32[]{:S(2)}, u32[]{:S(2)}) collective-permute-start(bf16[528,128]{1,0:T(8,128)(2,1)S(1)} %collective-permute-done.3.refs_1_), channel_id=1, source_target_pairs={{0,4},{4,8},{8,12},{12,14},{14,10},{10,6},{6,2},{2,0},{1,5},{5,9},... | collective-permute-start | bytes 405512 | tf_op jit(solution)/shard_map/ppermute | solution.py:149
  10.5 5.8 %collective-permute-start.6 = (bf16[528,128]{1,0:T(8,128)(2,1)S(1)}, bf16[528,128]{1,0:T(8,128)(2,1)S(1)}, u32[]{:S(2)}, u32[]{:S(2)}) collective-permute-start(bf16[528,128]{1,0:T(8,128)(2,1)S(1)} %collective-permute-done.4.refs_2_), channel_id=1, source_target_pairs={{0,2},{4,0},{8,4},{12,8},{14,12},{10,14},{6,10},{2,6},{1,3},{5,1},... | collective-permute-start | bytes 405512 | tf_op jit(solution)/shard_map/ppermute | solution.py:150
  11.1 9.8 %collective-permute-start.2 = (bf16[528,128]{1,0:T(8,128)(2,1)S(1)}, bf16[528,128]{1,0:T(8,128)(2,1)S(1)}, u32[]{:S(2)}, u32[]{:S(2)}) collective-permute-start(bf16[528,128]{1,0:T(8,128)(2,1)S(1)} %collective-permute-done.refs_1_), channel_id=1, source_target_pairs={{0,4},{4,8},{8,12},{12,14},{14,10},{10,6},{6,2},{2,0},{1,5},{5,9},... | collective-permute-start | bytes 405512 | tf_op jit(solution)/shard_map/ppermute | solution.py:149
  12.5 8.4 %collective-permute-start.10 = (bf16[528,128]{1,0:T(8,128)(2,1)S(1)}, bf16[528,128]{1,0:T(8,128)(2,1)S(1)}, u32[]{:S(2)}, u32[]{:S(2)}) collective-permute-start(bf16[528,128]{1,0:T(8,128)(2,1)S(1)} %collective-permute-done.1.refs_2_), channel_id=1, source_target_pairs={{0,2},{4,0},{8,4},{12,8},{14,12},{10,14},{6,10},{2,6},{1,3},{5,1},... | collective-permute-start | bytes 405512 | tf_op jit(solution)/shard_map/ppermute | solution.py:150
  16.3 5.6 %collective-permute-start.8 = (bf16[528,128]{1,0:T(8,128)(2,1)S(1)}, bf16[528,128]{1,0:T(8,128)(2,1)S(1)}, u32[]{:S(2)}, u32[]{:S(2)}) collective-permute-start(bf16[528,128]{1,0:T(8,128)(2,1)S(1)} %collective-permute-done.5.refs_3_), channel_id=1, source_target_pairs={{0,4},{4,8},{8,12},{12,14},{14,10},{10,6},{6,2},{2,0},{1,5},{5,9},... | collective-permute-start | bytes 405512 | tf_op jit(solution)/shard_map/ppermute | solution.py:149
  17.9 5.0 %collective-permute-start.9 = (bf16[528,128]{1,0:T(8,128)(2,1)S(1)}, bf16[528,128]{1,0:T(8,128)(2,1)S(1)}, u32[]{:S(2)}, u32[]{:S(2)}) collective-permute-start(bf16[528,128]{1,0:T(8,128)(2,1)S(1)} %collective-permute-done.6.refs_4_), channel_id=1, source_target_pairs={{0,2},{4,0},{8,4},{12,8},{14,12},{10,14},{6,10},{2,6},{1,3},{5,1},... | collective-permute-start | bytes 405512 | tf_op jit(solution)/shard_map/ppermute | solution.py:150
  18.4 8.1 %collective-permute-start.14 = (bf16[528,128]{1,0:T(8,128)(2,1)S(1)}, bf16[528,128]{1,0:T(8,128)(2,1)S(1)}, u32[]{:S(2)}, u32[]{:S(2)}) collective-permute-start(bf16[528,128]{1,0:T(8,128)(2,1)S(1)} %collective-permute-done.5.refs_3_), channel_id=1, source_target_pairs={{0,8},{4,12},{8,14},{12,10},{14,6},{10,2},{6,0},{2,4},{1,9},{5,13}... | collective-permute-start | bytes 405512 | tf_op jit(solution)/shard_map/ppermute | solution.py:146
  28.2 12.3 %collective-permute-start.15 = (bf16[528,512]{1,0:T(8,128)(2,1)S(1)}, bf16[528,512]{1,0:T(8,128)(2,1)S(1)}, u32[]{:S(2)}, u32[]{:S(2)}) collective-permute-start(bf16[528,512]{1,0:T(8,128)(2,1)S(1)} %shard_map.40), channel_id=1, source_target_pairs={{0,1},{1,0},{2,3},{3,2},{4,5},{5,4},{6,7},{7,6},{8,9},{9,8},{10,11... | collective-permute-start | bytes 1622024 | tf_op jit(solution)/shard_map/ppermute | solution.py:229
  29.8 6.3 %collective-permute-start.11 = (bf16[528,128]{1,0:T(8,128)(2,1)S(1)}, bf16[528,128]{1,0:T(8,128)(2,1)S(1)}, u32[]{:S(2)}, u32[]{:S(2)}) collective-permute-start(bf16[528,128]{1,0:T(8,128)(2,1)S(1)} %collective-permute-done.10.refs_4_), channel_id=1, source_target_pairs={{0,6},{4,2},{8,0},{12,4},{14,8},{10,12},{6,14},{2,10},{1,7},{5,3},... | collective-permute-start | bytes 405512 | tf_op jit(solution)/shard_map/ppermute | solution.py:146
  30.5 6.1 %collective-permute-start.12 = (bf16[528,128]{1,0:T(8,128)(2,1)S(1)}, bf16[528,128]{1,0:T(8,128)(2,1)S(1)}, u32[]{:S(2)}, u32[]{:S(2)}) collective-permute-start(bf16[528,128]{1,0:T(8,128)(2,1)S(1)} %collective-permute-done.2.refs_3_), channel_id=1, source_target_pairs={{0,4},{4,8},{8,12},{12,14},{14,10},{10,6},{6,2},{2,0},{1,5},{5,9},... | collective-permute-start | bytes 405512 | tf_op jit(solution)/shard_map/ppermute | solution.py:149
  30.5 6.9 %collective-permute-start.13 = (bf16[528,128]{1,0:T(8,128)(2,1)S(1)}, bf16[528,128]{1,0:T(8,128)(2,1)S(1)}, u32[]{:S(2)}, u32[]{:S(2)}) collective-permute-start(bf16[528,128]{1,0:T(8,128)(2,1)S(1)} %collective-permute-done.10.refs_4_), channel_id=1, source_target_pairs={{0,2},{4,0},{8,4},{12,8},{14,12},{10,14},{6,10},{2,6},{1,3},{5,1},... | collective-permute-start | bytes 405512 | tf_op jit(solution)/shard_map/ppermute | solution.py:150
  42.1 1.2 %collective-permute-start.16 = (f32[1,512]{1,0:T(1,128)S(1)}, f32[1,512]{1,0:T(1,128)S(1)}, u32[]{:S(2)}, u32[]{:S(2)}) collective-permute-start(f32[1,512]{1,0:T(1,128)S(1)} %get-tuple-element.36), channel_id=1, source_target_pairs={{0,16},{16,0},{1,17},{17,1},{2,18},{18,2},{3,19},{19,3},{4,20},{20... | collective-permute-start | bytes 6152 | tf_op jit(solution)/shard_map/ppermute | solution.py:241
  43.4 3.6 %collective-permute-start.17 = (f32[1,512]{1,0:T(1,128)S(1)}, f32[1,512]{1,0:T(1,128)S(1)}, u32[]{:S(2)}, u32[]{:S(2)}) collective-permute-start(f32[1,512]{1,0:T(1,128)S(1)} %add.12), channel_id=1, source_target_pairs={{0,1},{1,0},{2,3},{3,2},{4,5},{5,4},{6,7},{7,6},{8,9},{9,8},{10,11... | collective-permute-start | bytes 6152 | tf_op jit(solution)/shard_map/ppermute | solution.py:242

commit v4 on v3

--- a/solution.py
+++ b/solution.py
@@ -12,7 +12,8 @@
 LOG2E = 1.4426950408889634
 ID_ROWS = 16
 VMEM_BYTES = 24 * 1024 * 1024
-PLAN = ("S1", "K1", "S=W", "S2", "K2", "J", "S=W", "Sf2", "S3", "S=K", "Kf2", "K3")
+PACK_LIMIT = 24 << 20
+PLAN = ("S=K=T", "O", "S1", "K1", "S=W", "S2", "K2", "J", "S=W", "Sf2", "S3", "S=K", "C", "X", "Kf2", "K3")
 PLACE_LIMIT = 24 << 20
 
 
@@ -132,44 +133,6 @@
     vmem = pl.BlockSpec(memory_space=pltpu.VMEM)
     anywhere = pl.BlockSpec(memory_space=pl.ANY)
 
-    def gather_two(send, keep, window, join):
-        streams = {"S": [send[2]], "K": [keep[2]]}
-        ends = {"S": send[:2], "K": keep[:2]}
-
-        def move(name):
-            kind = name[0]
-            items = streams[kind]
-            if name[1] == "f":
-                hops = int(name[2])
-                front, rear = ends[kind]
-                src = front if kind == "S" else rear
-                items.append(lax.ppermute(src, "col", shift(hops if kind == "S" else -hops)))
-                return
-            front, rear = ends[kind]
-            front = lax.ppermute(front, "col", shift(1))
-            rear = lax.ppermute(rear, "col", shift(-1))
-            items.extend((front, rear))
-            ends[kind] = (front, rear)
-
-        def tie(*names):
-            nonlocal window
-            values = lax.optimization_barrier(tuple(window if n == "W" else (ends[n], streams[n][-1]) for n in names))
-            for n, v in zip(names, values):
-                if n == "W":
-                    window = v
-                else:
-                    ends[n] = v[0]
-                    streams[n][-1] = v[1]
-
-        for name in PLAN:
-            if name == "J":
-                window = join(window)
-            elif "=" in name:
-                tie(*name.split("="))
-            else:
-                move(name)
-        return streams["S"], streams["K"], window
-
     def gather_all(item):
         stacked = lax.all_gather(item, "col", axis=0)
         return [stacked[i] for i in range(size)]
@@ -180,7 +143,6 @@
         rows = count * block
         own = window_flow[0]
         half, columns = own.shape
-        other = lax.ppermute(own, "row", swap)
         item = jax.ShapeDtypeStruct((rows + ID_ROWS, block), flow_vals.dtype)
         params = pltpu.CompilerParams(vmem_limit_bytes=VMEM_BYTES)
         items = pl.pallas_call(
@@ -189,8 +151,9 @@
             in_specs=[vmem, anywhere],
             out_specs=(vmem,) * 2,
             scratch_shapes=[pltpu.SemaphoreType.DMA((2,))],
-            compiler_params=params,
+            compiler_params=pltpu.CompilerParams(vmem_limit_bytes=PACK_LIMIT),
         )(flow_cols.reshape(1, 2 * count), flow_vals.reshape(2 * rows, block))
+        theirs = own
         send, keep = items[:1] * 3, items[1:] * 3
 
         def place(mine, part, window=None):
@@ -206,27 +169,70 @@
                 cost_estimate=pl.CostEstimate(flops=0, bytes_accessed=2 * half * columns * 2, transcendentals=0),
             )(part, *given)
 
-        window = place(True, own)
-        if size == 8:
-            sends, keeps, window = gather_two(send, keep, window, lambda w: place(False, other, w))
-        else:
-            sends, keeps = gather_all(send[0]), gather_all(keep[0])
-            window = place(False, other, window)
         scratch = [
             pltpu.VMEM((max(size, 8), block), jnp.int32),
             pltpu.SMEM((max(size, 8), block), jnp.int32),
         ]
         sems = [pltpu.SemaphoreType.DMA(())]
         item_specs = [vmem] * size
-        code = pl.pallas_call(
-            functools.partial(send_kernel, size),
-            out_shape=jax.ShapeDtypeStruct((rows + ID_ROWS, columns), jnp.bfloat16),
-            in_specs=item_specs + [vmem],
-            out_specs=vmem,
-            scratch_shapes=scratch + [pltpu.VMEM((rows, columns), jnp.float32)] + sems,
-            compiler_params=params,
-        )(*sends, window)
-        code = lax.ppermute(code, "layer", swap)
+
+        def coded(sends, window):
+            return pl.pallas_call(
+                functools.partial(send_kernel, size),
+                out_shape=jax.ShapeDtypeStruct((rows + ID_ROWS, columns), jnp.bfloat16),
+                in_specs=item_specs + [vmem],
+                out_specs=vmem,
+                scratch_shapes=scratch + [pltpu.VMEM((rows, columns), jnp.float32)] + sems,
+                compiler_params=params,
+            )(*sends, window)
+
+        window = place(True, own)
+        if size == 8:
+            ends = {"S": (send[0], send[0]), "K": (keep[0], keep[0])}
+            lists = {"S": [send[0]], "K": [keep[0]]}
+            code = other = None
+
+            def tie(names):
+                nonlocal window, code, theirs, other
+                given = {"W": window, "C": code, "T": theirs, "O": other}
+                for n in "SK":
+                    given[n] = (ends[n], lists[n][-1])
+                done = lax.optimization_barrier(tuple(given[n] for n in names))
+                for n, value in zip(names, done):
+                    if n == "W":
+                        window = value
+                    elif n == "C":
+                        code = value
+                    elif n == "T":
+                        theirs = value
+                    elif n == "O":
+                        other = value
+                    else:
+                        ends[n], lists[n][-1] = value
+
+            for name in PLAN:
+                if name == "O":
+                    other = lax.ppermute(theirs, "row", swap)
+                elif name == "J":
+                    window = place(False, other, window)
+                elif name == "C":
+                    code = coded(lists["S"], window)
+                elif name == "X":
+                    code = lax.ppermute(code, "layer", swap)
+                elif "=" in name:
+                    tie(name.split("="))
+                elif name[1] == "f":
+                    kind, way = (name[0], 2 if name[0] == "S" else -2)
+                    lists[kind].append(lax.ppermute(ends[kind][0 if way > 0 else 1], "col", shift(way)))
+                else:
+                    kind = name[0]
+                    ends[kind] = tuple(lax.ppermute(e, "col", shift(w)) for e, w in zip(ends[kind], (1, -1)))
+                    lists[kind].extend(ends[kind])
+            keeps = lists["K"]
+        else:
+            sends, keeps = gather_all(send[0]), gather_all(keep[0])
+            window = place(False, lax.ppermute(own, "row", swap), window)
+            code = lax.ppermute(coded(sends, window), "layer", swap)
         square, sums = pl.pallas_call(
             functools.partial(keep_kernel, size),
             out_shape=(

time: 48.2 us -> 47 us (0.975)
  the two profiles are of different devices: /device:TPU:4 before, /device:TPU:0 now
where the time goes in v4:
time: 47 us; the launch traced here: 46.9 us
  starting transfers between devices  21.2 us (45%)
  waiting for transfers between devices  16.5 us (35%)
  Pallas kernels  4.22 us (9%)
  local copies, waits for them, and re-layouts  3.79 us (8%)
  other arithmetic  1.12 us (2%)
    ppermute x12, starting transfers between devices, body(): lax.ppermute(e, 'col', shift(w))  13.7 us
    ppermute x12, waiting for transfers between devices, body(): lax.ppermute(e, 'col', shift(w))  10.1 us
    ppermute x2, starting transfers between devices, body(): lax.ppermute(ends[kind][0 if way > 0 else 1], 'col', shift(way))  3.98 us
    unnamed x6, local copies, waits for them, and re-layouts  3.79 us
    ppermute x2, waiting for transfers between devices, body(): lax.ppermute(ends[kind][0 if way > 0 else 1], 'col', shift(way))  3.13 us
    ppermute x1, waiting for transfers between devices, body(): sums = sums + lax.ppermute(sums, 'layer', swap)  2.05 us
    pallas_call x1, Pallas kernels, coded(): pl.pallas_call(functools.partial(send_kernel, size), out_shape=jax.ShapeD...  1.73 us
    pallas_call x1, Pallas kernels, body(): pl.pallas_call(functools.partial(keep_kernel, size), out_shape=(jax.Shape...  1.59 us
  transfers between devices with their start and end apart: 18, of which 11 were waited for; matrix products, arithmetic and copies ran while one was open for 0% of the time, Pallas kernels for 1%

profile of v4, /device:TPU:0, one launch (start us, length us, event | category | flops | bytes accessed | tf_op | source)
XLA Modules:
  0.0 46.9 jit_solution(8034128119730635258)
XLA Ops:
  0.0 0.9 %copy-done.1 = bf16[8,1,1,128,128]{4,3,2,1,0:T(8,128)(2,1)S(1)} copy-done((bf16[8,1,1,128,128]{4,3,2,1,0:T(8,128)(2,1)S(1)}, bf16[8,1,1,128,128]{4,3,2,1,0:T(8,128)(2,1)}, u32[]{:S(2)}) %copy-start.1) | copy-done | bytes 262168
  2.5 2.6 %collective-permute-start.3 = (bf16[528,128]{1,0:T(8,128)(2,1)S(1)}, bf16[528,128]{1,0:T(8,128)(2,1)S(1)}, u32[]{:S(2)}, u32[]{:S(2)}) collective-permute-start(bf16[528,128]{1,0:T(8,128)(2,1)S(1)} %get-tuple-element.45.refs_0_), channel_id=1, source_target_pairs={{0,4},{4,8},{8,12},{12,14},{14,10},{10,6},{6,2},{2,0},{1,5},{5,9},... | collective-permute-start | bytes 405512 | tf_op jit(solution)/shard_map/ppermute | solution.py:229
  5.1 2.0 %collective-permute-start = (bf16[528,128]{1,0:T(8,128)(2,1)S(1)}, bf16[528,128]{1,0:T(8,128)(2,1)S(1)}, u32[]{:S(2)}, u32[]{:S(2)}) collective-permute-start(bf16[528,128]{1,0:T(8,128)(2,1)S(1)} %get-tuple-element.32.refs_0_), channel_id=1, source_target_pairs={{0,4},{4,8},{8,12},{12,14},{14,10},{10,6},{6,2},{2,0},{1,5},{5,9},... | collective-permute-start | bytes 405512 | tf_op jit(solution)/shard_map/ppermute | solution.py:229
  7.2 2.2 %copy-done = bf16[1,4096,512]{2,1,0:T(8,128)(2,1)S(1)} copy-done((bf16[1,4096,512]{2,1,0:T(8,128)(2,1)S(1)}, bf16[1,4096,512]{2,1,0:T(8,128)(2,1)}, u32[]{:S(2)}) %copy-start) | copy-done | bytes 4194328
  9.7 1.9 %collective-permute-done.4.refs_2_ = bf16[528,128]{1,0:T(8,128)(2,1)S(1)} collective-permute-done((bf16[528,128]{1,0:T(8,128)(2,1)S(1)}, bf16[528,128]{1,0:T(8,128)(2,1)S(1)}, u32[]{:S(2)}, u32[]{:S(2)}) %collective-permute-start.4) | collective-permute-done | bytes 135200 | tf_op jit(solution)/shard_map/ppermute | solution.py:229
  11.5 1.6 %collective-permute-start.5 = (bf16[528,128]{1,0:T(8,128)(2,1)S(1)}, bf16[528,128]{1,0:T(8,128)(2,1)S(1)}, u32[]{:S(2)}, u32[]{:S(2)}) collective-permute-start(bf16[528,128]{1,0:T(8,128)(2,1)S(1)} %collective-permute-done.3.refs_1_), channel_id=1, source_target_pairs={{0,4},{4,8},{8,12},{12,14},{14,10},{10,6},{6,2},{2,0},{1,5},{5,9},... | collective-permute-start | bytes 405512 | tf_op jit(solution)/shard_map/ppermute | solution.py:229
  13.6 1.6 %collective-permute-start.2 = (bf16[528,128]{1,0:T(8,128)(2,1)S(1)}, bf16[528,128]{1,0:T(8,128)(2,1)S(1)}, u32[]{:S(2)}, u32[]{:S(2)}) collective-permute-start(bf16[528,128]{1,0:T(8,128)(2,1)S(1)} %collective-permute-done.refs_1_), channel_id=1, source_target_pairs={{0,4},{4,8},{8,12},{12,14},{14,10},{10,6},{6,2},{2,0},{1,5},{5,9},... | collective-permute-start | bytes 405512 | tf_op jit(solution)/shard_map/ppermute | solution.py:229
  15.9 1.6 %collective-permute-done.5.refs_3_ = bf16[528,128]{1,0:T(8,128)(2,1)S(1)} collective-permute-done((bf16[528,128]{1,0:T(8,128)(2,1)S(1)}, bf16[528,128]{1,0:T(8,128)(2,1)S(1)}, u32[]{:S(2)}, u32[]{:S(2)}) %collective-permute-start.5) | collective-permute-done | bytes 135200 | tf_op jit(solution)/shard_map/ppermute | solution.py:229
  17.5 1.3 %collective-permute-done.6.refs_4_ = bf16[528,128]{1,0:T(8,128)(2,1)S(1)} collective-permute-done((bf16[528,128]{1,0:T(8,128)(2,1)S(1)}, bf16[528,128]{1,0:T(8,128)(2,1)S(1)}, u32[]{:S(2)}, u32[]{:S(2)}) %collective-permute-start.6) | collective-permute-done | bytes 135200 | tf_op jit(solution)/shard_map/ppermute | solution.py:229
  18.8 1.6 %collective-permute-start.8 = (bf16[528,128]{1,0:T(8,128)(2,1)S(1)}, bf16[528,128]{1,0:T(8,128)(2,1)S(1)}, u32[]{:S(2)}, u32[]{:S(2)}) collective-permute-start(bf16[528,128]{1,0:T(8,128)(2,1)S(1)} %collective-permute-done.5.refs_3_), channel_id=1, source_target_pairs={{0,4},{4,8},{8,12},{12,14},{14,10},{10,6},{6,2},{2,0},{1,5},{5,9},... | collective-permute-start | bytes 405512 | tf_op jit(solution)/shard_map/ppermute | solution.py:229
  20.8 2.6 %collective-permute-start.14 = (bf16[528,128]{1,0:T(8,128)(2,1)S(1)}, bf16[528,128]{1,0:T(8,128)(2,1)S(1)}, u32[]{:S(2)}, u32[]{:S(2)}) collective-permute-start(bf16[528,128]{1,0:T(8,128)(2,1)S(1)} %collective-permute-done.5.refs_3_), channel_id=1, source_target_pairs={{0,8},{4,12},{8,14},{12,10},{14,6},{10,2},{6,0},{2,4},{1,9},{5,13}... | collective-permute-start | bytes 405512 | tf_op jit(solution)/shard_map/ppermute | solution.py:226
  24.0 1.4 %collective-permute-done.9.refs_7_ = bf16[528,128]{1,0:T(8,128)(2,1)S(1)} collective-permute-done((bf16[528,128]{1,0:T(8,128)(2,1)S(1)}, bf16[528,128]{1,0:T(8,128)(2,1)S(1)}, u32[]{:S(2)}, u32[]{:S(2)}) %collective-permute-start.9) | collective-permute-done | bytes 135200 | tf_op jit(solution)/shard_map/ppermute | solution.py:229
  25.4 1.5 %collective-permute-done.14.refs_5_ = bf16[528,128]{1,0:T(8,128)(2,1)S(1)} collective-permute-done((bf16[528,128]{1,0:T(8,128)(2,1)S(1)}, bf16[528,128]{1,0:T(8,128)(2,1)S(1)}, u32[]{:S(2)}, u32[]{:S(2)}) %collective-permute-start.14) | collective-permute-done | bytes 135200 | tf_op jit(solution)/shard_map/ppermute | solution.py:226
  26.9 1.7 %shard_map.40 = bf16[528,512]{1,0:T(8,128)(2,1)S(1)} custom-call(bf16[528,128]{1,0:T(8,128)(2,1)S(1)} %get-tuple-element.45.refs_0_, bf16[528,128]{1,0:T(8,128)(2,1)S(1)} %collective-permute-done.3.refs_1_, bf16[528,128]{1,0:T(8,128)(2,1)S(1)} %collective-permute-done.4.refs_2_, bf16[528,128]{1,0:T(8,128)(2,1)S(1)} %collective-permute-done.5.refs_3_, ...), custom_call_target="tpu_custom_call" | custom-call | tf_op jit(solution)/shard_map/pallas_call | solution.py:180
  28.6 1.4 %collective-permute-start.15 = (bf16[528,512]{1,0:T(8,128)(2,1)S(1)}, bf16[528,512]{1,0:T(8,128)(2,1)S(1)}, u32[]{:S(2)}, u32[]{:S(2)}) collective-permute-start(bf16[528,512]{1,0:T(8,128)(2,1)S(1)} %shard_map.40), channel_id=1, source_target_pairs={{0,1},{1,0},{2,3},{3,2},{4,5},{5,4},{6,7},{7,6},{8,9},{9,8},{10,11... | collective-permute-start | bytes 1622024 | tf_op jit(solution)/shard_map/ppermute | solution.py:221
  30.0 1.4 %collective-permute-start.11 = (bf16[528,128]{1,0:T(8,128)(2,1)S(1)}, bf16[528,128]{1,0:T(8,128)(2,1)S(1)}, u32[]{:S(2)}, u32[]{:S(2)}) collective-permute-start(bf16[528,128]{1,0:T(8,128)(2,1)S(1)} %collective-permute-done.10.refs_4_), channel_id=1, source_target_pairs={{0,6},{4,2},{8,0},{12,4},{14,8},{10,12},{6,14},{2,10},{1,7},{5,3},... | collective-permute-start | bytes 405512 | tf_op jit(solution)/shard_map/ppermute | solution.py:226
  31.4 2.9 %collective-permute-start.12 = (bf16[528,128]{1,0:T(8,128)(2,1)S(1)}, bf16[528,128]{1,0:T(8,128)(2,1)S(1)}, u32[]{:S(2)}, u32[]{:S(2)}) collective-permute-start(bf16[528,128]{1,0:T(8,128)(2,1)S(1)} %collective-permute-done.2.refs_3_), channel_id=1, source_target_pairs={{0,4},{4,8},{8,12},{12,14},{14,10},{10,6},{6,2},{2,0},{1,5},{5,9},... | collective-permute-start | bytes 405512 | tf_op jit(solution)/shard_map/ppermute | solution.py:229
  34.3 1.6 %collective-permute-done.11.refs_5_ = bf16[528,128]{1,0:T(8,128)(2,1)S(1)} collective-permute-done((bf16[528,128]{1,0:T(8,128)(2,1)S(1)}, bf16[528,128]{1,0:T(8,128)(2,1)S(1)}, u32[]{:S(2)}, u32[]{:S(2)}) %collective-permute-start.11) | collective-permute-done | bytes 135200 | tf_op jit(solution)/shard_map/ppermute | solution.py:226
  36.9 2.5 %collective-permute-done.13.refs_7_ = bf16[528,128]{1,0:T(8,128)(2,1)S(1)} collective-permute-done((bf16[528,128]{1,0:T(8,128)(2,1)S(1)}, bf16[528,128]{1,0:T(8,128)(2,1)S(1)}, u32[]{:S(2)}, u32[]{:S(2)}) %collective-permute-start.13) | collective-permute-done | bytes 135200 | tf_op jit(solution)/shard_map/ppermute | solution.py:229
  39.3 1.6 %shard_map.41 = (f32[512,512]{1,0:T(8,128)S(1)}, f32[1,512]{1,0:T(1,128)S(1)}) custom-call(bf16[528,128]{1,0:T(8,128)(2,1)S(1)} %get-tuple-element.32.refs_0_, bf16[528,128]{1,0:T(8,128)(2,1)S(1)} %collective-permute-done.refs_1_, bf16[528,128]{1,0:T(8,128)(2,1)S(1)} %collective-permute-done.1.refs_2_, bf16[528,128]{1,0:T(8,128)(2,1)S(1)} %collective-permute-done.2.refs_3_, ...), custom_call_target="tpu_custom_call" | custom-call | tf_op jit(solution)/shard_map/pallas_call | solution.py:236
  41.0 1.1 %collective-permute-done.16 = f32[1,512]{1,0:T(1,128)S(1)} collective-permute-done((f32[1,512]{1,0:T(1,128)S(1)}, f32[1,512]{1,0:T(1,128)S(1)}, u32[]{:S(2)}, u32[]{:S(2)}) %collective-permute-start.16) | collective-permute-done | bytes 2080 | tf_op jit(solution)/shard_map/ppermute | solution.py:247
  42.2 1.5 %collective-permute-start.17 = (f32[1,512]{1,0:T(1,128)S(1)}, f32[1,512]{1,0:T(1,128)S(1)}, u32[]{:S(2)}, u32[]{:S(2)}) collective-permute-start(f32[1,512]{1,0:T(1,128)S(1)} %add.12), channel_id=1, source_target_pairs={{0,1},{1,0},{2,3},{3,2},{4,5},{5,4},{6,7},{7,6},{8,9},{9,8},{10,11... | collective-permute-start | bytes 6152 | tf_op jit(solution)/shard_map/ppermute | solution.py:248
  43.7 2.1 %collective-permute-done.17 = f32[1,512]{1,0:T(1,128)S(1)} collective-permute-done((f32[1,512]{1,0:T(1,128)S(1)}, f32[1,512]{1,0:T(1,128)S(1)}, u32[]{:S(2)}, u32[]{:S(2)}) %collective-permute-start.17) | collective-permute-done | bytes 2080 | tf_op jit(solution)/shard_map/ppermute | solution.py:248
  45.8 1.1 %broadcast_multiply_fusion = f32[512,512]{1,0:T(8,128)} fusion(f32[512,512]{1,0:T(8,128)S(1)} %get-tuple-element.49, f32[512]{0:T(512)S(1)} %bitcast.8), kind=kLoop, calls=%fused_computation | loop fusion | flops 262144 | bytes 2099200 | tf_op jit(solution)/shard_map/mul | solution.py:250
  (26 shorter events, 5.1 us)
Async XLA Ops:
  0.0 0.9 %copy-start.1 = (bf16[8,1,1,128,128]{4,3,2,1,0:T(8,128)(2,1)S(1)}, bf16[8,1,1,128,128]{4,3,2,1,0:T(8,128)(2,1)}, u32[]{:S(2)}) copy-start(bf16[8,1,1,128,128]{4,3,2,1,0:T(8,128)(2,1)} %param.4) | copy-start | bytes 786436
  1.0 0.7 %copy-start.2 = (s32[8,1,1]{0,2,1:T(1,128)S(1)}, s32[8,1,1]{0,2,1:T(1,128)}, u32[]{:S(2)}) copy-start(s32[8,1,1]{0,2,1:T(1,128)} %param.3) | copy-start | bytes 100
  1.9 13.7 %collective-permute-start.7 = (bf16[4096,512]{1,0:T(8,128)(2,1)}, bf16[4096,512]{1,0:T(8,128)(2,1)S(1)}, u32[]{:S(2)}, u32[]{:S(2)}) collective-permute-start(bf16[4096,512]{1,0:T(8,128)(2,1)} %bitcast.4), channel_id=1, source_target_pairs={{0,16},{16,0},{1,17},{17,1},{2,18},{18,2},{3,19},{19,3},{4,20},{20... | collective-permute-start | bytes 12582920 | tf_op jit(solution)/shard_map/ppermute | solution.py:215
  2.5 7.2 %collective-permute-start.3 = (bf16[528,128]{1,0:T(8,128)(2,1)S(1)}, bf16[528,128]{1,0:T(8,128)(2,1)S(1)}, u32[]{:S(2)}, u32[]{:S(2)}) collective-permute-start(bf16[528,128]{1,0:T(8,128)(2,1)S(1)} %get-tuple-element.45.refs_0_), channel_id=1, source_target_pairs={{0,4},{4,8},{8,12},{12,14},{14,10},{10,6},{6,2},{2,0},{1,5},{5,9},... | collective-permute-start | bytes 405512 | tf_op jit(solution)/shard_map/ppermute | solution.py:229
  5.1 6.4 %collective-permute-start.4 = (bf16[528,128]{1,0:T(8,128)(2,1)S(1)}, bf16[528,128]{1,0:T(8,128)(2,1)S(1)}, u32[]{:S(2)}, u32[]{:S(2)}) collective-permute-start(bf16[528,128]{1,0:T(8,128)(2,1)S(1)} %get-tuple-element.45.refs_0_), channel_id=1, source_target_pairs={{0,2},{4,0},{8,4},{12,8},{14,12},{10,14},{6,10},{2,6},{1,3},{5,1},... | collective-permute-start | bytes 405512 | tf_op jit(solution)/shard_map/ppermute | solution.py:229
  5.1 8.4 %collective-permute-start = (bf16[528,128]{1,0:T(8,128)(2,1)S(1)}, bf16[528,128]{1,0:T(8,128)(2,1)S(1)}, u32[]{:S(2)}, u32[]{:S(2)}) collective-permute-start(bf16[528,128]{1,0:T(8,128)(2,1)S(1)} %get-tuple-element.32.refs_0_), channel_id=1, source_target_pairs={{0,4},{4,8},{8,12},{12,14},{14,10},{10,6},{6,2},{2,0},{1,5},{5,9},... | collective-permute-start | bytes 405512 | tf_op jit(solution)/shard_map/ppermute | solution.py:229
  7.1 8.0 %collective-permute-start.1 = (bf16[528,128]{1,0:T(8,128)(2,1)S(1)}, bf16[528,128]{1,0:T(8,128)(2,1)S(1)}, u32[]{:S(2)}, u32[]{:S(2)}) collective-permute-start(bf16[528,128]{1,0:T(8,128)(2,1)S(1)} %get-tuple-element.32.refs_0_), channel_id=1, source_target_pairs={{0,2},{4,0},{8,4},{12,8},{14,12},{10,14},{6,10},{2,6},{1,3},{5,1},... | collective-permute-start | bytes 405512 | tf_op jit(solution)/shard_map/ppermute | solution.py:229
  7.2 2.2 %copy-start = (bf16[1,4096,512]{2,1,0:T(8,128)(2,1)S(1)}, bf16[1,4096,512]{2,1,0:T(8,128)(2,1)}, u32[]{:S(2)}) copy-start(bf16[1,4096,512]{2,1,0:T(8,128)(2,1)} %param.5) | copy-start | bytes 12582916
  11.5 6.0 %collective-permute-start.5 = (bf16[528,128]{1,0:T(8,128)(2,1)S(1)}, bf16[528,128]{1,0:T(8,128)(2,1)S(1)}, u32[]{:S(2)}, u32[]{:S(2)}) collective-permute-start(bf16[528,128]{1,0:T(8,128)(2,1)S(1)} %collective-permute-done.3.refs_1_), channel_id=1, source_target_pairs={{0,4},{4,8},{8,12},{12,14},{14,10},{10,6},{6,2},{2,0},{1,5},{5,9},... | collective-permute-start | bytes 405512 | tf_op jit(solution)/shard_map/ppermute | solution.py:229
  13.1 5.7 %collective-permute-start.6 = (bf16[528,128]{1,0:T(8,128)(2,1)S(1)}, bf16[528,128]{1,0:T(8,128)(2,1)S(1)}, u32[]{:S(2)}, u32[]{:S(2)}) collective-permute-start(bf16[528,128]{1,0:T(8,128)(2,1)S(1)} %collective-permute-done.4.refs_2_), channel_id=1, source_target_pairs={{0,2},{4,0},{8,4},{12,8},{14,12},{10,14},{6,10},{2,6},{1,3},{5,1},... | collective-permute-start | bytes 405512 | tf_op jit(solution)/shard_map/ppermute | solution.py:229
  13.6 9.8 %collective-permute-start.2 = (bf16[528,128]{1,0:T(8,128)(2,1)S(1)}, bf16[528,128]{1,0:T(8,128)(2,1)S(1)}, u32[]{:S(2)}, u32[]{:S(2)}) collective-permute-start(bf16[528,128]{1,0:T(8,128)(2,1)S(1)} %collective-permute-done.refs_1_), channel_id=1, source_target_pairs={{0,4},{4,8},{8,12},{12,14},{14,10},{10,6},{6,2},{2,0},{1,5},{5,9},... | collective-permute-start | bytes 405512 | tf_op jit(solution)/shard_map/ppermute | solution.py:229
  15.1 8.3 %collective-permute-start.10 = (bf16[528,128]{1,0:T(8,128)(2,1)S(1)}, bf16[528,128]{1,0:T(8,128)(2,1)S(1)}, u32[]{:S(2)}, u32[]{:S(2)}) collective-permute-start(bf16[528,128]{1,0:T(8,128)(2,1)S(1)} %collective-permute-done.1.refs_2_), channel_id=1, source_target_pairs={{0,2},{4,0},{8,4},{12,8},{14,12},{10,14},{6,10},{2,6},{1,3},{5,1},... | collective-permute-start | bytes 405512 | tf_op jit(solution)/shard_map/ppermute | solution.py:229
  18.8 5.2 %collective-permute-start.8 = (bf16[528,128]{1,0:T(8,128)(2,1)S(1)}, bf16[528,128]{1,0:T(8,128)(2,1)S(1)}, u32[]{:S(2)}, u32[]{:S(2)}) collective-permute-start(bf16[528,128]{1,0:T(8,128)(2,1)S(1)} %collective-permute-done.5.refs_3_), channel_id=1, source_target_pairs={{0,4},{4,8},{8,12},{12,14},{14,10},{10,6},{6,2},{2,0},{1,5},{5,9},... | collective-permute-start | bytes 405512 | tf_op jit(solution)/shard_map/ppermute | solution.py:229
  20.4 5.0 %collective-permute-start.9 = (bf16[528,128]{1,0:T(8,128)(2,1)S(1)}, bf16[528,128]{1,0:T(8,128)(2,1)S(1)}, u32[]{:S(2)}, u32[]{:S(2)}) collective-permute-start(bf16[528,128]{1,0:T(8,128)(2,1)S(1)} %collective-permute-done.6.refs_4_), channel_id=1, source_target_pairs={{0,2},{4,0},{8,4},{12,8},{14,12},{10,14},{6,10},{2,6},{1,3},{5,1},... | collective-permute-start | bytes 405512 | tf_op jit(solution)/shard_map/ppermute | solution.py:229
  20.8 6.1 %collective-permute-start.14 = (bf16[528,128]{1,0:T(8,128)(2,1)S(1)}, bf16[528,128]{1,0:T(8,128)(2,1)S(1)}, u32[]{:S(2)}, u32[]{:S(2)}) collective-permute-start(bf16[528,128]{1,0:T(8,128)(2,1)S(1)} %collective-permute-done.5.refs_3_), channel_id=1, source_target_pairs={{0,8},{4,12},{8,14},{12,10},{14,6},{10,2},{6,0},{2,4},{1,9},{5,13}... | collective-permute-start | bytes 405512 | tf_op jit(solution)/shard_map/ppermute | solution.py:226
  28.6 10.7 %collective-permute-start.15 = (bf16[528,512]{1,0:T(8,128)(2,1)S(1)}, bf16[528,512]{1,0:T(8,128)(2,1)S(1)}, u32[]{:S(2)}, u32[]{:S(2)}) collective-permute-start(bf16[528,512]{1,0:T(8,128)(2,1)S(1)} %shard_map.40), channel_id=1, source_target_pairs={{0,1},{1,0},{2,3},{3,2},{4,5},{5,4},{6,7},{7,6},{8,9},{9,8},{10,11... | collective-permute-start | bytes 1622024 | tf_op jit(solution)/shard_map/ppermute | solution.py:221
  30.0 5.9 %collective-permute-start.11 = (bf16[528,128]{1,0:T(8,128)(2,1)S(1)}, bf16[528,128]{1,0:T(8,128)(2,1)S(1)}, u32[]{:S(2)}, u32[]{:S(2)}) collective-permute-start(bf16[528,128]{1,0:T(8,128)(2,1)S(1)} %collective-permute-done.10.refs_4_), channel_id=1, source_target_pairs={{0,6},{4,2},{8,0},{12,4},{14,8},{10,12},{6,14},{2,10},{1,7},{5,3},... | collective-permute-start | bytes 405512 | tf_op jit(solution)/shard_map/ppermute | solution.py:226
  31.4 5.5 %collective-permute-start.12 = (bf16[528,128]{1,0:T(8,128)(2,1)S(1)}, bf16[528,128]{1,0:T(8,128)(2,1)S(1)}, u32[]{:S(2)}, u32[]{:S(2)}) collective-permute-start(bf16[528,128]{1,0:T(8,128)(2,1)S(1)} %collective-permute-done.2.refs_3_), channel_id=1, source_target_pairs={{0,4},{4,8},{8,12},{12,14},{14,10},{10,6},{6,2},{2,0},{1,5},{5,9},... | collective-permute-start | bytes 405512 | tf_op jit(solution)/shard_map/ppermute | solution.py:229
  34.3 5.0 %collective-permute-start.13 = (bf16[528,128]{1,0:T(8,128)(2,1)S(1)}, bf16[528,128]{1,0:T(8,128)(2,1)S(1)}, u32[]{:S(2)}, u32[]{:S(2)}) collective-permute-start(bf16[528,128]{1,0:T(8,128)(2,1)S(1)} %collective-permute-done.10.refs_4_), channel_id=1, source_target_pairs={{0,2},{4,0},{8,4},{12,8},{14,12},{10,14},{6,10},{2,6},{1,3},{5,1},... | collective-permute-start | bytes 405512 | tf_op jit(solution)/shard_map/ppermute | solution.py:229
  40.9 1.2 %collective-permute-start.16 = (f32[1,512]{1,0:T(1,128)S(1)}, f32[1,512]{1,0:T(1,128)S(1)}, u32[]{:S(2)}, u32[]{:S(2)}) collective-permute-start(f32[1,512]{1,0:T(1,128)S(1)} %get-tuple-element.50), channel_id=1, source_target_pairs={{0,16},{16,0},{1,17},{17,1},{2,18},{18,2},{3,19},{19,3},{4,20},{20... | collective-permute-start | bytes 6152 | tf_op jit(solution)/shard_map/ppermute | solution.py:247
  42.2 3.6 %collective-permute-start.17 = (f32[1,512]{1,0:T(1,128)S(1)}, f32[1,512]{1,0:T(1,128)S(1)}, u32[]{:S(2)}, u32[]{:S(2)}) collective-permute-start(f32[1,512]{1,0:T(1,128)S(1)} %add.12), channel_id=1, source_target_pairs={{0,1},{1,0},{2,3},{3,2},{4,5},{5,4},{6,7},{7,6},{8,9},{9,8},{10,11... | collective-permute-start | bytes 6152 | tf_op jit(solution)/shard_map/ppermute | solution.py:248

commit v5 on v4

--- a/solution.py
+++ b/solution.py
@@ -33,11 +33,25 @@
             )
         )
         copies[-1].start()
-    line = cols_ref[...].astype(jnp.float32).astype(jnp.bfloat16)
+    line = jnp.pad(cols_ref[...], ((0, 0), (0, block - cols_ref.shape[1])))
+    line = jnp.broadcast_to(line, (ID_ROWS, block)).astype(jnp.float32).astype(jnp.bfloat16)
     for out in outs:
-        out[rows : rows + ID_ROWS, 0 : line.shape[1]] = jnp.broadcast_to(line, (ID_ROWS, line.shape[1]))
+        out[rows : rows + ID_ROWS, :] = line
     for copy in copies:
         copy.wait()
+
+
+def pick_kernel(first_ref, last_ref, out_ref):
+    col = lax.axis_index("col")
+    odd = lax.rem(col + lax.div(col, 2), 2)
+
+    @pl.when(odd == 0)
+    def _():
+        out_ref[...] = first_ref[...]
+
+    @pl.when(odd != 0)
+    def _():
+        out_ref[...] = last_ref[...]
 
 
 def place_kernel(mine, part_ref, *refs):
@@ -50,19 +64,16 @@
     copy.wait()
 
 
-def products(part, items, window, ids_v, ids_s, sem, finish):
+def products(part, items, window, finish):
     block = items[0].shape[1]
     rows = items[0].shape[0] - ID_ROWS
     live_end = window.shape[0] // block
-    for s, item in enumerate(items):
-        ids_v[pl.ds(s, 1)] = item[rows : rows + 1, :].astype(jnp.float32).astype(jnp.int32)
-    to_scalar = pltpu.make_async_copy(ids_v, ids_s, sem)
-    to_scalar.start()
-    to_scalar.wait()
+    lanes = lax.broadcasted_iota(jnp.int32, (1, block), 1)
+    lines = [item[rows : rows + 1, :].astype(jnp.float32).astype(jnp.int32) for item in items]
     for j in range(rows // block):
         left, right = [], []
         for s in range(len(items)):
-            col = ids_s[s, part * (rows // block) + j]
+            col = jnp.sum(jnp.where(lanes == part * (rows // block) + j, lines[s], 0))
             live = jnp.where(col < live_end, 1.0, 0.0).astype(jnp.float32)
             piece = items[s][j * block : (j + 1) * block, :]
             left.append((piece.astype(jnp.float32) * live).astype(jnp.bfloat16))
@@ -79,14 +90,14 @@
 
 
 def send_kernel(slots, *refs):
-    items, (window, code_ref, ids_v, ids_s, total, sem) = refs[:slots], refs[slots:]
+    items, (window, code_ref, total) = refs[:slots], refs[slots:]
     block = items[0].shape[1]
     rows = total.shape[0]
 
     def finish(j, value):
         total[j * block : (j + 1) * block, :] = value
 
-    products(1 - lax.axis_index("layer"), items, window, ids_v, ids_s, sem, finish)
+    products(1 - lax.axis_index("layer"), items, window, finish)
     most = jnp.max(jnp.abs(total[...]), axis=0, keepdims=True)
     scale = (most * 1.01 + 1e-30).astype(jnp.bfloat16)
     inverse = CODE_SPAN / scale.astype(jnp.float32)
@@ -98,7 +109,7 @@
 
 
 def keep_kernel(slots, *refs):
-    items, (window, code_ref, square_ref, sum_ref, ids_v, ids_s, sem) = refs[:slots], refs[slots:]
+    items, (window, code_ref, square_ref, sum_ref) = refs[:slots], refs[slots:]
     block = items[0].shape[1]
     rows = square_ref.shape[0]
     scale = code_ref[rows : rows + 1, :].astype(jnp.float32) * (1.0 / CODE_SPAN)
@@ -112,7 +123,7 @@
         square_ref[j * block : (j + 1) * block, :] = square
         sums.append(jnp.sum(square, axis=0, keepdims=True))
 
-    products(lax.axis_index("layer"), items, window, ids_v, ids_s, sem, finish)
+    products(lax.axis_index("layer"), items, window, finish)
     sum_ref[...] = functools.reduce(jnp.add, sums)
 
 
@@ -132,6 +143,8 @@
     swap = [(0, 1), (1, 0)]
     vmem = pl.BlockSpec(memory_space=pltpu.VMEM)
     anywhere = pl.BlockSpec(memory_space=pl.ANY)
+
+    across = [(order[a], order[b]) for a, b in ((6, 1), (5, 2), (2, 5), (1, 6), (3, 0), (0, 3), (7, 4), (4, 7))] if size == 8 else []
 
     def gather_all(item):
         stacked = lax.all_gather(item, "col", axis=0)
@@ -156,6 +169,11 @@
         theirs = own
         send, keep = items[:1] * 3, items[1:] * 3
 
+        def pick(first, last):
+            return pl.pallas_call(
+                pick_kernel, out_shape=item, in_specs=[vmem, vmem], out_specs=vmem, compiler_params=params
+            )(first, last)
+
         def place(mine, part, window=None):
             given = [] if window is None else [window]
             return pl.pallas_call(
@@ -169,11 +187,6 @@
                 cost_estimate=pl.CostEstimate(flops=0, bytes_accessed=2 * half * columns * 2, transcendentals=0),
             )(part, *given)
 
-        scratch = [
-            pltpu.VMEM((max(size, 8), block), jnp.int32),
-            pltpu.SMEM((max(size, 8), block), jnp.int32),
-        ]
-        sems = [pltpu.SemaphoreType.DMA(())]
         item_specs = [vmem] * size
 
         def coded(sends, window):
@@ -182,12 +195,13 @@
                 out_shape=jax.ShapeDtypeStruct((rows + ID_ROWS, columns), jnp.bfloat16),
                 in_specs=item_specs + [vmem],
                 out_specs=vmem,
-                scratch_shapes=scratch + [pltpu.VMEM((rows, columns), jnp.float32)] + sems,
+                scratch_shapes=[pltpu.VMEM((rows, columns), jnp.float32)],
                 compiler_params=params,
             )(*sends, window)
 
         window = place(True, own)
         if size == 8:
+            chosen = {}
             ends = {"S": (send[0], send[0]), "K": (keep[0], keep[0])}
             lists = {"S": [send[0]], "K": [keep[0]]}
             code = other = None
@@ -197,12 +211,15 @@
                 given = {"W": window, "C": code, "T": theirs, "O": other}
                 for n in "SK":
                     given[n] = (ends[n], lists[n][-1])
+                    given[n + "p"] = chosen.get(n)
                 done = lax.optimization_barrier(tuple(given[n] for n in names))
                 for n, value in zip(names, done):
                     if n == "W":
                         window = value
                     elif n == "C":
                         code = value
+                    elif n[-1] == "p":
+                        chosen[n[0]] = value
                     elif n == "T":
                         theirs = value
                     elif n == "O":
@@ -224,6 +241,10 @@
                 elif name[1] == "f":
                     kind, way = (name[0], 2 if name[0] == "S" else -2)
                     lists[kind].append(lax.ppermute(ends[kind][0 if way > 0 else 1], "col", shift(way)))
+                elif name[1] == "p":
+                    chosen[name[0]] = pick(*ends[name[0]])
+                elif name[1] == "m":
+                    lists[name[0]].append(lax.ppermute(chosen[name[0]], "col", across))
                 else:
                     kind = name[0]
                     ends[kind] = tuple(lax.ppermute(e, "col", shift(w)) for e, w in zip(ends[kind], (1, -1)))
@@ -241,7 +262,6 @@
             ),
             in_specs=item_specs + [vmem, vmem],
             out_specs=(vmem, vmem),
-            scratch_shapes=scratch + sems,
             compiler_params=params,
         )(*keeps, window, code)
         sums = sums + lax.ppermute(sums, "row", swap)

time: 47 us -> 46.2 us (0.983)
  Pallas kernels: 4.22 us -> 3.4 us
where the time goes in v5:
time: 46.2 us; the launch traced here: 46 us
  starting transfers between devices  21.2 us (46%)
  waiting for transfers between devices  16.5 us (36%)
  local copies, waits for them, and re-layouts  3.79 us (8%)
  Pallas kernels  3.4 us (7%)
  other arithmetic  1.12 us (2%)
    ppermute x12, starting transfers between devices, body(): lax.ppermute(e, 'col', shift(w))  13.7 us
    ppermute x12, waiting for transfers between devices, body(): lax.ppermute(e, 'col', shift(w))  10.1 us
    ppermute x2, starting transfers between devices, body(): lax.ppermute(ends[kind][0 if way > 0 else 1], 'col', shift(way))  3.98 us
    unnamed x6, local copies, waits for them, and re-layouts  3.79 us
    ppermute x2, waiting for transfers between devices, body(): lax.ppermute(ends[kind][0 if way > 0 else 1], 'col', shift(way))  3.13 us
    ppermute x1, waiting for transfers between devices, body(): sums = sums + lax.ppermute(sums, 'layer', swap)  2.06 us
    ppermute x1, starting transfers between devices, body(): sums = sums + lax.ppermute(sums, 'layer', swap)  1.52 us
    ppermute x1, starting transfers between devices, body(): code = lax.ppermute(code, 'layer', swap)  1.4 us
  transfers between devices with their start and end apart: 18, of which 11 were waited for; matrix products, arithmetic and copies ran while one was open for 0% of the time, Pallas kernels for 1%

profile of v5, /device:TPU:0, one launch (start us, length us, event | category | flops | bytes accessed | tf_op | source)
XLA Modules:
  0.0 46.0 jit_solution(7239367535004298339)
XLA Ops:
  0.0 0.9 %copy-done.1 = bf16[8,1,1,128,128]{4,3,2,1,0:T(8,128)(2,1)S(1)} copy-done((bf16[8,1,1,128,128]{4,3,2,1,0:T(8,128)(2,1)S(1)}, bf16[8,1,1,128,128]{4,3,2,1,0:T(8,128)(2,1)}, u32[]{:S(2)}) %copy-start.1) | copy-done | bytes 262168
  2.5 2.6 %collective-permute-start.3 = (bf16[528,128]{1,0:T(8,128)(2,1)S(1)}, bf16[528,128]{1,0:T(8,128)(2,1)S(1)}, u32[]{:S(2)}, u32[]{:S(2)}) collective-permute-start(bf16[528,128]{1,0:T(8,128)(2,1)S(1)} %get-tuple-element.45.refs_0_), channel_id=1, source_target_pairs={{0,4},{4,8},{8,12},{12,14},{14,10},{10,6},{6,2},{2,0},{1,5},{5,9},... | collective-permute-start | bytes 405512 | tf_op jit(solution)/shard_map/ppermute | solution.py:250
  5.1 2.0 %collective-permute-start = (bf16[528,128]{1,0:T(8,128)(2,1)S(1)}, bf16[528,128]{1,0:T(8,128)(2,1)S(1)}, u32[]{:S(2)}, u32[]{:S(2)}) collective-permute-start(bf16[528,128]{1,0:T(8,128)(2,1)S(1)} %get-tuple-element.32.refs_0_), channel_id=1, source_target_pairs={{0,4},{4,8},{8,12},{12,14},{14,10},{10,6},{6,2},{2,0},{1,5},{5,9},... | collective-permute-start | bytes 405512 | tf_op jit(solution)/shard_map/ppermute | solution.py:250
  7.2 2.2 %copy-done = bf16[1,4096,512]{2,1,0:T(8,128)(2,1)S(1)} copy-done((bf16[1,4096,512]{2,1,0:T(8,128)(2,1)S(1)}, bf16[1,4096,512]{2,1,0:T(8,128)(2,1)}, u32[]{:S(2)}) %copy-start) | copy-done | bytes 4194328
  9.7 1.9 %collective-permute-done.4.refs_2_ = bf16[528,128]{1,0:T(8,128)(2,1)S(1)} collective-permute-done((bf16[528,128]{1,0:T(8,128)(2,1)S(1)}, bf16[528,128]{1,0:T(8,128)(2,1)S(1)}, u32[]{:S(2)}, u32[]{:S(2)}) %collective-permute-start.4) | collective-permute-done | bytes 135200 | tf_op jit(solution)/shard_map/ppermute | solution.py:250
  11.5 1.6 %collective-permute-start.5 = (bf16[528,128]{1,0:T(8,128)(2,1)S(1)}, bf16[528,128]{1,0:T(8,128)(2,1)S(1)}, u32[]{:S(2)}, u32[]{:S(2)}) collective-permute-start(bf16[528,128]{1,0:T(8,128)(2,1)S(1)} %collective-permute-done.3.refs_1_), channel_id=1, source_target_pairs={{0,4},{4,8},{8,12},{12,14},{14,10},{10,6},{6,2},{2,0},{1,5},{5,9},... | collective-permute-start | bytes 405512 | tf_op jit(solution)/shard_map/ppermute | solution.py:250
  13.6 1.6 %collective-permute-start.2 = (bf16[528,128]{1,0:T(8,128)(2,1)S(1)}, bf16[528,128]{1,0:T(8,128)(2,1)S(1)}, u32[]{:S(2)}, u32[]{:S(2)}) collective-permute-start(bf16[528,128]{1,0:T(8,128)(2,1)S(1)} %collective-permute-done.refs_1_), channel_id=1, source_target_pairs={{0,4},{4,8},{8,12},{12,14},{14,10},{10,6},{6,2},{2,0},{1,5},{5,9},... | collective-permute-start | bytes 405512 | tf_op jit(solution)/shard_map/ppermute | solution.py:250
  15.9 1.6 %collective-permute-done.5.refs_3_ = bf16[528,128]{1,0:T(8,128)(2,1)S(1)} collective-permute-done((bf16[528,128]{1,0:T(8,128)(2,1)S(1)}, bf16[528,128]{1,0:T(8,128)(2,1)S(1)}, u32[]{:S(2)}, u32[]{:S(2)}) %collective-permute-start.5) | collective-permute-done | bytes 135200 | tf_op jit(solution)/shard_map/ppermute | solution.py:250
  17.5 1.3 %collective-permute-done.6.refs_4_ = bf16[528,128]{1,0:T(8,128)(2,1)S(1)} collective-permute-done((bf16[528,128]{1,0:T(8,128)(2,1)S(1)}, bf16[528,128]{1,0:T(8,128)(2,1)S(1)}, u32[]{:S(2)}, u32[]{:S(2)}) %collective-permute-start.6) | collective-permute-done | bytes 135200 | tf_op jit(solution)/shard_map/ppermute | solution.py:250
  18.8 1.6 %collective-permute-start.8 = (bf16[528,128]{1,0:T(8,128)(2,1)S(1)}, bf16[528,128]{1,0:T(8,128)(2,1)S(1)}, u32[]{:S(2)}, u32[]{:S(2)}) collective-permute-start(bf16[528,128]{1,0:T(8,128)(2,1)S(1)} %collective-permute-done.5.refs_3_), channel_id=1, source_target_pairs={{0,4},{4,8},{8,12},{12,14},{14,10},{10,6},{6,2},{2,0},{1,5},{5,9},... | collective-permute-start | bytes 405512 | tf_op jit(solution)/shard_map/ppermute | solution.py:250
  20.8 2.6 %collective-permute-start.14 = (bf16[528,128]{1,0:T(8,128)(2,1)S(1)}, bf16[528,128]{1,0:T(8,128)(2,1)S(1)}, u32[]{:S(2)}, u32[]{:S(2)}) collective-permute-start(bf16[528,128]{1,0:T(8,128)(2,1)S(1)} %collective-permute-done.5.refs_3_), channel_id=1, source_target_pairs={{0,8},{4,12},{8,14},{12,10},{14,6},{10,2},{6,0},{2,4},{1,9},{5,13}... | collective-permute-start | bytes 405512 | tf_op jit(solution)/shard_map/ppermute | solution.py:243
  24.0 1.4 %collective-permute-done.9.refs_7_ = bf16[528,128]{1,0:T(8,128)(2,1)S(1)} collective-permute-done((bf16[528,128]{1,0:T(8,128)(2,1)S(1)}, bf16[528,128]{1,0:T(8,128)(2,1)S(1)}, u32[]{:S(2)}, u32[]{:S(2)}) %collective-permute-start.9) | collective-permute-done | bytes 135200 | tf_op jit(solution)/shard_map/ppermute | solution.py:250
  25.4 1.5 %collective-permute-done.14.refs_5_ = bf16[528,128]{1,0:T(8,128)(2,1)S(1)} collective-permute-done((bf16[528,128]{1,0:T(8,128)(2,1)S(1)}, bf16[528,128]{1,0:T(8,128)(2,1)S(1)}, u32[]{:S(2)}, u32[]{:S(2)}) %collective-permute-start.14) | collective-permute-done | bytes 135200 | tf_op jit(solution)/shard_map/ppermute | solution.py:243
  26.9 1.3 %shard_map.40 = bf16[528,512]{1,0:T(8,128)(2,1)S(1)} custom-call(bf16[528,128]{1,0:T(8,128)(2,1)S(1)} %get-tuple-element.45.refs_0_, bf16[528,128]{1,0:T(8,128)(2,1)S(1)} %collective-permute-done.3.refs_1_, bf16[528,128]{1,0:T(8,128)(2,1)S(1)} %collective-permute-done.4.refs_2_, bf16[528,128]{1,0:T(8,128)(2,1)S(1)} %collective-permute-done.5.refs_3_, ...), custom_call_target="tpu_custom_call" | custom-call | tf_op jit(solution)/shard_map/pallas_call | solution.py:193
  28.2 1.4 %collective-permute-start.15 = (bf16[528,512]{1,0:T(8,128)(2,1)S(1)}, bf16[528,512]{1,0:T(8,128)(2,1)S(1)}, u32[]{:S(2)}, u32[]{:S(2)}) collective-permute-start(bf16[528,512]{1,0:T(8,128)(2,1)S(1)} %shard_map.40), channel_id=1, source_target_pairs={{0,1},{1,0},{2,3},{3,2},{4,5},{5,4},{6,7},{7,6},{8,9},{9,8},{10,11... | collective-permute-start | bytes 1622024 | tf_op jit(solution)/shard_map/ppermute | solution.py:238
  29.6 1.4 %collective-permute-start.11 = (bf16[528,128]{1,0:T(8,128)(2,1)S(1)}, bf16[528,128]{1,0:T(8,128)(2,1)S(1)}, u32[]{:S(2)}, u32[]{:S(2)}) collective-permute-start(bf16[528,128]{1,0:T(8,128)(2,1)S(1)} %collective-permute-done.10.refs_4_), channel_id=1, source_target_pairs={{0,6},{4,2},{8,0},{12,4},{14,8},{10,12},{6,14},{2,10},{1,7},{5,3},... | collective-permute-start | bytes 405512 | tf_op jit(solution)/shard_map/ppermute | solution.py:243
  31.0 2.9 %collective-permute-start.12 = (bf16[528,128]{1,0:T(8,128)(2,1)S(1)}, bf16[528,128]{1,0:T(8,128)(2,1)S(1)}, u32[]{:S(2)}, u32[]{:S(2)}) collective-permute-start(bf16[528,128]{1,0:T(8,128)(2,1)S(1)} %collective-permute-done.2.refs_3_), channel_id=1, source_target_pairs={{0,4},{4,8},{8,12},{12,14},{14,10},{10,6},{6,2},{2,0},{1,5},{5,9},... | collective-permute-start | bytes 405512 | tf_op jit(solution)/shard_map/ppermute | solution.py:250
  33.9 1.6 %collective-permute-done.11.refs_5_ = bf16[528,128]{1,0:T(8,128)(2,1)S(1)} collective-permute-done((bf16[528,128]{1,0:T(8,128)(2,1)S(1)}, bf16[528,128]{1,0:T(8,128)(2,1)S(1)}, u32[]{:S(2)}, u32[]{:S(2)}) %collective-permute-start.11) | collective-permute-done | bytes 135200 | tf_op jit(solution)/shard_map/ppermute | solution.py:243
  36.5 2.5 %collective-permute-done.13.refs_7_ = bf16[528,128]{1,0:T(8,128)(2,1)S(1)} collective-permute-done((bf16[528,128]{1,0:T(8,128)(2,1)S(1)}, bf16[528,128]{1,0:T(8,128)(2,1)S(1)}, u32[]{:S(2)}, u32[]{:S(2)}) %collective-permute-start.13) | collective-permute-done | bytes 135200 | tf_op jit(solution)/shard_map/ppermute | solution.py:250
  38.9 1.2 %shard_map.41 = (f32[512,512]{1,0:T(8,128)S(1)}, f32[1,512]{1,0:T(1,128)S(1)}) custom-call(bf16[528,128]{1,0:T(8,128)(2,1)S(1)} %get-tuple-element.32.refs_0_, bf16[528,128]{1,0:T(8,128)(2,1)S(1)} %collective-permute-done.refs_1_, bf16[528,128]{1,0:T(8,128)(2,1)S(1)} %collective-permute-done.1.refs_2_, bf16[528,128]{1,0:T(8,128)(2,1)S(1)} %collective-permute-done.2.refs_3_, ...), custom_call_target="tpu_custom_call" | custom-call | tf_op jit(solution)/shard_map/pallas_call | solution.py:257
  40.2 1.1 %collective-permute-done.16 = f32[1,512]{1,0:T(1,128)S(1)} collective-permute-done((f32[1,512]{1,0:T(1,128)S(1)}, f32[1,512]{1,0:T(1,128)S(1)}, u32[]{:S(2)}, u32[]{:S(2)}) %collective-permute-start.16) | collective-permute-done | bytes 2080 | tf_op jit(solution)/shard_map/ppermute | solution.py:267
  41.3 1.5 %collective-permute-start.17 = (f32[1,512]{1,0:T(1,128)S(1)}, f32[1,512]{1,0:T(1,128)S(1)}, u32[]{:S(2)}, u32[]{:S(2)}) collective-permute-start(f32[1,512]{1,0:T(1,128)S(1)} %add.12), channel_id=1, source_target_pairs={{0,1},{1,0},{2,3},{3,2},{4,5},{5,4},{6,7},{7,6},{8,9},{9,8},{10,11... | collective-permute-start | bytes 6152 | tf_op jit(solution)/shard_map/ppermute | solution.py:268
  42.9 2.1 %collective-permute-done.17 = f32[1,512]{1,0:T(1,128)S(1)} collective-permute-done((f32[1,512]{1,0:T(1,128)S(1)}, f32[1,512]{1,0:T(1,128)S(1)}, u32[]{:S(2)}, u32[]{:S(2)}) %collective-permute-start.17) | collective-permute-done | bytes 2080 | tf_op jit(solution)/shard_map/ppermute | solution.py:268
  44.9 1.1 %broadcast_multiply_fusion = f32[512,512]{1,0:T(8,128)} fusion(f32[512,512]{1,0:T(8,128)S(1)} %get-tuple-element.49, f32[512]{0:T(512)S(1)} %bitcast.8), kind=kLoop, calls=%fused_computation | loop fusion | flops 262144 | bytes 2099200 | tf_op jit(solution)/shard_map/mul | solution.py:270
  (26 shorter events, 5.1 us)
Async XLA Ops:
  0.0 0.9 %copy-start.1 = (bf16[8,1,1,128,128]{4,3,2,1,0:T(8,128)(2,1)S(1)}, bf16[8,1,1,128,128]{4,3,2,1,0:T(8,128)(2,1)}, u32[]{:S(2)}) copy-start(bf16[8,1,1,128,128]{4,3,2,1,0:T(8,128)(2,1)} %param.4) | copy-start | bytes 786436
  1.0 0.7 %copy-start.2 = (s32[8,1,1]{0,2,1:T(1,128)S(1)}, s32[8,1,1]{0,2,1:T(1,128)}, u32[]{:S(2)}) copy-start(s32[8,1,1]{0,2,1:T(1,128)} %param.3) | copy-start | bytes 100
  1.9 13.7 %collective-permute-start.7 = (bf16[4096,512]{1,0:T(8,128)(2,1)}, bf16[4096,512]{1,0:T(8,128)(2,1)S(1)}, u32[]{:S(2)}, u32[]{:S(2)}) collective-permute-start(bf16[4096,512]{1,0:T(8,128)(2,1)} %bitcast.4), channel_id=1, source_target_pairs={{0,16},{16,0},{1,17},{17,1},{2,18},{18,2},{3,19},{19,3},{4,20},{20... | collective-permute-start | bytes 12582920 | tf_op jit(solution)/shard_map/ppermute | solution.py:232
  2.5 7.2 %collective-permute-start.3 = (bf16[528,128]{1,0:T(8,128)(2,1)S(1)}, bf16[528,128]{1,0:T(8,128)(2,1)S(1)}, u32[]{:S(2)}, u32[]{:S(2)}) collective-permute-start(bf16[528,128]{1,0:T(8,128)(2,1)S(1)} %get-tuple-element.45.refs_0_), channel_id=1, source_target_pairs={{0,4},{4,8},{8,12},{12,14},{14,10},{10,6},{6,2},{2,0},{1,5},{5,9},... | collective-permute-start | bytes 405512 | tf_op jit(solution)/shard_map/ppermute | solution.py:250
  5.1 6.4 %collective-permute-start.4 = (bf16[528,128]{1,0:T(8,128)(2,1)S(1)}, bf16[528,128]{1,0:T(8,128)(2,1)S(1)}, u32[]{:S(2)}, u32[]{:S(2)}) collective-permute-start(bf16[528,128]{1,0:T(8,128)(2,1)S(1)} %get-tuple-element.45.refs_0_), channel_id=1, source_target_pairs={{0,2},{4,0},{8,4},{12,8},{14,12},{10,14},{6,10},{2,6},{1,3},{5,1},... | collective-permute-start | bytes 405512 | tf_op jit(solution)/shard_map/ppermute | solution.py:250
  5.1 8.4 %collective-permute-start = (bf16[528,128]{1,0:T(8,128)(2,1)S(1)}, bf16[528,128]{1,0:T(8,128)(2,1)S(1)}, u32[]{:S(2)}, u32[]{:S(2)}) collective-permute-start(bf16[528,128]{1,0:T(8,128)(2,1)S(1)} %get-tuple-element.32.refs_0_), channel_id=1, source_target_pairs={{0,4},{4,8},{8,12},{12,14},{14,10},{10,6},{6,2},{2,0},{1,5},{5,9},... | collective-permute-start | bytes 405512 | tf_op jit(solution)/shard_map/ppermute | solution.py:250
  7.1 8.0 %collective-permute-start.1 = (bf16[528,128]{1,0:T(8,128)(2,1)S(1)}, bf16[528,128]{1,0:T(8,128)(2,1)S(1)}, u32[]{:S(2)}, u32[]{:S(2)}) collective-permute-start(bf16[528,128]{1,0:T(8,128)(2,1)S(1)} %get-tuple-element.32.refs_0_), channel_id=1, source_target_pairs={{0,2},{4,0},{8,4},{12,8},{14,12},{10,14},{6,10},{2,6},{1,3},{5,1},... | collective-permute-start | bytes 405512 | tf_op jit(solution)/shard_map/ppermute | solution.py:250
  7.2 2.2 %copy-start = (bf16[1,4096,512]{2,1,0:T(8,128)(2,1)S(1)}, bf16[1,4096,512]{2,1,0:T(8,128)(2,1)}, u32[]{:S(2)}) copy-start(bf16[1,4096,512]{2,1,0:T(8,128)(2,1)} %param.5) | copy-start | bytes 12582916
  11.5 6.0 %collective-permute-start.5 = (bf16[528,128]{1,0:T(8,128)(2,1)S(1)}, bf16[528,128]{1,0:T(8,128)(2,1)S(1)}, u32[]{:S(2)}, u32[]{:S(2)}) collective-permute-start(bf16[528,128]{1,0:T(8,128)(2,1)S(1)} %collective-permute-done.3.refs_1_), channel_id=1, source_target_pairs={{0,4},{4,8},{8,12},{12,14},{14,10},{10,6},{6,2},{2,0},{1,5},{5,9},... | collective-permute-start | bytes 405512 | tf_op jit(solution)/shard_map/ppermute | solution.py:250
  13.1 5.7 %collective-permute-start.6 = (bf16[528,128]{1,0:T(8,128)(2,1)S(1)}, bf16[528,128]{1,0:T(8,128)(2,1)S(1)}, u32[]{:S(2)}, u32[]{:S(2)}) collective-permute-start(bf16[528,128]{1,0:T(8,128)(2,1)S(1)} %collective-permute-done.4.refs_2_), channel_id=1, source_target_pairs={{0,2},{4,0},{8,4},{12,8},{14,12},{10,14},{6,10},{2,6},{1,3},{5,1},... | collective-permute-start | bytes 405512 | tf_op jit(solution)/shard_map/ppermute | solution.py:250
  13.6 9.8 %collective-permute-start.2 = (bf16[528,128]{1,0:T(8,128)(2,1)S(1)}, bf16[528,128]{1,0:T(8,128)(2,1)S(1)}, u32[]{:S(2)}, u32[]{:S(2)}) collective-permute-start(bf16[528,128]{1,0:T(8,128)(2,1)S(1)} %collective-permute-done.refs_1_), channel_id=1, source_target_pairs={{0,4},{4,8},{8,12},{12,14},{14,10},{10,6},{6,2},{2,0},{1,5},{5,9},... | collective-permute-start | bytes 405512 | tf_op jit(solution)/shard_map/ppermute | solution.py:250
  15.1 8.3 %collective-permute-start.10 = (bf16[528,128]{1,0:T(8,128)(2,1)S(1)}, bf16[528,128]{1,0:T(8,128)(2,1)S(1)}, u32[]{:S(2)}, u32[]{:S(2)}) collective-permute-start(bf16[528,128]{1,0:T(8,128)(2,1)S(1)} %collective-permute-done.1.refs_2_), channel_id=1, source_target_pairs={{0,2},{4,0},{8,4},{12,8},{14,12},{10,14},{6,10},{2,6},{1,3},{5,1},... | collective-permute-start | bytes 405512 | tf_op jit(solution)/shard_map/ppermute | solution.py:250
  18.8 5.2 %collective-permute-start.8 = (bf16[528,128]{1,0:T(8,128)(2,1)S(1)}, bf16[528,128]{1,0:T(8,128)(2,1)S(1)}, u32[]{:S(2)}, u32[]{:S(2)}) collective-permute-start(bf16[528,128]{1,0:T(8,128)(2,1)S(1)} %collective-permute-done.5.refs_3_), channel_id=1, source_target_pairs={{0,4},{4,8},{8,12},{12,14},{14,10},{10,6},{6,2},{2,0},{1,5},{5,9},... | collective-permute-start | bytes 405512 | tf_op jit(solution)/shard_map/ppermute | solution.py:250
  20.4 5.0 %collective-permute-start.9 = (bf16[528,128]{1,0:T(8,128)(2,1)S(1)}, bf16[528,128]{1,0:T(8,128)(2,1)S(1)}, u32[]{:S(2)}, u32[]{:S(2)}) collective-permute-start(bf16[528,128]{1,0:T(8,128)(2,1)S(1)} %collective-permute-done.6.refs_4_), channel_id=1, source_target_pairs={{0,2},{4,0},{8,4},{12,8},{14,12},{10,14},{6,10},{2,6},{1,3},{5,1},... | collective-permute-start | bytes 405512 | tf_op jit(solution)/shard_map/ppermute | solution.py:250
  20.8 6.1 %collective-permute-start.14 = (bf16[528,128]{1,0:T(8,128)(2,1)S(1)}, bf16[528,128]{1,0:T(8,128)(2,1)S(1)}, u32[]{:S(2)}, u32[]{:S(2)}) collective-permute-start(bf16[528,128]{1,0:T(8,128)(2,1)S(1)} %collective-permute-done.5.refs_3_), channel_id=1, source_target_pairs={{0,8},{4,12},{8,14},{12,10},{14,6},{10,2},{6,0},{2,4},{1,9},{5,13}... | collective-permute-start | bytes 405512 | tf_op jit(solution)/shard_map/ppermute | solution.py:243
  28.2 10.7 %collective-permute-start.15 = (bf16[528,512]{1,0:T(8,128)(2,1)S(1)}, bf16[528,512]{1,0:T(8,128)(2,1)S(1)}, u32[]{:S(2)}, u32[]{:S(2)}) collective-permute-start(bf16[528,512]{1,0:T(8,128)(2,1)S(1)} %shard_map.40), channel_id=1, source_target_pairs={{0,1},{1,0},{2,3},{3,2},{4,5},{5,4},{6,7},{7,6},{8,9},{9,8},{10,11... | collective-permute-start | bytes 1622024 | tf_op jit(solution)/shard_map/ppermute | solution.py:238
  29.6 5.9 %collective-permute-start.11 = (bf16[528,128]{1,0:T(8,128)(2,1)S(1)}, bf16[528,128]{1,0:T(8,128)(2,1)S(1)}, u32[]{:S(2)}, u32[]{:S(2)}) collective-permute-start(bf16[528,128]{1,0:T(8,128)(2,1)S(1)} %collective-permute-done.10.refs_4_), channel_id=1, source_target_pairs={{0,6},{4,2},{8,0},{12,4},{14,8},{10,12},{6,14},{2,10},{1,7},{5,3},... | collective-permute-start | bytes 405512 | tf_op jit(solution)/shard_map/ppermute | solution.py:243
  31.0 5.5 %collective-permute-start.12 = (bf16[528,128]{1,0:T(8,128)(2,1)S(1)}, bf16[528,128]{1,0:T(8,128)(2,1)S(1)}, u32[]{:S(2)}, u32[]{:S(2)}) collective-permute-start(bf16[528,128]{1,0:T(8,128)(2,1)S(1)} %collective-permute-done.2.refs_3_), channel_id=1, source_target_pairs={{0,4},{4,8},{8,12},{12,14},{14,10},{10,6},{6,2},{2,0},{1,5},{5,9},... | collective-permute-start | bytes 405512 | tf_op jit(solution)/shard_map/ppermute | solution.py:250
  33.9 5.0 %collective-permute-start.13 = (bf16[528,128]{1,0:T(8,128)(2,1)S(1)}, bf16[528,128]{1,0:T(8,128)(2,1)S(1)}, u32[]{:S(2)}, u32[]{:S(2)}) collective-permute-start(bf16[528,128]{1,0:T(8,128)(2,1)S(1)} %collective-permute-done.10.refs_4_), channel_id=1, source_target_pairs={{0,2},{4,0},{8,4},{12,8},{14,12},{10,14},{6,10},{2,6},{1,3},{5,1},... | collective-permute-start | bytes 405512 | tf_op jit(solution)/shard_map/ppermute | solution.py:250
  40.1 1.2 %collective-permute-start.16 = (f32[1,512]{1,0:T(1,128)S(1)}, f32[1,512]{1,0:T(1,128)S(1)}, u32[]{:S(2)}, u32[]{:S(2)}) collective-permute-start(f32[1,512]{1,0:T(1,128)S(1)} %get-tuple-element.50), channel_id=1, source_target_pairs={{0,16},{16,0},{1,17},{17,1},{2,18},{18,2},{3,19},{19,3},{4,20},{20... | collective-permute-start | bytes 6152 | tf_op jit(solution)/shard_map/ppermute | solution.py:267
  41.3 3.6 %collective-permute-start.17 = (f32[1,512]{1,0:T(1,128)S(1)}, f32[1,512]{1,0:T(1,128)S(1)}, u32[]{:S(2)}, u32[]{:S(2)}) collective-permute-start(f32[1,512]{1,0:T(1,128)S(1)} %add.12), channel_id=1, source_target_pairs={{0,1},{1,0},{2,3},{3,2},{4,5},{5,4},{6,7},{7,6},{8,9},{9,8},{10,11... | collective-permute-start | bytes 6152 | tf_op jit(solution)/shard_map/ppermute | solution.py:268

commit v6 on v5

--- a/solution.py
+++ b/solution.py
@@ -12,9 +12,7 @@
 LOG2E = 1.4426950408889634
 ID_ROWS = 16
 VMEM_BYTES = 24 * 1024 * 1024
-PACK_LIMIT = 24 << 20
-PLAN = ("S=K=T", "O", "S1", "K1", "S=W", "S2", "K2", "J", "S=W", "Sf2", "S3", "S=K", "C", "X", "Kf2", "K3")
-PLACE_LIMIT = 24 << 20
+PLAN = ("S=K=T", "O", "S1", "K1", "S=W", "Sp", "Kp", "S2", "K2", "J", "S=W=Sp=Kp", "S3", "Sm", "S=K", "C", "X", "K3", "Km")
 
 
 def pack_kernel(cols_ref, vals_ref, *refs):
@@ -127,24 +125,17 @@
     sum_ref[...] = functools.reduce(jnp.add, sums)
 
 
-def ring_of(mesh):
-    size = mesh.shape["col"]
-    if size != 8:
-        return list(range(size))
-    return [0, 2, 4, 6, 7, 5, 3, 1]
-
-
 def solution(mesh):
     size = mesh.shape["col"]
-    order = ring_of(mesh)
+    ring = [0, 2, 4, 6, 7, 5, 3, 1]
+    across = [(ring[a], ring[b]) for a, b in ((6, 1), (5, 2), (2, 5), (1, 6), (3, 0), (0, 3), (7, 4), (4, 7))]
+
     def shift(hops):
-        return [(order[i], order[(i + hops) % size]) for i in range(size)]
+        return [(ring[i], ring[(i + hops) % len(ring)]) for i in range(len(ring))]
 
     swap = [(0, 1), (1, 0)]
     vmem = pl.BlockSpec(memory_space=pltpu.VMEM)
     anywhere = pl.BlockSpec(memory_space=pl.ANY)
-
-    across = [(order[a], order[b]) for a, b in ((6, 1), (5, 2), (2, 5), (1, 6), (3, 0), (0, 3), (7, 4), (4, 7))] if size == 8 else []
 
     def gather_all(item):
         stacked = lax.all_gather(item, "col", axis=0)
@@ -164,7 +155,7 @@
             in_specs=[vmem, anywhere],
             out_specs=(vmem,) * 2,
             scratch_shapes=[pltpu.SemaphoreType.DMA((2,))],
-            compiler_params=pltpu.CompilerParams(vmem_limit_bytes=PACK_LIMIT),
+            compiler_params=params,
         )(flow_cols.reshape(1, 2 * count), flow_vals.reshape(2 * rows, block))
         theirs = own
         send, keep = items[:1] * 3, items[1:] * 3
@@ -183,7 +174,7 @@
                 out_specs=vmem,
                 scratch_shapes=[pltpu.SemaphoreType.DMA(())],
                 input_output_aliases={1: 0} if given else {},
-                compiler_params=pltpu.CompilerParams(vmem_limit_bytes=PLACE_LIMIT),
+                compiler_params=params,
                 cost_estimate=pl.CostEstimate(flops=0, bytes_accessed=2 * half * columns * 2, transcendentals=0),
             )(part, *given)
 
@@ -238,9 +229,6 @@
                     code = lax.ppermute(code, "layer", swap)
                 elif "=" in name:
                     tie(name.split("="))
-                elif name[1] == "f":
-                    kind, way = (name[0], 2 if name[0] == "S" else -2)
-                    lists[kind].append(lax.ppermute(ends[kind][0 if way > 0 else 1], "col", shift(way)))
                 elif name[1] == "p":
                     chosen[name[0]] = pick(*ends[name[0]])
                 elif name[1] == "m":
@@ -264,8 +252,8 @@
             out_specs=(vmem, vmem),
             compiler_params=params,
         )(*keeps, window, code)
-        sums = sums + lax.ppermute(sums, "row", swap)
-        sums = sums + lax.ppermute(sums, "layer", swap)
+        cross = [(0, 3), (1, 2), (2, 1), (3, 0)]
+        sums = sums + lax.ppermute(sums, "row", swap) + lax.ppermute(sums, "layer", swap) + lax.ppermute(sums, ("row", "layer"), cross)
         total_rows = rows * lax.axis_size("row") * lax.axis_size("layer")
         return square * (1.0 / (sums / total_rows + 1e-6))
 

time: 46.2 us -> 45.9 us (level)
    ppermute x12, waiting for transfers between devices: 10.1 us -> 6.53 us  [body(): lax.ppermute(e, 'col', shift(w))]
    ppermute x4 -> x5, waiting for transfers between devices: 6.33 us -> 9.34 us  [the longest x2 6.64 us: body(): lists[name[0]].append(lax.ppermute(chosen[name[0]], 'col', across))]
    ppermute x12, starting transfers between devices: 13.7 us -> 12.9 us  [body(): lax.ppermute(e, 'col', shift(w))]
    ppermute x4 -> x5, starting transfers between devices: 5.57 us -> 6.17 us  [the longest x2 4.24 us: body(): lists[name[0]].append(lax.ppermute(chosen[name[0]], 'col', across))]
  transfers between devices with their start and end apart: 18 -> 19, of which waited for: 11 -> 10; matrix products, arithmetic and copies ran while one was open for 0% -> 0% of each run, Pallas kernels for 1% -> 1%
where the time goes in v6:
time: 45.9 us; the launch traced here: 45.8 us
  starting transfers between devices  21.1 us (46%)
  waiting for transfers between devices  16.2 us (35%)
  local copies, waits for them, and re-layouts  3.79 us (8%)
  Pallas kernels  3.42 us (7%)
  other arithmetic  1.11 us (2%)
    ppermute x12, starting transfers between devices, body(): lax.ppermute(e, 'col', shift(w))  12.9 us
    ppermute x2, waiting for transfers between devices, body(): lists[name[0]].append(lax.ppermute(chosen[name[0]], 'col', across))  6.64 us
    ppermute x12, waiting for transfers between devices, body(): lax.ppermute(e, 'col', shift(w))  6.53 us
    ppermute x2, starting transfers between devices, body(): lists[name[0]].append(lax.ppermute(chosen[name[0]], 'col', across))  4.24 us
    unnamed x6, local copies, waits for them, and re-layouts  3.79 us
    ppermute x1, waiting for transfers between devices, body(): lax.ppermute(sums, 'layer', swap)  1.78 us
    ppermute x1, starting transfers between devices, body(): lax.ppermute(sums, 'layer', swap)  1.56 us
    ppermute x1, starting transfers between devices, body(): code = lax.ppermute(code, 'layer', swap)  1.55 us
  transfers between devices with their start and end apart: 19, of which 10 were waited for; matrix products, arithmetic and copies ran while one was open for 0% of the time, Pallas kernels for 1%

profile of v6, /device:TPU:0, one launch (start us, length us, event | category | flops | bytes accessed | tf_op | source)
XLA Modules:
  0.0 45.8 jit_solution(16603244229863693891)
XLA Ops:
  0.0 0.9 %copy-done.1 = bf16[8,1,1,128,128]{4,3,2,1,0:T(8,128)(2,1)S(1)} copy-done((bf16[8,1,1,128,128]{4,3,2,1,0:T(8,128)(2,1)S(1)}, bf16[8,1,1,128,128]{4,3,2,1,0:T(8,128)(2,1)}, u32[]{:S(2)}) %copy-start.1) | copy-done | bytes 262168
  2.5 2.6 %collective-permute-start.3 = (bf16[528,128]{1,0:T(8,128)(2,1)S(1)}, bf16[528,128]{1,0:T(8,128)(2,1)S(1)}, u32[]{:S(2)}, u32[]{:S(2)}) collective-permute-start(bf16[528,128]{1,0:T(8,128)(2,1)S(1)} %get-tuple-element.49.refs_0_), channel_id=1, source_target_pairs={{0,4},{4,8},{8,12},{12,14},{14,10},{10,6},{6,2},{2,0},{1,5},{5,9},... | collective-permute-start | bytes 405512 | tf_op jit(solution)/shard_map/ppermute | solution.py:238
  5.1 2.0 %collective-permute-start = (bf16[528,128]{1,0:T(8,128)(2,1)S(1)}, bf16[528,128]{1,0:T(8,128)(2,1)S(1)}, u32[]{:S(2)}, u32[]{:S(2)}) collective-permute-start(bf16[528,128]{1,0:T(8,128)(2,1)S(1)} %get-tuple-element.34.refs_0_), channel_id=1, source_target_pairs={{0,4},{4,8},{8,12},{12,14},{14,10},{10,6},{6,2},{2,0},{1,5},{5,9},... | collective-permute-start | bytes 405512 | tf_op jit(solution)/shard_map/ppermute | solution.py:238
  7.2 2.2 %copy-done = bf16[1,4096,512]{2,1,0:T(8,128)(2,1)S(1)} copy-done((bf16[1,4096,512]{2,1,0:T(8,128)(2,1)S(1)}, bf16[1,4096,512]{2,1,0:T(8,128)(2,1)}, u32[]{:S(2)}) %copy-start) | copy-done | bytes 4194328
  9.7 1.9 %collective-permute-done.4.last_ref.refs_2_ = bf16[528,128]{1,0:T(8,128)(2,1)S(1)} collective-permute-done((bf16[528,128]{1,0:T(8,128)(2,1)S(1)}, bf16[528,128]{1,0:T(8,128)(2,1)S(1)}, u32[]{:S(2)}, u32[]{:S(2)}) %collective-permute-start.4) | collective-permute-done | bytes 135200 | tf_op jit(solution)/shard_map/ppermute | solution.py:238
  11.5 1.6 %collective-permute-start.5 = (bf16[528,128]{1,0:T(8,128)(2,1)S(1)}, bf16[528,128]{1,0:T(8,128)(2,1)S(1)}, u32[]{:S(2)}, u32[]{:S(2)}) collective-permute-start(bf16[528,128]{1,0:T(8,128)(2,1)S(1)} %collective-permute-done.3.first_ref.refs_1_), channel_id=1, source_target_pairs={{0,4},{4,8},{8,12},{12,14},{14,10},{10,6},{6,2},{2,0},{1,5},{5,9},... | collective-permute-start | bytes 405512 | tf_op jit(solution)/shard_map/ppermute | solution.py:238
  13.6 1.6 %collective-permute-start.2 = (bf16[528,128]{1,0:T(8,128)(2,1)S(1)}, bf16[528,128]{1,0:T(8,128)(2,1)S(1)}, u32[]{:S(2)}, u32[]{:S(2)}) collective-permute-start(bf16[528,128]{1,0:T(8,128)(2,1)S(1)} %collective-permute-done.first_ref.refs_1_), channel_id=1, source_target_pairs={{0,4},{4,8},{8,12},{12,14},{14,10},{10,6},{6,2},{2,0},{1,5},{5,9},... | collective-permute-start | bytes 405512 | tf_op jit(solution)/shard_map/ppermute | solution.py:238
  16.0 1.4 %collective-permute-done.5.refs_3_ = bf16[528,128]{1,0:T(8,128)(2,1)S(1)} collective-permute-done((bf16[528,128]{1,0:T(8,128)(2,1)S(1)}, bf16[528,128]{1,0:T(8,128)(2,1)S(1)}, u32[]{:S(2)}, u32[]{:S(2)}) %collective-permute-start.5) | collective-permute-done | bytes 135200 | tf_op jit(solution)/shard_map/ppermute | solution.py:238
  17.5 1.4 %collective-permute-done.6.refs_4_ = bf16[528,128]{1,0:T(8,128)(2,1)S(1)} collective-permute-done((bf16[528,128]{1,0:T(8,128)(2,1)S(1)}, bf16[528,128]{1,0:T(8,128)(2,1)S(1)}, u32[]{:S(2)}, u32[]{:S(2)}) %collective-permute-start.6) | collective-permute-done | bytes 135200 | tf_op jit(solution)/shard_map/ppermute | solution.py:238
  18.9 2.8 %collective-permute-start.10 = (bf16[528,128]{1,0:T(8,128)(2,1)S(1)}, bf16[528,128]{1,0:T(8,128)(2,1)S(1)}, u32[]{:S(2)}, u32[]{:S(2)}) collective-permute-start(bf16[528,128]{1,0:T(8,128)(2,1)S(1)} %shard_map.40), channel_id=1, source_target_pairs={{6,4},{10,8},{8,10},{4,6},{12,0},{0,12},{2,14},{14,2},{7,5},{11,9}... | collective-permute-start | bytes 405512 | tf_op jit(solution)/shard_map/ppermute | solution.py:235
  21.7 2.0 %collective-permute-start.9 = (bf16[528,128]{1,0:T(8,128)(2,1)S(1)}, bf16[528,128]{1,0:T(8,128)(2,1)S(1)}, u32[]{:S(2)}, u32[]{:S(2)}) collective-permute-start(bf16[528,128]{1,0:T(8,128)(2,1)S(1)} %collective-permute-done.6.refs_4_), channel_id=1, source_target_pairs={{0,2},{4,0},{8,4},{12,8},{14,12},{10,14},{6,10},{2,6},{1,3},{5,1},... | collective-permute-start | bytes 405512 | tf_op jit(solution)/shard_map/ppermute | solution.py:238
  23.7 3.2 %collective-permute-done.10.refs_7_ = bf16[528,128]{1,0:T(8,128)(2,1)S(1)} collective-permute-done((bf16[528,128]{1,0:T(8,128)(2,1)S(1)}, bf16[528,128]{1,0:T(8,128)(2,1)S(1)}, u32[]{:S(2)}, u32[]{:S(2)}) %collective-permute-start.10) | collective-permute-done | bytes 135200 | tf_op jit(solution)/shard_map/ppermute | solution.py:235
  26.8 0.9 %collective-permute-done.9.refs_6_ = bf16[528,128]{1,0:T(8,128)(2,1)S(1)} collective-permute-done((bf16[528,128]{1,0:T(8,128)(2,1)S(1)}, bf16[528,128]{1,0:T(8,128)(2,1)S(1)}, u32[]{:S(2)}, u32[]{:S(2)}) %collective-permute-start.9) | collective-permute-done | bytes 135200 | tf_op jit(solution)/shard_map/ppermute | solution.py:238
  27.7 1.3 %shard_map.42 = bf16[528,512]{1,0:T(8,128)(2,1)S(1)} custom-call(bf16[528,128]{1,0:T(8,128)(2,1)S(1)} %get-tuple-element.49.refs_0_, bf16[528,128]{1,0:T(8,128)(2,1)S(1)} %collective-permute-done.3.first_ref.refs_1_, bf16[528,128]{1,0:T(8,128)(2,1)S(1)} %collective-permute-done.4.last_ref.refs_2_, bf16[528,128]{1,0:T(8,128)(2,1)S(1)} %collective-permute-done.5.refs_3_, ...), custom_call_target="tpu_custom_call" | custom-call | tf_op jit(solution)/shard_map/pallas_call | solution.py:184
  29.0 1.6 %collective-permute-start.15 = (bf16[528,512]{1,0:T(8,128)(2,1)S(1)}, bf16[528,512]{1,0:T(8,128)(2,1)S(1)}, u32[]{:S(2)}, u32[]{:S(2)}) collective-permute-start(bf16[528,512]{1,0:T(8,128)(2,1)S(1)} %shard_map.42), channel_id=1, source_target_pairs={{0,1},{1,0},{2,3},{3,2},{4,5},{5,4},{6,7},{7,6},{8,9},{9,8},{10,11... | collective-permute-start | bytes 1622024 | tf_op jit(solution)/shard_map/ppermute | solution.py:229
  30.6 1.5 %collective-permute-start.14 = (bf16[528,128]{1,0:T(8,128)(2,1)S(1)}, bf16[528,128]{1,0:T(8,128)(2,1)S(1)}, u32[]{:S(2)}, u32[]{:S(2)}) collective-permute-start(bf16[528,128]{1,0:T(8,128)(2,1)S(1)} %shard_map.41), channel_id=1, source_target_pairs={{6,4},{10,8},{8,10},{4,6},{12,0},{0,12},{2,14},{14,2},{7,5},{11,9}... | collective-permute-start | bytes 405512 | tf_op jit(solution)/shard_map/ppermute | solution.py:235
  32.0 2.0 %collective-permute-start.13 = (bf16[528,128]{1,0:T(8,128)(2,1)S(1)}, bf16[528,128]{1,0:T(8,128)(2,1)S(1)}, u32[]{:S(2)}, u32[]{:S(2)}) collective-permute-start(bf16[528,128]{1,0:T(8,128)(2,1)S(1)} %collective-permute-done.11.refs_4_), channel_id=1, source_target_pairs={{0,2},{4,0},{8,4},{12,8},{14,12},{10,14},{6,10},{2,6},{1,3},{5,1},... | collective-permute-start | bytes 405512 | tf_op jit(solution)/shard_map/ppermute | solution.py:238
  34.1 3.5 %collective-permute-done.14.refs_7_ = bf16[528,128]{1,0:T(8,128)(2,1)S(1)} collective-permute-done((bf16[528,128]{1,0:T(8,128)(2,1)S(1)}, bf16[528,128]{1,0:T(8,128)(2,1)S(1)}, u32[]{:S(2)}, u32[]{:S(2)}) %collective-permute-start.14) | collective-permute-done | bytes 135200 | tf_op jit(solution)/shard_map/ppermute | solution.py:235
  37.5 1.0 %collective-permute-done.13.refs_6_ = bf16[528,128]{1,0:T(8,128)(2,1)S(1)} collective-permute-done((bf16[528,128]{1,0:T(8,128)(2,1)S(1)}, bf16[528,128]{1,0:T(8,128)(2,1)S(1)}, u32[]{:S(2)}, u32[]{:S(2)}) %collective-permute-start.13) | collective-permute-done | bytes 135200 | tf_op jit(solution)/shard_map/ppermute | solution.py:238
  38.8 1.2 %shard_map.43 = (f32[512,512]{1,0:T(8,128)S(1)}, f32[1,512]{1,0:T(1,128)S(1)}) custom-call(bf16[528,128]{1,0:T(8,128)(2,1)S(1)} %get-tuple-element.34.refs_0_, bf16[528,128]{1,0:T(8,128)(2,1)S(1)} %collective-permute-done.first_ref.refs_1_, bf16[528,128]{1,0:T(8,128)(2,1)S(1)} %collective-permute-done.1.last_ref.refs_2_, ...), custom_call_target="tpu_custom_call" | custom-call | tf_op jit(solution)/shard_map/pallas_call | solution.py:245
  40.1 1.6 %collective-permute-start.17 = (f32[1,512]{1,0:T(1,128)S(1)}, f32[1,512]{1,0:T(1,128)S(1)}, u32[]{:S(2)}, u32[]{:S(2)}) collective-permute-start(f32[1,512]{1,0:T(1,128)S(1)} %get-tuple-element.54), channel_id=1, source_target_pairs={{0,1},{1,0},{2,3},{3,2},{4,5},{5,4},{6,7},{7,6},{8,9},{9,8},{10,11... | collective-permute-start | bytes 6152 | tf_op jit(solution)/shard_map/ppermute | solution.py:256
  41.9 1.8 %collective-permute-done.17 = f32[1,512]{1,0:T(1,128)S(1)} collective-permute-done((f32[1,512]{1,0:T(1,128)S(1)}, f32[1,512]{1,0:T(1,128)S(1)}, u32[]{:S(2)}, u32[]{:S(2)}) %collective-permute-start.17) | collective-permute-done | bytes 2080 | tf_op jit(solution)/shard_map/ppermute | solution.py:256
  43.7 0.9 %collective-permute-done.18 = f32[1,512]{1,0:T(1,128)S(1)} collective-permute-done((f32[1,512]{1,0:T(1,128)S(1)}, f32[1,512]{1,0:T(1,128)S(1)}, u32[]{:S(2)}, u32[]{:S(2)}) %collective-permute-start.18) | collective-permute-done | bytes 2080 | tf_op jit(solution)/shard_map/ppermute | solution.py:256
  44.7 1.1 %broadcast_multiply_fusion = f32[512,512]{1,0:T(8,128)} fusion(f32[512,512]{1,0:T(8,128)S(1)} %get-tuple-element.53, f32[512]{0:T(512)S(1)} %bitcast.8), kind=kLoop, calls=%fused_computation | loop fusion | flops 262144 | bytes 2099200 | tf_op jit(solution)/shard_map/mul | solution.py:258
  (29 shorter events, 3.8 us)
Async XLA Ops:
  0.0 0.9 %copy-start.1 = (bf16[8,1,1,128,128]{4,3,2,1,0:T(8,128)(2,1)S(1)}, bf16[8,1,1,128,128]{4,3,2,1,0:T(8,128)(2,1)}, u32[]{:S(2)}) copy-start(bf16[8,1,1,128,128]{4,3,2,1,0:T(8,128)(2,1)} %param.4) | copy-start | bytes 786436
  1.0 0.7 %copy-start.2 = (s32[8,1,1]{0,2,1:T(1,128)S(1)}, s32[8,1,1]{0,2,1:T(1,128)}, u32[]{:S(2)}) copy-start(s32[8,1,1]{0,2,1:T(1,128)} %param.3) | copy-start | bytes 100
  1.9 13.8 %collective-permute-start.7 = (bf16[4096,512]{1,0:T(8,128)(2,1)}, bf16[4096,512]{1,0:T(8,128)(2,1)S(1)}, u32[]{:S(2)}, u32[]{:S(2)}) collective-permute-start(bf16[4096,512]{1,0:T(8,128)(2,1)} %bitcast.4), channel_id=1, source_target_pairs={{0,16},{16,0},{1,17},{17,1},{2,18},{18,2},{3,19},{19,3},{4,20},{20... | collective-permute-start | bytes 12582920 | tf_op jit(solution)/shard_map/ppermute | solution.py:223
  2.5 7.2 %collective-permute-start.3 = (bf16[528,128]{1,0:T(8,128)(2,1)S(1)}, bf16[528,128]{1,0:T(8,128)(2,1)S(1)}, u32[]{:S(2)}, u32[]{:S(2)}) collective-permute-start(bf16[528,128]{1,0:T(8,128)(2,1)S(1)} %get-tuple-element.49.refs_0_), channel_id=1, source_target_pairs={{0,4},{4,8},{8,12},{12,14},{14,10},{10,6},{6,2},{2,0},{1,5},{5,9},... | collective-permute-start | bytes 405512 | tf_op jit(solution)/shard_map/ppermute | solution.py:238
  5.1 6.4 %collective-permute-start.4 = (bf16[528,128]{1,0:T(8,128)(2,1)S(1)}, bf16[528,128]{1,0:T(8,128)(2,1)S(1)}, u32[]{:S(2)}, u32[]{:S(2)}) collective-permute-start(bf16[528,128]{1,0:T(8,128)(2,1)S(1)} %get-tuple-element.49.refs_0_), channel_id=1, source_target_pairs={{0,2},{4,0},{8,4},{12,8},{14,12},{10,14},{6,10},{2,6},{1,3},{5,1},... | collective-permute-start | bytes 405512 | tf_op jit(solution)/shard_map/ppermute | solution.py:238
  5.1 8.5 %collective-permute-start = (bf16[528,128]{1,0:T(8,128)(2,1)S(1)}, bf16[528,128]{1,0:T(8,128)(2,1)S(1)}, u32[]{:S(2)}, u32[]{:S(2)}) collective-permute-start(bf16[528,128]{1,0:T(8,128)(2,1)S(1)} %get-tuple-element.34.refs_0_), channel_id=1, source_target_pairs={{0,4},{4,8},{8,12},{12,14},{14,10},{10,6},{6,2},{2,0},{1,5},{5,9},... | collective-permute-start | bytes 405512 | tf_op jit(solution)/shard_map/ppermute | solution.py:238
  7.1 8.1 %collective-permute-start.1 = (bf16[528,128]{1,0:T(8,128)(2,1)S(1)}, bf16[528,128]{1,0:T(8,128)(2,1)S(1)}, u32[]{:S(2)}, u32[]{:S(2)}) collective-permute-start(bf16[528,128]{1,0:T(8,128)(2,1)S(1)} %get-tuple-element.34.refs_0_), channel_id=1, source_target_pairs={{0,2},{4,0},{8,4},{12,8},{14,12},{10,14},{6,10},{2,6},{1,3},{5,1},... | collective-permute-start | bytes 405512 | tf_op jit(solution)/shard_map/ppermute | solution.py:238
  7.2 2.2 %copy-start = (bf16[1,4096,512]{2,1,0:T(8,128)(2,1)S(1)}, bf16[1,4096,512]{2,1,0:T(8,128)(2,1)}, u32[]{:S(2)}) copy-start(bf16[1,4096,512]{2,1,0:T(8,128)(2,1)} %param.5) | copy-start | bytes 12582916
  11.5 6.0 %collective-permute-start.5 = (bf16[528,128]{1,0:T(8,128)(2,1)S(1)}, bf16[528,128]{1,0:T(8,128)(2,1)S(1)}, u32[]{:S(2)}, u32[]{:S(2)}) collective-permute-start(bf16[528,128]{1,0:T(8,128)(2,1)S(1)} %collective-permute-done.3.first_ref.refs_1_), channel_id=1, source_target_pairs={{0,4},{4,8},{8,12},{12,14},{14,10},{10,6},{6,2},{2,0},{1,5},{5,9},... | collective-permute-start | bytes 405512 | tf_op jit(solution)/shard_map/ppermute | solution.py:238
  13.1 5.8 %collective-permute-start.6 = (bf16[528,128]{1,0:T(8,128)(2,1)S(1)}, bf16[528,128]{1,0:T(8,128)(2,1)S(1)}, u32[]{:S(2)}, u32[]{:S(2)}) collective-permute-start(bf16[528,128]{1,0:T(8,128)(2,1)S(1)} %collective-permute-done.4.last_ref.refs_2_), channel_id=1, source_target_pairs={{0,2},{4,0},{8,4},{12,8},{14,12},{10,14},{6,10},{2,6},{1,3},{5,1},... | collective-permute-start | bytes 405512 | tf_op jit(solution)/shard_map/ppermute | solution.py:238
  13.6 10.1 %collective-permute-start.2 = (bf16[528,128]{1,0:T(8,128)(2,1)S(1)}, bf16[528,128]{1,0:T(8,128)(2,1)S(1)}, u32[]{:S(2)}, u32[]{:S(2)}) collective-permute-start(bf16[528,128]{1,0:T(8,128)(2,1)S(1)} %collective-permute-done.first_ref.refs_1_), channel_id=1, source_target_pairs={{0,4},{4,8},{8,12},{12,14},{14,10},{10,6},{6,2},{2,0},{1,5},{5,9},... | collective-permute-start | bytes 405512 | tf_op jit(solution)/shard_map/ppermute | solution.py:238
  15.2 8.4 %collective-permute-start.11 = (bf16[528,128]{1,0:T(8,128)(2,1)S(1)}, bf16[528,128]{1,0:T(8,128)(2,1)S(1)}, u32[]{:S(2)}, u32[]{:S(2)}) collective-permute-start(bf16[528,128]{1,0:T(8,128)(2,1)S(1)} %collective-permute-done.1.last_ref.refs_2_), channel_id=1, source_target_pairs={{0,2},{4,0},{8,4},{12,8},{14,12},{10,14},{6,10},{2,6},{1,3},{5,1},... | collective-permute-start | bytes 405512 | tf_op jit(solution)/shard_map/ppermute | solution.py:238
  18.9 8.0 %collective-permute-start.10 = (bf16[528,128]{1,0:T(8,128)(2,1)S(1)}, bf16[528,128]{1,0:T(8,128)(2,1)S(1)}, u32[]{:S(2)}, u32[]{:S(2)}) collective-permute-start(bf16[528,128]{1,0:T(8,128)(2,1)S(1)} %shard_map.40), channel_id=1, source_target_pairs={{6,4},{10,8},{8,10},{4,6},{12,0},{0,12},{2,14},{14,2},{7,5},{11,9}... | collective-permute-start | bytes 405512 | tf_op jit(solution)/shard_map/ppermute | solution.py:235
  21.6 5.2 %collective-permute-start.8 = (bf16[528,128]{1,0:T(8,128)(2,1)S(1)}, bf16[528,128]{1,0:T(8,128)(2,1)S(1)}, u32[]{:S(2)}, u32[]{:S(2)}) collective-permute-start(bf16[528,128]{1,0:T(8,128)(2,1)S(1)} %collective-permute-done.5.refs_3_), channel_id=1, source_target_pairs={{0,4},{4,8},{8,12},{12,14},{14,10},{10,6},{6,2},{2,0},{1,5},{5,9},... | collective-permute-start | bytes 405512 | tf_op jit(solution)/shard_map/ppermute | solution.py:238
  21.7 6.0 %collective-permute-start.9 = (bf16[528,128]{1,0:T(8,128)(2,1)S(1)}, bf16[528,128]{1,0:T(8,128)(2,1)S(1)}, u32[]{:S(2)}, u32[]{:S(2)}) collective-permute-start(bf16[528,128]{1,0:T(8,128)(2,1)S(1)} %collective-permute-done.6.refs_4_), channel_id=1, source_target_pairs={{0,2},{4,0},{8,4},{12,8},{14,12},{10,14},{6,10},{2,6},{1,3},{5,1},... | collective-permute-start | bytes 405512 | tf_op jit(solution)/shard_map/ppermute | solution.py:238
  29.0 9.8 %collective-permute-start.15 = (bf16[528,512]{1,0:T(8,128)(2,1)S(1)}, bf16[528,512]{1,0:T(8,128)(2,1)S(1)}, u32[]{:S(2)}, u32[]{:S(2)}) collective-permute-start(bf16[528,512]{1,0:T(8,128)(2,1)S(1)} %shard_map.42), channel_id=1, source_target_pairs={{0,1},{1,0},{2,3},{3,2},{4,5},{5,4},{6,7},{7,6},{8,9},{9,8},{10,11... | collective-permute-start | bytes 1622024 | tf_op jit(solution)/shard_map/ppermute | solution.py:229
  30.6 7.0 %collective-permute-start.14 = (bf16[528,128]{1,0:T(8,128)(2,1)S(1)}, bf16[528,128]{1,0:T(8,128)(2,1)S(1)}, u32[]{:S(2)}, u32[]{:S(2)}) collective-permute-start(bf16[528,128]{1,0:T(8,128)(2,1)S(1)} %shard_map.41), channel_id=1, source_target_pairs={{6,4},{10,8},{8,10},{4,6},{12,0},{0,12},{2,14},{14,2},{7,5},{11,9}... | collective-permute-start | bytes 405512 | tf_op jit(solution)/shard_map/ppermute | solution.py:235
  32.0 5.5 %collective-permute-start.12 = (bf16[528,128]{1,0:T(8,128)(2,1)S(1)}, bf16[528,128]{1,0:T(8,128)(2,1)S(1)}, u32[]{:S(2)}, u32[]{:S(2)}) collective-permute-start(bf16[528,128]{1,0:T(8,128)(2,1)S(1)} %collective-permute-done.2.refs_3_), channel_id=1, source_target_pairs={{0,4},{4,8},{8,12},{12,14},{14,10},{10,6},{6,2},{2,0},{1,5},{5,9},... | collective-permute-start | bytes 405512 | tf_op jit(solution)/shard_map/ppermute | solution.py:238
  32.0 6.5 %collective-permute-start.13 = (bf16[528,128]{1,0:T(8,128)(2,1)S(1)}, bf16[528,128]{1,0:T(8,128)(2,1)S(1)}, u32[]{:S(2)}, u32[]{:S(2)}) collective-permute-start(bf16[528,128]{1,0:T(8,128)(2,1)S(1)} %collective-permute-done.11.refs_4_), channel_id=1, source_target_pairs={{0,2},{4,0},{8,4},{12,8},{14,12},{10,14},{6,10},{2,6},{1,3},{5,1},... | collective-permute-start | bytes 405512 | tf_op jit(solution)/shard_map/ppermute | solution.py:238
  40.0 1.9 %collective-permute-start.16 = (f32[1,512]{1,0:T(1,128)S(1)}, f32[1,512]{1,0:T(1,128)S(1)}, u32[]{:S(2)}, u32[]{:S(2)}) collective-permute-start(f32[1,512]{1,0:T(1,128)S(1)} %get-tuple-element.54), channel_id=1, source_target_pairs={{0,16},{16,0},{1,17},{17,1},{2,18},{18,2},{3,19},{19,3},{4,20},{20... | collective-permute-start | bytes 6152 | tf_op jit(solution)/shard_map/ppermute | solution.py:256
  40.1 3.7 %collective-permute-start.17 = (f32[1,512]{1,0:T(1,128)S(1)}, f32[1,512]{1,0:T(1,128)S(1)}, u32[]{:S(2)}, u32[]{:S(2)}) collective-permute-start(f32[1,512]{1,0:T(1,128)S(1)} %get-tuple-element.54), channel_id=1, source_target_pairs={{0,1},{1,0},{2,3},{3,2},{4,5},{5,4},{6,7},{7,6},{8,9},{9,8},{10,11... | collective-permute-start | bytes 6152 | tf_op jit(solution)/shard_map/ppermute | solution.py:256
  41.6 3.0 %collective-permute-start.18 = (f32[1,512]{1,0:T(1,128)S(1)}, f32[1,512]{1,0:T(1,128)S(1)}, u32[]{:S(2)}, u32[]{:S(2)}) collective-permute-start(f32[1,512]{1,0:T(1,128)S(1)} %get-tuple-element.54), channel_id=1, source_target_pairs={{0,17},{1,16},{16,1},{17,0},{2,19},{3,18},{18,3},{19,2},{4,21},{5,... | collective-permute-start | bytes 6152 | tf_op jit(solution)/shard_map/ppermute | solution.py:256

commit v7 on v6

--- a/solution.py
+++ b/solution.py
@@ -41,7 +41,7 @@
 
 def pick_kernel(first_ref, last_ref, out_ref):
     col = lax.axis_index("col")
-    odd = lax.rem(col + lax.div(col, 2), 2)
+    odd = lax.rem(col + lax.div(col, 2) + 1, 2)
 
     @pl.when(odd == 0)
     def _():
@@ -127,7 +127,7 @@
 
 def solution(mesh):
     size = mesh.shape["col"]
-    ring = [0, 2, 4, 6, 7, 5, 3, 1]
+    ring = [6, 4, 2, 0, 1, 3, 5, 7]
     across = [(ring[a], ring[b]) for a, b in ((6, 1), (5, 2), (2, 5), (1, 6), (3, 0), (0, 3), (7, 4), (4, 7))]
 
     def shift(hops):

time: 45.9 us -> 45.4 us (0.989)
  starting transfers between devices: 21.1 us -> 20.4 us
    ppermute x12, waiting for transfers between devices: 6.53 us -> 7.38 us  [body(): lax.ppermute(e, 'col', shift(w))]
    ppermute x2, starting transfers between devices: 4.24 us -> 3.44 us  [body(): lists[name[0]].append(lax.ppermute(chosen[name[0]], 'col', across))]
  transfers between devices with their start and end apart: 19 -> 19, of which waited for: 10 -> 11; matrix products, arithmetic and copies ran while one was open for 0% -> 0% of each run, Pallas kernels for 1% -> 1%
where the time goes in v7:
time: 45.4 us; the launch traced here: 45.2 us
  starting transfers between devices  20.4 us (45%)
  waiting for transfers between devices  16.4 us (36%)
  local copies, waits for them, and re-layouts  3.79 us (8%)
  Pallas kernels  3.42 us (8%)
  other arithmetic  1.11 us (2%)
    ppermute x12, starting transfers between devices, body(): lax.ppermute(e, 'col', shift(w))  13 us
    ppermute x12, waiting for transfers between devices, body(): lax.ppermute(e, 'col', shift(w))  7.38 us
    ppermute x2, waiting for transfers between devices, body(): lists[name[0]].append(lax.ppermute(chosen[name[0]], 'col', across))  6.43 us
    unnamed x6, local copies, waits for them, and re-layouts  3.79 us
    ppermute x2, starting transfers between devices, body(): lists[name[0]].append(lax.ppermute(chosen[name[0]], 'col', across))  3.44 us
    ppermute x1, waiting for transfers between devices, body(): lax.ppermute(sums, 'layer', swap)  1.78 us
    ppermute x1, starting transfers between devices, body(): code = lax.ppermute(code, 'layer', swap)  1.55 us
    ppermute x1, starting transfers between devices, body(): lax.ppermute(sums, 'layer', swap)  1.4 us
  transfers between devices with their start and end apart: 19, of which 11 were waited for; matrix products, arithmetic and copies ran while one was open for 0% of the time, Pallas kernels for 1%

profile of v7, /device:TPU:0, one launch (start us, length us, event | category | flops | bytes accessed | tf_op | source)
XLA Modules:
  0.0 45.2 jit_solution(4354876656368900405)
XLA Ops:
  0.0 0.9 %copy-done.1 = bf16[8,1,1,128,128]{4,3,2,1,0:T(8,128)(2,1)S(1)} copy-done((bf16[8,1,1,128,128]{4,3,2,1,0:T(8,128)(2,1)S(1)}, bf16[8,1,1,128,128]{4,3,2,1,0:T(8,128)(2,1)}, u32[]{:S(2)}) %copy-start.1) | copy-done | bytes 262168
  2.5 2.6 %collective-permute-start.3 = (bf16[528,128]{1,0:T(8,128)(2,1)S(1)}, bf16[528,128]{1,0:T(8,128)(2,1)S(1)}, u32[]{:S(2)}, u32[]{:S(2)}) collective-permute-start(bf16[528,128]{1,0:T(8,128)(2,1)S(1)} %get-tuple-element.49.refs_0_), channel_id=1, source_target_pairs={{12,8},{8,4},{4,0},{0,2},{2,6},{6,10},{10,14},{14,12},{13,9},{9,5}... | collective-permute-start | bytes 405512 | tf_op jit(solution)/shard_map/ppermute | solution.py:238
  5.2 1.9 %collective-permute-start = (bf16[528,128]{1,0:T(8,128)(2,1)S(1)}, bf16[528,128]{1,0:T(8,128)(2,1)S(1)}, u32[]{:S(2)}, u32[]{:S(2)}) collective-permute-start(bf16[528,128]{1,0:T(8,128)(2,1)S(1)} %get-tuple-element.34.refs_0_), channel_id=1, source_target_pairs={{12,8},{8,4},{4,0},{0,2},{2,6},{6,10},{10,14},{14,12},{13,9},{9,5}... | collective-permute-start | bytes 405512 | tf_op jit(solution)/shard_map/ppermute | solution.py:238
  7.2 2.2 %copy-done = bf16[1,4096,512]{2,1,0:T(8,128)(2,1)S(1)} copy-done((bf16[1,4096,512]{2,1,0:T(8,128)(2,1)S(1)}, bf16[1,4096,512]{2,1,0:T(8,128)(2,1)}, u32[]{:S(2)}) %copy-start) | copy-done | bytes 4194328
  9.7 1.8 %collective-permute-done.4.last_ref.refs_2_ = bf16[528,128]{1,0:T(8,128)(2,1)S(1)} collective-permute-done((bf16[528,128]{1,0:T(8,128)(2,1)S(1)}, bf16[528,128]{1,0:T(8,128)(2,1)S(1)}, u32[]{:S(2)}, u32[]{:S(2)}) %collective-permute-start.4) | collective-permute-done | bytes 135200 | tf_op jit(solution)/shard_map/ppermute | solution.py:238
  11.5 1.6 %collective-permute-start.5 = (bf16[528,128]{1,0:T(8,128)(2,1)S(1)}, bf16[528,128]{1,0:T(8,128)(2,1)S(1)}, u32[]{:S(2)}, u32[]{:S(2)}) collective-permute-start(bf16[528,128]{1,0:T(8,128)(2,1)S(1)} %collective-permute-done.3.first_ref.refs_1_), channel_id=1, source_target_pairs={{12,8},{8,4},{4,0},{0,2},{2,6},{6,10},{10,14},{14,12},{13,9},{9,5}... | collective-permute-start | bytes 405512 | tf_op jit(solution)/shard_map/ppermute | solution.py:238
  13.5 1.6 %collective-permute-start.2 = (bf16[528,128]{1,0:T(8,128)(2,1)S(1)}, bf16[528,128]{1,0:T(8,128)(2,1)S(1)}, u32[]{:S(2)}, u32[]{:S(2)}) collective-permute-start(bf16[528,128]{1,0:T(8,128)(2,1)S(1)} %collective-permute-done.first_ref.refs_1_), channel_id=1, source_target_pairs={{12,8},{8,4},{4,0},{0,2},{2,6},{6,10},{10,14},{14,12},{13,9},{9,5}... | collective-permute-start | bytes 405512 | tf_op jit(solution)/shard_map/ppermute | solution.py:238
  16.0 1.5 %collective-permute-done.5.refs_3_ = bf16[528,128]{1,0:T(8,128)(2,1)S(1)} collective-permute-done((bf16[528,128]{1,0:T(8,128)(2,1)S(1)}, bf16[528,128]{1,0:T(8,128)(2,1)S(1)}, u32[]{:S(2)}, u32[]{:S(2)}) %collective-permute-start.5) | collective-permute-done | bytes 135200 | tf_op jit(solution)/shard_map/ppermute | solution.py:238
  17.5 1.3 %collective-permute-done.6.refs_4_ = bf16[528,128]{1,0:T(8,128)(2,1)S(1)} collective-permute-done((bf16[528,128]{1,0:T(8,128)(2,1)S(1)}, bf16[528,128]{1,0:T(8,128)(2,1)S(1)}, u32[]{:S(2)}, u32[]{:S(2)}) %collective-permute-start.6) | collective-permute-done | bytes 135200 | tf_op jit(solution)/shard_map/ppermute | solution.py:238
  18.8 1.8 %collective-permute-start.10 = (bf16[528,128]{1,0:T(8,128)(2,1)S(1)}, bf16[528,128]{1,0:T(8,128)(2,1)S(1)}, u32[]{:S(2)}, u32[]{:S(2)}) collective-permute-start(bf16[528,128]{1,0:T(8,128)(2,1)S(1)} %shard_map.40), channel_id=1, source_target_pairs={{10,8},{6,4},{4,6},{8,10},{0,12},{12,0},{14,2},{2,14},{11,9},{7,5}... | collective-permute-start | bytes 405512 | tf_op jit(solution)/shard_map/ppermute | solution.py:235
  20.6 1.6 %collective-permute-start.8 = (bf16[528,128]{1,0:T(8,128)(2,1)S(1)}, bf16[528,128]{1,0:T(8,128)(2,1)S(1)}, u32[]{:S(2)}, u32[]{:S(2)}) collective-permute-start(bf16[528,128]{1,0:T(8,128)(2,1)S(1)} %collective-permute-done.5.refs_3_), channel_id=1, source_target_pairs={{12,8},{8,4},{4,0},{0,2},{2,6},{6,10},{10,14},{14,12},{13,9},{9,5}... | collective-permute-start | bytes 405512 | tf_op jit(solution)/shard_map/ppermute | solution.py:238
  22.6 3.2 %collective-permute-done.10.refs_7_ = bf16[528,128]{1,0:T(8,128)(2,1)S(1)} collective-permute-done((bf16[528,128]{1,0:T(8,128)(2,1)S(1)}, bf16[528,128]{1,0:T(8,128)(2,1)S(1)}, u32[]{:S(2)}, u32[]{:S(2)}) %collective-permute-start.10) | collective-permute-done | bytes 135200 | tf_op jit(solution)/shard_map/ppermute | solution.py:235
  25.8 1.3 %collective-permute-done.8.refs_5_ = bf16[528,128]{1,0:T(8,128)(2,1)S(1)} collective-permute-done((bf16[528,128]{1,0:T(8,128)(2,1)S(1)}, bf16[528,128]{1,0:T(8,128)(2,1)S(1)}, u32[]{:S(2)}, u32[]{:S(2)}) %collective-permute-start.8) | collective-permute-done | bytes 135200 | tf_op jit(solution)/shard_map/ppermute | solution.py:238
  27.2 1.3 %shard_map.42 = bf16[528,512]{1,0:T(8,128)(2,1)S(1)} custom-call(bf16[528,128]{1,0:T(8,128)(2,1)S(1)} %get-tuple-element.49.refs_0_, bf16[528,128]{1,0:T(8,128)(2,1)S(1)} %collective-permute-done.3.first_ref.refs_1_, bf16[528,128]{1,0:T(8,128)(2,1)S(1)} %collective-permute-done.4.last_ref.refs_2_, bf16[528,128]{1,0:T(8,128)(2,1)S(1)} %collective-permute-done.5.refs_3_, ...), custom_call_target="tpu_custom_call" | custom-call | tf_op jit(solution)/shard_map/pallas_call | solution.py:184
  28.5 1.6 %collective-permute-start.15 = (bf16[528,512]{1,0:T(8,128)(2,1)S(1)}, bf16[528,512]{1,0:T(8,128)(2,1)S(1)}, u32[]{:S(2)}, u32[]{:S(2)}) collective-permute-start(bf16[528,512]{1,0:T(8,128)(2,1)S(1)} %shard_map.42), channel_id=1, source_target_pairs={{0,1},{1,0},{2,3},{3,2},{4,5},{5,4},{6,7},{7,6},{8,9},{9,8},{10,11... | collective-permute-start | bytes 1622024 | tf_op jit(solution)/shard_map/ppermute | solution.py:229
  30.1 1.7 %collective-permute-start.14 = (bf16[528,128]{1,0:T(8,128)(2,1)S(1)}, bf16[528,128]{1,0:T(8,128)(2,1)S(1)}, u32[]{:S(2)}, u32[]{:S(2)}) collective-permute-start(bf16[528,128]{1,0:T(8,128)(2,1)S(1)} %shard_map.41), channel_id=1, source_target_pairs={{10,8},{6,4},{4,6},{8,10},{0,12},{12,0},{14,2},{2,14},{11,9},{7,5}... | collective-permute-start | bytes 405512 | tf_op jit(solution)/shard_map/ppermute | solution.py:235
  31.7 1.7 %collective-permute-start.12 = (bf16[528,128]{1,0:T(8,128)(2,1)S(1)}, bf16[528,128]{1,0:T(8,128)(2,1)S(1)}, u32[]{:S(2)}, u32[]{:S(2)}) collective-permute-start(bf16[528,128]{1,0:T(8,128)(2,1)S(1)} %collective-permute-done.2.refs_3_), channel_id=1, source_target_pairs={{12,8},{8,4},{4,0},{0,2},{2,6},{6,10},{10,14},{14,12},{13,9},{9,5}... | collective-permute-start | bytes 405512 | tf_op jit(solution)/shard_map/ppermute | solution.py:238
  33.7 3.3 %collective-permute-done.14.refs_7_ = bf16[528,128]{1,0:T(8,128)(2,1)S(1)} collective-permute-done((bf16[528,128]{1,0:T(8,128)(2,1)S(1)}, bf16[528,128]{1,0:T(8,128)(2,1)S(1)}, u32[]{:S(2)}, u32[]{:S(2)}) %collective-permute-start.14) | collective-permute-done | bytes 135200 | tf_op jit(solution)/shard_map/ppermute | solution.py:235
  37.0 1.2 %collective-permute-done.12.refs_5_ = bf16[528,128]{1,0:T(8,128)(2,1)S(1)} collective-permute-done((bf16[528,128]{1,0:T(8,128)(2,1)S(1)}, bf16[528,128]{1,0:T(8,128)(2,1)S(1)}, u32[]{:S(2)}, u32[]{:S(2)}) %collective-permute-start.12) | collective-permute-done | bytes 135200 | tf_op jit(solution)/shard_map/ppermute | solution.py:238
  38.4 1.2 %shard_map.43 = (f32[512,512]{1,0:T(8,128)S(1)}, f32[1,512]{1,0:T(1,128)S(1)}) custom-call(bf16[528,128]{1,0:T(8,128)(2,1)S(1)} %get-tuple-element.34.refs_0_, bf16[528,128]{1,0:T(8,128)(2,1)S(1)} %collective-permute-done.first_ref.refs_1_, bf16[528,128]{1,0:T(8,128)(2,1)S(1)} %collective-permute-done.1.last_ref.refs_2_, ...), custom_call_target="tpu_custom_call" | custom-call | tf_op jit(solution)/shard_map/pallas_call | solution.py:245
  39.7 1.4 %collective-permute-start.17 = (f32[1,512]{1,0:T(1,128)S(1)}, f32[1,512]{1,0:T(1,128)S(1)}, u32[]{:S(2)}, u32[]{:S(2)}) collective-permute-start(f32[1,512]{1,0:T(1,128)S(1)} %get-tuple-element.54), channel_id=1, source_target_pairs={{0,1},{1,0},{2,3},{3,2},{4,5},{5,4},{6,7},{7,6},{8,9},{9,8},{10,11... | collective-permute-start | bytes 6152 | tf_op jit(solution)/shard_map/ppermute | solution.py:256
  41.5 1.8 %collective-permute-done.17 = f32[1,512]{1,0:T(1,128)S(1)} collective-permute-done((f32[1,512]{1,0:T(1,128)S(1)}, f32[1,512]{1,0:T(1,128)S(1)}, u32[]{:S(2)}, u32[]{:S(2)}) %collective-permute-start.17) | collective-permute-done | bytes 2080 | tf_op jit(solution)/shard_map/ppermute | solution.py:256
  43.3 0.8 %collective-permute-done.18 = f32[1,512]{1,0:T(1,128)S(1)} collective-permute-done((f32[1,512]{1,0:T(1,128)S(1)}, f32[1,512]{1,0:T(1,128)S(1)}, u32[]{:S(2)}, u32[]{:S(2)}) %collective-permute-start.18) | collective-permute-done | bytes 2080 | tf_op jit(solution)/shard_map/ppermute | solution.py:256
  44.1 1.1 %broadcast_multiply_fusion = f32[512,512]{1,0:T(8,128)} fusion(f32[512,512]{1,0:T(8,128)S(1)} %get-tuple-element.53, f32[512]{0:T(512)S(1)} %bitcast.8), kind=kLoop, calls=%fused_computation | loop fusion | flops 262144 | bytes 2099200 | tf_op jit(solution)/shard_map/mul | solution.py:258
  (29 shorter events, 5.1 us)
Async XLA Ops:
  0.0 0.9 %copy-start.1 = (bf16[8,1,1,128,128]{4,3,2,1,0:T(8,128)(2,1)S(1)}, bf16[8,1,1,128,128]{4,3,2,1,0:T(8,128)(2,1)}, u32[]{:S(2)}) copy-start(bf16[8,1,1,128,128]{4,3,2,1,0:T(8,128)(2,1)} %param.4) | copy-start | bytes 786436
  1.0 0.7 %copy-start.2 = (s32[8,1,1]{0,2,1:T(1,128)S(1)}, s32[8,1,1]{0,2,1:T(1,128)}, u32[]{:S(2)}) copy-start(s32[8,1,1]{0,2,1:T(1,128)} %param.3) | copy-start | bytes 100
  1.9 13.8 %collective-permute-start.7 = (bf16[4096,512]{1,0:T(8,128)(2,1)}, bf16[4096,512]{1,0:T(8,128)(2,1)S(1)}, u32[]{:S(2)}, u32[]{:S(2)}) collective-permute-start(bf16[4096,512]{1,0:T(8,128)(2,1)} %bitcast.4), channel_id=1, source_target_pairs={{0,16},{16,0},{1,17},{17,1},{2,18},{18,2},{3,19},{19,3},{4,20},{20... | collective-permute-start | bytes 12582920 | tf_op jit(solution)/shard_map/ppermute | solution.py:223
  2.5 7.2 %collective-permute-start.3 = (bf16[528,128]{1,0:T(8,128)(2,1)S(1)}, bf16[528,128]{1,0:T(8,128)(2,1)S(1)}, u32[]{:S(2)}, u32[]{:S(2)}) collective-permute-start(bf16[528,128]{1,0:T(8,128)(2,1)S(1)} %get-tuple-element.49.refs_0_), channel_id=1, source_target_pairs={{12,8},{8,4},{4,0},{0,2},{2,6},{6,10},{10,14},{14,12},{13,9},{9,5}... | collective-permute-start | bytes 405512 | tf_op jit(solution)/shard_map/ppermute | solution.py:238
  5.0 6.4 %collective-permute-start.4 = (bf16[528,128]{1,0:T(8,128)(2,1)S(1)}, bf16[528,128]{1,0:T(8,128)(2,1)S(1)}, u32[]{:S(2)}, u32[]{:S(2)}) collective-permute-start(bf16[528,128]{1,0:T(8,128)(2,1)S(1)} %get-tuple-element.49.refs_0_), channel_id=1, source_target_pairs={{12,14},{8,12},{4,8},{0,4},{2,0},{6,2},{10,6},{14,10},{13,15},{9,1... | collective-permute-start | bytes 405512 | tf_op jit(solution)/shard_map/ppermute | solution.py:238
  5.2 8.3 %collective-permute-start = (bf16[528,128]{1,0:T(8,128)(2,1)S(1)}, bf16[528,128]{1,0:T(8,128)(2,1)S(1)}, u32[]{:S(2)}, u32[]{:S(2)}) collective-permute-start(bf16[528,128]{1,0:T(8,128)(2,1)S(1)} %get-tuple-element.34.refs_0_), channel_id=1, source_target_pairs={{12,8},{8,4},{4,0},{0,2},{2,6},{6,10},{10,14},{14,12},{13,9},{9,5}... | collective-permute-start | bytes 405512 | tf_op jit(solution)/shard_map/ppermute | solution.py:238
  7.1 8.1 %collective-permute-start.1 = (bf16[528,128]{1,0:T(8,128)(2,1)S(1)}, bf16[528,128]{1,0:T(8,128)(2,1)S(1)}, u32[]{:S(2)}, u32[]{:S(2)}) collective-permute-start(bf16[528,128]{1,0:T(8,128)(2,1)S(1)} %get-tuple-element.34.refs_0_), channel_id=1, source_target_pairs={{12,14},{8,12},{4,8},{0,4},{2,0},{6,2},{10,6},{14,10},{13,15},{9,1... | collective-permute-start | bytes 405512 | tf_op jit(solution)/shard_map/ppermute | solution.py:238
  7.2 2.2 %copy-start = (bf16[1,4096,512]{2,1,0:T(8,128)(2,1)S(1)}, bf16[1,4096,512]{2,1,0:T(8,128)(2,1)}, u32[]{:S(2)}) copy-start(bf16[1,4096,512]{2,1,0:T(8,128)(2,1)} %param.5) | copy-start | bytes 12582916
  11.5 6.1 %collective-permute-start.5 = (bf16[528,128]{1,0:T(8,128)(2,1)S(1)}, bf16[528,128]{1,0:T(8,128)(2,1)S(1)}, u32[]{:S(2)}, u32[]{:S(2)}) collective-permute-start(bf16[528,128]{1,0:T(8,128)(2,1)S(1)} %collective-permute-done.3.first_ref.refs_1_), channel_id=1, source_target_pairs={{12,8},{8,4},{4,0},{0,2},{2,6},{6,10},{10,14},{14,12},{13,9},{9,5}... | collective-permute-start | bytes 405512 | tf_op jit(solution)/shard_map/ppermute | solution.py:238
  13.1 5.8 %collective-permute-start.6 = (bf16[528,128]{1,0:T(8,128)(2,1)S(1)}, bf16[528,128]{1,0:T(8,128)(2,1)S(1)}, u32[]{:S(2)}, u32[]{:S(2)}) collective-permute-start(bf16[528,128]{1,0:T(8,128)(2,1)S(1)} %collective-permute-done.4.last_ref.refs_2_), channel_id=1, source_target_pairs={{12,14},{8,12},{4,8},{0,4},{2,0},{6,2},{10,6},{14,10},{13,15},{9,1... | collective-permute-start | bytes 405512 | tf_op jit(solution)/shard_map/ppermute | solution.py:238
  13.5 9.1 %collective-permute-start.2 = (bf16[528,128]{1,0:T(8,128)(2,1)S(1)}, bf16[528,128]{1,0:T(8,128)(2,1)S(1)}, u32[]{:S(2)}, u32[]{:S(2)}) collective-permute-start(bf16[528,128]{1,0:T(8,128)(2,1)S(1)} %collective-permute-done.first_ref.refs_1_), channel_id=1, source_target_pairs={{12,8},{8,4},{4,0},{0,2},{2,6},{6,10},{10,14},{14,12},{13,9},{9,5}... | collective-permute-start | bytes 405512 | tf_op jit(solution)/shard_map/ppermute | solution.py:238
  15.2 7.4 %collective-permute-start.11 = (bf16[528,128]{1,0:T(8,128)(2,1)S(1)}, bf16[528,128]{1,0:T(8,128)(2,1)S(1)}, u32[]{:S(2)}, u32[]{:S(2)}) collective-permute-start(bf16[528,128]{1,0:T(8,128)(2,1)S(1)} %collective-permute-done.1.last_ref.refs_2_), channel_id=1, source_target_pairs={{12,14},{8,12},{4,8},{0,4},{2,0},{6,2},{10,6},{14,10},{13,15},{9,1... | collective-permute-start | bytes 405512 | tf_op jit(solution)/shard_map/ppermute | solution.py:238
  18.8 7.0 %collective-permute-start.10 = (bf16[528,128]{1,0:T(8,128)(2,1)S(1)}, bf16[528,128]{1,0:T(8,128)(2,1)S(1)}, u32[]{:S(2)}, u32[]{:S(2)}) collective-permute-start(bf16[528,128]{1,0:T(8,128)(2,1)S(1)} %shard_map.40), channel_id=1, source_target_pairs={{10,8},{6,4},{4,6},{8,10},{0,12},{12,0},{14,2},{2,14},{11,9},{7,5}... | collective-permute-start | bytes 405512 | tf_op jit(solution)/shard_map/ppermute | solution.py:235
  20.6 6.5 %collective-permute-start.8 = (bf16[528,128]{1,0:T(8,128)(2,1)S(1)}, bf16[528,128]{1,0:T(8,128)(2,1)S(1)}, u32[]{:S(2)}, u32[]{:S(2)}) collective-permute-start(bf16[528,128]{1,0:T(8,128)(2,1)S(1)} %collective-permute-done.5.refs_3_), channel_id=1, source_target_pairs={{12,8},{8,4},{4,0},{0,2},{2,6},{6,10},{10,14},{14,12},{13,9},{9,5}... | collective-permute-start | bytes 405512 | tf_op jit(solution)/shard_map/ppermute | solution.py:238
  22.2 5.0 %collective-permute-start.9 = (bf16[528,128]{1,0:T(8,128)(2,1)S(1)}, bf16[528,128]{1,0:T(8,128)(2,1)S(1)}, u32[]{:S(2)}, u32[]{:S(2)}) collective-permute-start(bf16[528,128]{1,0:T(8,128)(2,1)S(1)} %collective-permute-done.6.refs_4_), channel_id=1, source_target_pairs={{12,14},{8,12},{4,8},{0,4},{2,0},{6,2},{10,6},{14,10},{13,15},{9,1... | collective-permute-start | bytes 405512 | tf_op jit(solution)/shard_map/ppermute | solution.py:238
  28.5 9.9 %collective-permute-start.15 = (bf16[528,512]{1,0:T(8,128)(2,1)S(1)}, bf16[528,512]{1,0:T(8,128)(2,1)S(1)}, u32[]{:S(2)}, u32[]{:S(2)}) collective-permute-start(bf16[528,512]{1,0:T(8,128)(2,1)S(1)} %shard_map.42), channel_id=1, source_target_pairs={{0,1},{1,0},{2,3},{3,2},{4,5},{5,4},{6,7},{7,6},{8,9},{9,8},{10,11... | collective-permute-start | bytes 1622024 | tf_op jit(solution)/shard_map/ppermute | solution.py:229
  30.1 7.0 %collective-permute-start.14 = (bf16[528,128]{1,0:T(8,128)(2,1)S(1)}, bf16[528,128]{1,0:T(8,128)(2,1)S(1)}, u32[]{:S(2)}, u32[]{:S(2)}) collective-permute-start(bf16[528,128]{1,0:T(8,128)(2,1)S(1)} %shard_map.41), channel_id=1, source_target_pairs={{10,8},{6,4},{4,6},{8,10},{0,12},{12,0},{14,2},{2,14},{11,9},{7,5}... | collective-permute-start | bytes 405512 | tf_op jit(solution)/shard_map/ppermute | solution.py:235
  31.7 6.5 %collective-permute-start.12 = (bf16[528,128]{1,0:T(8,128)(2,1)S(1)}, bf16[528,128]{1,0:T(8,128)(2,1)S(1)}, u32[]{:S(2)}, u32[]{:S(2)}) collective-permute-start(bf16[528,128]{1,0:T(8,128)(2,1)S(1)} %collective-permute-done.2.refs_3_), channel_id=1, source_target_pairs={{12,8},{8,4},{4,0},{0,2},{2,6},{6,10},{10,14},{14,12},{13,9},{9,5}... | collective-permute-start | bytes 405512 | tf_op jit(solution)/shard_map/ppermute | solution.py:238
  33.4 5.0 %collective-permute-start.13 = (bf16[528,128]{1,0:T(8,128)(2,1)S(1)}, bf16[528,128]{1,0:T(8,128)(2,1)S(1)}, u32[]{:S(2)}, u32[]{:S(2)}) collective-permute-start(bf16[528,128]{1,0:T(8,128)(2,1)S(1)} %collective-permute-done.11.refs_4_), channel_id=1, source_target_pairs={{12,14},{8,12},{4,8},{0,4},{2,0},{6,2},{10,6},{14,10},{13,15},{9,1... | collective-permute-start | bytes 405512 | tf_op jit(solution)/shard_map/ppermute | solution.py:238
  39.6 1.9 %collective-permute-start.16 = (f32[1,512]{1,0:T(1,128)S(1)}, f32[1,512]{1,0:T(1,128)S(1)}, u32[]{:S(2)}, u32[]{:S(2)}) collective-permute-start(f32[1,512]{1,0:T(1,128)S(1)} %get-tuple-element.54), channel_id=1, source_target_pairs={{0,16},{16,0},{1,17},{17,1},{2,18},{18,2},{3,19},{19,3},{4,20},{20... | collective-permute-start | bytes 6152 | tf_op jit(solution)/shard_map/ppermute | solution.py:256
  39.7 3.7 %collective-permute-start.17 = (f32[1,512]{1,0:T(1,128)S(1)}, f32[1,512]{1,0:T(1,128)S(1)}, u32[]{:S(2)}, u32[]{:S(2)}) collective-permute-start(f32[1,512]{1,0:T(1,128)S(1)} %get-tuple-element.54), channel_id=1, source_target_pairs={{0,1},{1,0},{2,3},{3,2},{4,5},{5,4},{6,7},{7,6},{8,9},{9,8},{10,11... | collective-permute-start | bytes 6152 | tf_op jit(solution)/shard_map/ppermute | solution.py:256
  41.1 3.0 %collective-permute-start.18 = (f32[1,512]{1,0:T(1,128)S(1)}, f32[1,512]{1,0:T(1,128)S(1)}, u32[]{:S(2)}, u32[]{:S(2)}) collective-permute-start(f32[1,512]{1,0:T(1,128)S(1)} %get-tuple-element.54), channel_id=1, source_target_pairs={{0,17},{1,16},{16,1},{17,0},{2,19},{3,18},{18,3},{19,2},{4,21},{5,... | collective-permute-start | bytes 6152 | tf_op jit(solution)/shard_map/ppermute | solution.py:256

commit v8 on v7

--- a/solution.py
+++ b/solution.py
@@ -11,6 +11,7 @@
 CODE_MID = 125.0
 LOG2E = 1.4426950408889634
 ID_ROWS = 16
+LATE = 3
 VMEM_BYTES = 24 * 1024 * 1024
 PLAN = ("S=K=T", "O", "S1", "K1", "S=W", "Sp", "Kp", "S2", "K2", "J", "S=W=Sp=Kp", "S3", "Sm", "S=K", "C", "X", "K3", "Km")
 
@@ -87,13 +88,24 @@
         )
 
 
-def send_kernel(slots, *refs):
-    items, (window, code_ref, total) = refs[:slots], refs[slots:]
-    block = items[0].shape[1]
-    rows = total.shape[0]
+def early_kernel(slots, kept, *refs):
+    items, (window, total) = refs[:slots], refs[slots:]
+    block = items[0].shape[1]
+    layer = lax.axis_index("layer")
 
     def finish(j, value):
         total[j * block : (j + 1) * block, :] = value
+
+    products(layer if kept else 1 - layer, items, window, finish)
+
+
+def send_kernel(slots, *refs):
+    items, (window, early, code_ref, total) = refs[:slots], refs[slots:]
+    block = items[0].shape[1]
+    rows = total.shape[0]
+
+    def finish(j, value):
+        total[j * block : (j + 1) * block, :] = value + early[j * block : (j + 1) * block, :]
 
     products(1 - lax.axis_index("layer"), items, window, finish)
     most = jnp.max(jnp.abs(total[...]), axis=0, keepdims=True)
@@ -178,17 +190,25 @@
                 cost_estimate=pl.CostEstimate(flops=0, bytes_accessed=2 * half * columns * 2, transcendentals=0),
             )(part, *given)
 
-        item_specs = [vmem] * size
+        def started(items, window, kept):
+            return pl.pallas_call(
+                functools.partial(early_kernel, len(items), kept),
+                out_shape=jax.ShapeDtypeStruct((rows, columns), jnp.float32),
+                in_specs=[vmem] * (len(items) + 1),
+                out_specs=vmem,
+                compiler_params=params,
+            )(*items, window)
+
 
         def coded(sends, window):
             return pl.pallas_call(
-                functools.partial(send_kernel, size),
+                functools.partial(send_kernel, LATE),
                 out_shape=jax.ShapeDtypeStruct((rows + ID_ROWS, columns), jnp.bfloat16),
-                in_specs=item_specs + [vmem],
+                in_specs=[vmem] * (LATE + 2),
                 out_specs=vmem,
                 scratch_shapes=[pltpu.VMEM((rows, columns), jnp.float32)],
                 compiler_params=params,
-            )(*sends, window)
+            )(*sends[-LATE:], window, started(sends[:-LATE], window, False))
 
         window = place(True, own)
         if size == 8:
@@ -248,7 +268,7 @@
                 jax.ShapeDtypeStruct((rows, columns), jnp.float32),
                 jax.ShapeDtypeStruct((1, columns), jnp.float32),
             ),
-            in_specs=item_specs + [vmem, vmem],
+            in_specs=[vmem] * (size + 2),
             out_specs=(vmem, vmem),
             compiler_params=params,
         )(*keeps, window, code)

time: 45.4 us -> 45.1 us (level)
  waiting for transfers between devices: 16.4 us -> 15.6 us
    ppermute x2, waiting for transfers between devices: 6.43 us -> 5.65 us  [body(): lists[name[0]].append(lax.ppermute(chosen[name[0]], 'col', across))]
    pallas_call x1 -> x2, Pallas kernels: 1.32 us -> 1.76 us  [the longest x1 1 us: coded(): pl.pallas_call(functools.partial(send_kernel, LATE), out_shape=jax.ShapeD...]
  transfers between devices with their start and end apart: 19 -> 19, of which waited for: 11 -> 11; matrix products, arithmetic and copies ran while one was open for 0% -> 0% of each run, Pallas kernels for 1% -> 3%
where the time goes in v8:
time: 45.1 us; the launch traced here: 44.9 us
  starting transfers between devices  20.4 us (45%)
  waiting for transfers between devices  15.6 us (35%)
  Pallas kernels  3.84 us (9%)
  local copies, waits for them, and re-layouts  3.79 us (8%)
  other arithmetic  1.11 us (2%)
    ppermute x12, starting transfers between devices, body(): lax.ppermute(e, 'col', shift(w))  13 us
    ppermute x12, waiting for transfers between devices, body(): lax.ppermute(e, 'col', shift(w))  7.39 us
    ppermute x2, waiting for transfers between devices, body(): lists[name[0]].append(lax.ppermute(chosen[name[0]], 'col', across))  5.65 us
    unnamed x6, local copies, waits for them, and re-layouts  3.79 us
    ppermute x2, starting transfers between devices, body(): lists[name[0]].append(lax.ppermute(chosen[name[0]], 'col', across))  3.44 us
    ppermute x1, waiting for transfers between devices, body(): lax.ppermute(sums, 'layer', swap)  1.78 us
    ppermute x1, starting transfers between devices, body(): code = lax.ppermute(code, 'layer', swap)  1.55 us
    ppermute x1, starting transfers between devices, body(): lax.ppermute(sums, 'layer', swap)  1.39 us
  transfers between devices with their start and end apart: 19, of which 11 were waited for; matrix products, arithmetic and copies ran while one was open for 0% of the time, Pallas kernels for 3%

profile of v8, /device:TPU:0, one launch (start us, length us, event | category | flops | bytes accessed | tf_op | source)
XLA Modules:
  0.0 44.9 jit_solution(8357051296052303851)
XLA Ops:
  0.0 0.9 %copy-done.1 = bf16[8,1,1,128,128]{4,3,2,1,0:T(8,128)(2,1)S(1)} copy-done((bf16[8,1,1,128,128]{4,3,2,1,0:T(8,128)(2,1)S(1)}, bf16[8,1,1,128,128]{4,3,2,1,0:T(8,128)(2,1)}, u32[]{:S(2)}) %copy-start.1) | copy-done | bytes 262168
  2.5 2.6 %collective-permute-start.3 = (bf16[528,128]{1,0:T(8,128)(2,1)S(1)}, bf16[528,128]{1,0:T(8,128)(2,1)S(1)}, u32[]{:S(2)}, u32[]{:S(2)}) collective-permute-start(bf16[528,128]{1,0:T(8,128)(2,1)S(1)} %get-tuple-element.50.refs_0_), channel_id=1, source_target_pairs={{12,8},{8,4},{4,0},{0,2},{2,6},{6,10},{10,14},{14,12},{13,9},{9,5}... | collective-permute-start | bytes 405512 | tf_op jit(solution)/shard_map/ppermute | solution.py:258
  5.2 1.9 %collective-permute-start = (bf16[528,128]{1,0:T(8,128)(2,1)S(1)}, bf16[528,128]{1,0:T(8,128)(2,1)S(1)}, u32[]{:S(2)}, u32[]{:S(2)}) collective-permute-start(bf16[528,128]{1,0:T(8,128)(2,1)S(1)} %get-tuple-element.34.refs_0_), channel_id=1, source_target_pairs={{12,8},{8,4},{4,0},{0,2},{2,6},{6,10},{10,14},{14,12},{13,9},{9,5}... | collective-permute-start | bytes 405512 | tf_op jit(solution)/shard_map/ppermute | solution.py:258
  7.2 2.2 %copy-done = bf16[1,4096,512]{2,1,0:T(8,128)(2,1)S(1)} copy-done((bf16[1,4096,512]{2,1,0:T(8,128)(2,1)S(1)}, bf16[1,4096,512]{2,1,0:T(8,128)(2,1)}, u32[]{:S(2)}) %copy-start) | copy-done | bytes 4194328
  9.7 1.8 %collective-permute-done.4.last_ref.refs_2_ = bf16[528,128]{1,0:T(8,128)(2,1)S(1)} collective-permute-done((bf16[528,128]{1,0:T(8,128)(2,1)S(1)}, bf16[528,128]{1,0:T(8,128)(2,1)S(1)}, u32[]{:S(2)}, u32[]{:S(2)}) %collective-permute-start.4) | collective-permute-done | bytes 135200 | tf_op jit(solution)/shard_map/ppermute | solution.py:258
  11.5 1.6 %collective-permute-start.5 = (bf16[528,128]{1,0:T(8,128)(2,1)S(1)}, bf16[528,128]{1,0:T(8,128)(2,1)S(1)}, u32[]{:S(2)}, u32[]{:S(2)}) collective-permute-start(bf16[528,128]{1,0:T(8,128)(2,1)S(1)} %collective-permute-done.3.first_ref.refs_1_), channel_id=1, source_target_pairs={{12,8},{8,4},{4,0},{0,2},{2,6},{6,10},{10,14},{14,12},{13,9},{9,5}... | collective-permute-start | bytes 405512 | tf_op jit(solution)/shard_map/ppermute | solution.py:258
  13.5 1.6 %collective-permute-start.2 = (bf16[528,128]{1,0:T(8,128)(2,1)S(1)}, bf16[528,128]{1,0:T(8,128)(2,1)S(1)}, u32[]{:S(2)}, u32[]{:S(2)}) collective-permute-start(bf16[528,128]{1,0:T(8,128)(2,1)S(1)} %collective-permute-done.first_ref.refs_1_), channel_id=1, source_target_pairs={{12,8},{8,4},{4,0},{0,2},{2,6},{6,10},{10,14},{14,12},{13,9},{9,5}... | collective-permute-start | bytes 405512 | tf_op jit(solution)/shard_map/ppermute | solution.py:258
  16.0 1.5 %collective-permute-done.5.refs_3_ = bf16[528,128]{1,0:T(8,128)(2,1)S(1)} collective-permute-done((bf16[528,128]{1,0:T(8,128)(2,1)S(1)}, bf16[528,128]{1,0:T(8,128)(2,1)S(1)}, u32[]{:S(2)}, u32[]{:S(2)}) %collective-permute-start.5) | collective-permute-done | bytes 135200 | tf_op jit(solution)/shard_map/ppermute | solution.py:258
  17.5 1.3 %collective-permute-done.6.refs_4_ = bf16[528,128]{1,0:T(8,128)(2,1)S(1)} collective-permute-done((bf16[528,128]{1,0:T(8,128)(2,1)S(1)}, bf16[528,128]{1,0:T(8,128)(2,1)S(1)}, u32[]{:S(2)}, u32[]{:S(2)}) %collective-permute-start.6) | collective-permute-done | bytes 135200 | tf_op jit(solution)/shard_map/ppermute | solution.py:258
  18.8 1.8 %collective-permute-start.10 = (bf16[528,128]{1,0:T(8,128)(2,1)S(1)}, bf16[528,128]{1,0:T(8,128)(2,1)S(1)}, u32[]{:S(2)}, u32[]{:S(2)}) collective-permute-start(bf16[528,128]{1,0:T(8,128)(2,1)S(1)} %shard_map.40), channel_id=1, source_target_pairs={{10,8},{6,4},{4,6},{8,10},{0,12},{12,0},{14,2},{2,14},{11,9},{7,5}... | collective-permute-start | bytes 405512 | tf_op jit(solution)/shard_map/ppermute | solution.py:255
  20.6 1.6 %collective-permute-start.8 = (bf16[528,128]{1,0:T(8,128)(2,1)S(1)}, bf16[528,128]{1,0:T(8,128)(2,1)S(1)}, u32[]{:S(2)}, u32[]{:S(2)}) collective-permute-start(bf16[528,128]{1,0:T(8,128)(2,1)S(1)} %collective-permute-done.5.refs_3_), channel_id=1, source_target_pairs={{12,8},{8,4},{4,0},{0,2},{2,6},{6,10},{10,14},{14,12},{13,9},{9,5}... | collective-permute-start | bytes 405512 | tf_op jit(solution)/shard_map/ppermute | solution.py:258
  22.6 0.8 %shard_map.42.refs_4_ = f32[512,512]{1,0:T(8,128)S(1)} custom-call(bf16[528,128]{1,0:T(8,128)(2,1)S(1)} %get-tuple-element.50.refs_0_, bf16[528,128]{1,0:T(8,128)(2,1)S(1)} %collective-permute-done.3.first_ref.refs_1_, bf16[528,128]{1,0:T(8,128)(2,1)S(1)} %collective-permute-done.4.last_ref.refs_2_, bf16[528,128]{1,0:T(8,128)(2,1)S(1)} %collective-permute-done.5.refs_3_, ...), custom_call_target="tpu_custom_call" | custom-call | tf_op jit(solution)/shard_map/pallas_call | solution.py:194
  23.4 2.4 %collective-permute-done.10.refs_2_ = bf16[528,128]{1,0:T(8,128)(2,1)S(1)} collective-permute-done((bf16[528,128]{1,0:T(8,128)(2,1)S(1)}, bf16[528,128]{1,0:T(8,128)(2,1)S(1)}, u32[]{:S(2)}, u32[]{:S(2)}) %collective-permute-start.10) | collective-permute-done | bytes 135200 | tf_op jit(solution)/shard_map/ppermute | solution.py:255
  25.8 1.3 %collective-permute-done.8.refs_0_ = bf16[528,128]{1,0:T(8,128)(2,1)S(1)} collective-permute-done((bf16[528,128]{1,0:T(8,128)(2,1)S(1)}, bf16[528,128]{1,0:T(8,128)(2,1)S(1)}, u32[]{:S(2)}, u32[]{:S(2)}) %collective-permute-start.8) | collective-permute-done | bytes 135200 | tf_op jit(solution)/shard_map/ppermute | solution.py:258
  27.2 1.0 %shard_map.43 = bf16[528,512]{1,0:T(8,128)(2,1)S(1)} custom-call(bf16[528,128]{1,0:T(8,128)(2,1)S(1)} %collective-permute-done.8.refs_0_, bf16[528,128]{1,0:T(8,128)(2,1)S(1)} %collective-permute-done.9.refs_1_, bf16[528,128]{1,0:T(8,128)(2,1)S(1)} %collective-permute-done.10.refs_2_, bf16[8192,512]{1,0:T(8,128)(2,1)S(1)} %shard_map.39.refs_5_.refs_3_.refs_8_, ...), custom_call_target="tpu_custom_call" | custom-call | tf_op jit(solution)/shard_map/pallas_call | solution.py:204
  28.2 1.6 %collective-permute-start.15 = (bf16[528,512]{1,0:T(8,128)(2,1)S(1)}, bf16[528,512]{1,0:T(8,128)(2,1)S(1)}, u32[]{:S(2)}, u32[]{:S(2)}) collective-permute-start(bf16[528,512]{1,0:T(8,128)(2,1)S(1)} %shard_map.43), channel_id=1, source_target_pairs={{0,1},{1,0},{2,3},{3,2},{4,5},{5,4},{6,7},{7,6},{8,9},{9,8},{10,11... | collective-permute-start | bytes 1622024 | tf_op jit(solution)/shard_map/ppermute | solution.py:249
  29.7 1.7 %collective-permute-start.14 = (bf16[528,128]{1,0:T(8,128)(2,1)S(1)}, bf16[528,128]{1,0:T(8,128)(2,1)S(1)}, u32[]{:S(2)}, u32[]{:S(2)}) collective-permute-start(bf16[528,128]{1,0:T(8,128)(2,1)S(1)} %shard_map.41), channel_id=1, source_target_pairs={{10,8},{6,4},{4,6},{8,10},{0,12},{12,0},{14,2},{2,14},{11,9},{7,5}... | collective-permute-start | bytes 405512 | tf_op jit(solution)/shard_map/ppermute | solution.py:255
  31.4 1.7 %collective-permute-start.12 = (bf16[528,128]{1,0:T(8,128)(2,1)S(1)}, bf16[528,128]{1,0:T(8,128)(2,1)S(1)}, u32[]{:S(2)}, u32[]{:S(2)}) collective-permute-start(bf16[528,128]{1,0:T(8,128)(2,1)S(1)} %collective-permute-done.2.refs_3_), channel_id=1, source_target_pairs={{12,8},{8,4},{4,0},{0,2},{2,6},{6,10},{10,14},{14,12},{13,9},{9,5}... | collective-permute-start | bytes 405512 | tf_op jit(solution)/shard_map/ppermute | solution.py:258
  33.4 3.3 %collective-permute-done.14.refs_7_ = bf16[528,128]{1,0:T(8,128)(2,1)S(1)} collective-permute-done((bf16[528,128]{1,0:T(8,128)(2,1)S(1)}, bf16[528,128]{1,0:T(8,128)(2,1)S(1)}, u32[]{:S(2)}, u32[]{:S(2)}) %collective-permute-start.14) | collective-permute-done | bytes 135200 | tf_op jit(solution)/shard_map/ppermute | solution.py:255
  36.7 1.2 %collective-permute-done.12.refs_5_ = bf16[528,128]{1,0:T(8,128)(2,1)S(1)} collective-permute-done((bf16[528,128]{1,0:T(8,128)(2,1)S(1)}, bf16[528,128]{1,0:T(8,128)(2,1)S(1)}, u32[]{:S(2)}, u32[]{:S(2)}) %collective-permute-start.12) | collective-permute-done | bytes 135200 | tf_op jit(solution)/shard_map/ppermute | solution.py:258
  38.1 1.2 %shard_map.44 = (f32[512,512]{1,0:T(8,128)S(1)}, f32[1,512]{1,0:T(1,128)S(1)}) custom-call(bf16[528,128]{1,0:T(8,128)(2,1)S(1)} %get-tuple-element.34.refs_0_, bf16[528,128]{1,0:T(8,128)(2,1)S(1)} %collective-permute-done.first_ref.refs_1_, bf16[528,128]{1,0:T(8,128)(2,1)S(1)} %collective-permute-done.1.last_ref.refs_2_, ...), custom_call_target="tpu_custom_call" | custom-call | tf_op jit(solution)/shard_map/pallas_call | solution.py:265
  39.3 1.4 %collective-permute-start.17 = (f32[1,512]{1,0:T(1,128)S(1)}, f32[1,512]{1,0:T(1,128)S(1)}, u32[]{:S(2)}, u32[]{:S(2)}) collective-permute-start(f32[1,512]{1,0:T(1,128)S(1)} %get-tuple-element.54), channel_id=1, source_target_pairs={{0,1},{1,0},{2,3},{3,2},{4,5},{5,4},{6,7},{7,6},{8,9},{9,8},{10,11... | collective-permute-start | bytes 6152 | tf_op jit(solution)/shard_map/ppermute | solution.py:276
  41.2 1.8 %collective-permute-done.17 = f32[1,512]{1,0:T(1,128)S(1)} collective-permute-done((f32[1,512]{1,0:T(1,128)S(1)}, f32[1,512]{1,0:T(1,128)S(1)}, u32[]{:S(2)}, u32[]{:S(2)}) %collective-permute-start.17) | collective-permute-done | bytes 2080 | tf_op jit(solution)/shard_map/ppermute | solution.py:276
  43.8 1.1 %broadcast_multiply_fusion = f32[512,512]{1,0:T(8,128)} fusion(f32[512,512]{1,0:T(8,128)S(1)} %get-tuple-element.53, f32[512]{0:T(512)S(1)} %bitcast.8), kind=kLoop, calls=%fused_computation | loop fusion | flops 262144 | bytes 2099200 | tf_op jit(solution)/shard_map/mul | solution.py:278
  (30 shorter events, 5.8 us)
Async XLA Ops:
  0.0 0.9 %copy-start.1 = (bf16[8,1,1,128,128]{4,3,2,1,0:T(8,128)(2,1)S(1)}, bf16[8,1,1,128,128]{4,3,2,1,0:T(8,128)(2,1)}, u32[]{:S(2)}) copy-start(bf16[8,1,1,128,128]{4,3,2,1,0:T(8,128)(2,1)} %param.4) | copy-start | bytes 786436
  1.0 0.7 %copy-start.2 = (s32[8,1,1]{0,2,1:T(1,128)S(1)}, s32[8,1,1]{0,2,1:T(1,128)}, u32[]{:S(2)}) copy-start(s32[8,1,1]{0,2,1:T(1,128)} %param.3) | copy-start | bytes 100
  1.9 13.8 %collective-permute-start.7 = (bf16[4096,512]{1,0:T(8,128)(2,1)}, bf16[4096,512]{1,0:T(8,128)(2,1)S(1)}, u32[]{:S(2)}, u32[]{:S(2)}) collective-permute-start(bf16[4096,512]{1,0:T(8,128)(2,1)} %bitcast.4), channel_id=1, source_target_pairs={{0,16},{16,0},{1,17},{17,1},{2,18},{18,2},{3,19},{19,3},{4,20},{20... | collective-permute-start | bytes 12582920 | tf_op jit(solution)/shard_map/ppermute | solution.py:243
  2.5 7.2 %collective-permute-start.3 = (bf16[528,128]{1,0:T(8,128)(2,1)S(1)}, bf16[528,128]{1,0:T(8,128)(2,1)S(1)}, u32[]{:S(2)}, u32[]{:S(2)}) collective-permute-start(bf16[528,128]{1,0:T(8,128)(2,1)S(1)} %get-tuple-element.50.refs_0_), channel_id=1, source_target_pairs={{12,8},{8,4},{4,0},{0,2},{2,6},{6,10},{10,14},{14,12},{13,9},{9,5}... | collective-permute-start | bytes 405512 | tf_op jit(solution)/shard_map/ppermute | solution.py:258
  5.0 6.4 %collective-permute-start.4 = (bf16[528,128]{1,0:T(8,128)(2,1)S(1)}, bf16[528,128]{1,0:T(8,128)(2,1)S(1)}, u32[]{:S(2)}, u32[]{:S(2)}) collective-permute-start(bf16[528,128]{1,0:T(8,128)(2,1)S(1)} %get-tuple-element.50.refs_0_), channel_id=1, source_target_pairs={{12,14},{8,12},{4,8},{0,4},{2,0},{6,2},{10,6},{14,10},{13,15},{9,1... | collective-permute-start | bytes 405512 | tf_op jit(solution)/shard_map/ppermute | solution.py:258
  5.2 8.3 %collective-permute-start = (bf16[528,128]{1,0:T(8,128)(2,1)S(1)}, bf16[528,128]{1,0:T(8,128)(2,1)S(1)}, u32[]{:S(2)}, u32[]{:S(2)}) collective-permute-start(bf16[528,128]{1,0:T(8,128)(2,1)S(1)} %get-tuple-element.34.refs_0_), channel_id=1, source_target_pairs={{12,8},{8,4},{4,0},{0,2},{2,6},{6,10},{10,14},{14,12},{13,9},{9,5}... | collective-permute-start | bytes 405512 | tf_op jit(solution)/shard_map/ppermute | solution.py:258
  7.1 8.1 %collective-permute-start.1 = (bf16[528,128]{1,0:T(8,128)(2,1)S(1)}, bf16[528,128]{1,0:T(8,128)(2,1)S(1)}, u32[]{:S(2)}, u32[]{:S(2)}) collective-permute-start(bf16[528,128]{1,0:T(8,128)(2,1)S(1)} %get-tuple-element.34.refs_0_), channel_id=1, source_target_pairs={{12,14},{8,12},{4,8},{0,4},{2,0},{6,2},{10,6},{14,10},{13,15},{9,1... | collective-permute-start | bytes 405512 | tf_op jit(solution)/shard_map/ppermute | solution.py:258
  7.2 2.2 %copy-start = (bf16[1,4096,512]{2,1,0:T(8,128)(2,1)S(1)}, bf16[1,4096,512]{2,1,0:T(8,128)(2,1)}, u32[]{:S(2)}) copy-start(bf16[1,4096,512]{2,1,0:T(8,128)(2,1)} %param.5) | copy-start | bytes 12582916
  11.5 6.1 %collective-permute-start.5 = (bf16[528,128]{1,0:T(8,128)(2,1)S(1)}, bf16[528,128]{1,0:T(8,128)(2,1)S(1)}, u32[]{:S(2)}, u32[]{:S(2)}) collective-permute-start(bf16[528,128]{1,0:T(8,128)(2,1)S(1)} %collective-permute-done.3.first_ref.refs_1_), channel_id=1, source_target_pairs={{12,8},{8,4},{4,0},{0,2},{2,6},{6,10},{10,14},{14,12},{13,9},{9,5}... | collective-permute-start | bytes 405512 | tf_op jit(solution)/shard_map/ppermute | solution.py:258
  13.1 5.8 %collective-permute-start.6 = (bf16[528,128]{1,0:T(8,128)(2,1)S(1)}, bf16[528,128]{1,0:T(8,128)(2,1)S(1)}, u32[]{:S(2)}, u32[]{:S(2)}) collective-permute-start(bf16[528,128]{1,0:T(8,128)(2,1)S(1)} %collective-permute-done.4.last_ref.refs_2_), channel_id=1, source_target_pairs={{12,14},{8,12},{4,8},{0,4},{2,0},{6,2},{10,6},{14,10},{13,15},{9,1... | collective-permute-start | bytes 405512 | tf_op jit(solution)/shard_map/ppermute | solution.py:258
  13.5 9.8 %collective-permute-start.2 = (bf16[528,128]{1,0:T(8,128)(2,1)S(1)}, bf16[528,128]{1,0:T(8,128)(2,1)S(1)}, u32[]{:S(2)}, u32[]{:S(2)}) collective-permute-start(bf16[528,128]{1,0:T(8,128)(2,1)S(1)} %collective-permute-done.first_ref.refs_1_), channel_id=1, source_target_pairs={{12,8},{8,4},{4,0},{0,2},{2,6},{6,10},{10,14},{14,12},{13,9},{9,5}... | collective-permute-start | bytes 405512 | tf_op jit(solution)/shard_map/ppermute | solution.py:258
  15.2 8.2 %collective-permute-start.11 = (bf16[528,128]{1,0:T(8,128)(2,1)S(1)}, bf16[528,128]{1,0:T(8,128)(2,1)S(1)}, u32[]{:S(2)}, u32[]{:S(2)}) collective-permute-start(bf16[528,128]{1,0:T(8,128)(2,1)S(1)} %collective-permute-done.1.last_ref.refs_2_), channel_id=1, source_target_pairs={{12,14},{8,12},{4,8},{0,4},{2,0},{6,2},{10,6},{14,10},{13,15},{9,1... | collective-permute-start | bytes 405512 | tf_op jit(solution)/shard_map/ppermute | solution.py:258
  18.8 7.0 %collective-permute-start.10 = (bf16[528,128]{1,0:T(8,128)(2,1)S(1)}, bf16[528,128]{1,0:T(8,128)(2,1)S(1)}, u32[]{:S(2)}, u32[]{:S(2)}) collective-permute-start(bf16[528,128]{1,0:T(8,128)(2,1)S(1)} %shard_map.40), channel_id=1, source_target_pairs={{10,8},{6,4},{4,6},{8,10},{0,12},{12,0},{14,2},{2,14},{11,9},{7,5}... | collective-permute-start | bytes 405512 | tf_op jit(solution)/shard_map/ppermute | solution.py:255
  20.6 6.5 %collective-permute-start.8 = (bf16[528,128]{1,0:T(8,128)(2,1)S(1)}, bf16[528,128]{1,0:T(8,128)(2,1)S(1)}, u32[]{:S(2)}, u32[]{:S(2)}) collective-permute-start(bf16[528,128]{1,0:T(8,128)(2,1)S(1)} %collective-permute-done.5.refs_3_), channel_id=1, source_target_pairs={{12,8},{8,4},{4,0},{0,2},{2,6},{6,10},{10,14},{14,12},{13,9},{9,5}... | collective-permute-start | bytes 405512 | tf_op jit(solution)/shard_map/ppermute | solution.py:258
  22.2 5.0 %collective-permute-start.9 = (bf16[528,128]{1,0:T(8,128)(2,1)S(1)}, bf16[528,128]{1,0:T(8,128)(2,1)S(1)}, u32[]{:S(2)}, u32[]{:S(2)}) collective-permute-start(bf16[528,128]{1,0:T(8,128)(2,1)S(1)} %collective-permute-done.6.refs_4_), channel_id=1, source_target_pairs={{12,14},{8,12},{4,8},{0,4},{2,0},{6,2},{10,6},{14,10},{13,15},{9,1... | collective-permute-start | bytes 405512 | tf_op jit(solution)/shard_map/ppermute | solution.py:258
  28.2 9.9 %collective-permute-start.15 = (bf16[528,512]{1,0:T(8,128)(2,1)S(1)}, bf16[528,512]{1,0:T(8,128)(2,1)S(1)}, u32[]{:S(2)}, u32[]{:S(2)}) collective-permute-start(bf16[528,512]{1,0:T(8,128)(2,1)S(1)} %shard_map.43), channel_id=1, source_target_pairs={{0,1},{1,0},{2,3},{3,2},{4,5},{5,4},{6,7},{7,6},{8,9},{9,8},{10,11... | collective-permute-start | bytes 1622024 | tf_op jit(solution)/shard_map/ppermute | solution.py:249
  29.7 7.0 %collective-permute-start.14 = (bf16[528,128]{1,0:T(8,128)(2,1)S(1)}, bf16[528,128]{1,0:T(8,128)(2,1)S(1)}, u32[]{:S(2)}, u32[]{:S(2)}) collective-permute-start(bf16[528,128]{1,0:T(8,128)(2,1)S(1)} %shard_map.41), channel_id=1, source_target_pairs={{10,8},{6,4},{4,6},{8,10},{0,12},{12,0},{14,2},{2,14},{11,9},{7,5}... | collective-permute-start | bytes 405512 | tf_op jit(solution)/shard_map/ppermute | solution.py:255
  31.4 6.5 %collective-permute-start.12 = (bf16[528,128]{1,0:T(8,128)(2,1)S(1)}, bf16[528,128]{1,0:T(8,128)(2,1)S(1)}, u32[]{:S(2)}, u32[]{:S(2)}) collective-permute-start(bf16[528,128]{1,0:T(8,128)(2,1)S(1)} %collective-permute-done.2.refs_3_), channel_id=1, source_target_pairs={{12,8},{8,4},{4,0},{0,2},{2,6},{6,10},{10,14},{14,12},{13,9},{9,5}... | collective-permute-start | bytes 405512 | tf_op jit(solution)/shard_map/ppermute | solution.py:258
  33.1 5.0 %collective-permute-start.13 = (bf16[528,128]{1,0:T(8,128)(2,1)S(1)}, bf16[528,128]{1,0:T(8,128)(2,1)S(1)}, u32[]{:S(2)}, u32[]{:S(2)}) collective-permute-start(bf16[528,128]{1,0:T(8,128)(2,1)S(1)} %collective-permute-done.11.refs_4_), channel_id=1, source_target_pairs={{12,14},{8,12},{4,8},{0,4},{2,0},{6,2},{10,6},{14,10},{13,15},{9,1... | collective-permute-start | bytes 405512 | tf_op jit(solution)/shard_map/ppermute | solution.py:258
  39.3 1.9 %collective-permute-start.16 = (f32[1,512]{1,0:T(1,128)S(1)}, f32[1,512]{1,0:T(1,128)S(1)}, u32[]{:S(2)}, u32[]{:S(2)}) collective-permute-start(f32[1,512]{1,0:T(1,128)S(1)} %get-tuple-element.54), channel_id=1, source_target_pairs={{0,16},{16,0},{1,17},{17,1},{2,18},{18,2},{3,19},{19,3},{4,20},{20... | collective-permute-start | bytes 6152 | tf_op jit(solution)/shard_map/ppermute | solution.py:276
  39.3 3.7 %collective-permute-start.17 = (f32[1,512]{1,0:T(1,128)S(1)}, f32[1,512]{1,0:T(1,128)S(1)}, u32[]{:S(2)}, u32[]{:S(2)}) collective-permute-start(f32[1,512]{1,0:T(1,128)S(1)} %get-tuple-element.54), channel_id=1, source_target_pairs={{0,1},{1,0},{2,3},{3,2},{4,5},{5,4},{6,7},{7,6},{8,9},{9,8},{10,11... | collective-permute-start | bytes 6152 | tf_op jit(solution)/shard_map/ppermute | solution.py:276
  40.7 3.0 %collective-permute-start.18 = (f32[1,512]{1,0:T(1,128)S(1)}, f32[1,512]{1,0:T(1,128)S(1)}, u32[]{:S(2)}, u32[]{:S(2)}) collective-permute-start(f32[1,512]{1,0:T(1,128)S(1)} %get-tuple-element.54), channel_id=1, source_target_pairs={{0,17},{1,16},{16,1},{17,0},{2,19},{3,18},{18,3},{19,2},{4,21},{5,... | collective-permute-start | bytes 6152 | tf_op jit(solution)/shard_map/ppermute | solution.py:276

commit v9 on v8

--- a/solution.py
+++ b/solution.py
@@ -13,7 +13,7 @@
 ID_ROWS = 16
 LATE = 3
 VMEM_BYTES = 24 * 1024 * 1024
-PLAN = ("S=K=T", "O", "S1", "K1", "S=W", "Sp", "Kp", "S2", "K2", "J", "S=W=Sp=Kp", "S3", "Sm", "S=K", "C", "X", "K3", "Km")
+PLAN = ("S=K=T", "O", "S1", "K1", "S=W", "Sp", "Kp", "S2", "K2", "J", "S=W=Sp=Kp", "S3", "Sm", "S=K", "C", "X", "Km", "K3")
 
 
 def pack_kernel(cols_ref, vals_ref, *refs):
@@ -119,7 +119,7 @@
 
 
 def keep_kernel(slots, *refs):
-    items, (window, code_ref, square_ref, sum_ref) = refs[:slots], refs[slots:]
+    items, (window, early, code_ref, square_ref, sum_ref) = refs[:slots], refs[slots:]
     block = items[0].shape[1]
     rows = square_ref.shape[0]
     scale = code_ref[rows : rows + 1, :].astype(jnp.float32) * (1.0 / CODE_SPAN)
@@ -128,7 +128,7 @@
     def finish(j, value):
         code = code_ref[j * block : (j + 1) * block, :].astype(jnp.float32)
         size = (jnp.log(jnp.abs(code)) * LOG2E + CODE_MID) * scale
-        full = value + jnp.where(code < 0, -size, size)
+        full = value + early[j * block : (j + 1) * block, :] + jnp.where(code < 0, -size, size)
         square = full * full
         square_ref[j * block : (j + 1) * block, :] = square
         sums.append(jnp.sum(square, axis=0, keepdims=True))
@@ -263,15 +263,15 @@
             window = place(False, lax.ppermute(own, "row", swap), window)
             code = lax.ppermute(coded(sends, window), "layer", swap)
         square, sums = pl.pallas_call(
-            functools.partial(keep_kernel, size),
+            functools.partial(keep_kernel, LATE),
             out_shape=(
                 jax.ShapeDtypeStruct((rows, columns), jnp.float32),
                 jax.ShapeDtypeStruct((1, columns), jnp.float32),
             ),
-            in_specs=[vmem] * (size + 2),
+            in_specs=[vmem] * (LATE + 3),
             out_specs=(vmem, vmem),
             compiler_params=params,
-        )(*keeps, window, code)
+        )(*keeps[-LATE:], window, started(keeps[:-LATE], window, True), code)
         cross = [(0, 3), (1, 2), (2, 1), (3, 0)]
         sums = sums + lax.ppermute(sums, "row", swap) + lax.ppermute(sums, "layer", swap) + lax.ppermute(sums, ("row", "layer"), cross)
         total_rows = rows * lax.axis_size("row") * lax.axis_size("layer")

time: 45.1 us -> 44.8 us (level)
  waiting for transfers between devices: 15.6 us -> 14.8 us
  Pallas kernels: 3.84 us -> 4.33 us
    ppermute x2, waiting for transfers between devices: 5.65 us -> 4.89 us  [body(): lists[name[0]].append(lax.ppermute(chosen[name[0]], 'col', across))]
    pallas_call x1 -> x2, Pallas kernels: 0.76 us -> 1.52 us  [started(): pl.pallas_call(functools.partial(early_kernel, len(items), kept), out_sha...]
  transfers between devices with their start and end apart: 19 -> 19, of which waited for: 11 -> 11; matrix products, arithmetic and copies ran while one was open for 0% -> 0% of each run, Pallas kernels for 3% -> 5%
where the time goes in v9:
time: 44.8 us; the launch traced here: 44.6 us
  starting transfers between devices  20.4 us (46%)
  waiting for transfers between devices  14.8 us (33%)
  Pallas kernels  4.33 us (10%)
  local copies, waits for them, and re-layouts  3.79 us (8%)
  other arithmetic  1.11 us (2%)
    ppermute x12, starting transfers between devices, body(): lax.ppermute(e, 'col', shift(w))  13 us
    ppermute x12, waiting for transfers between devices, body(): lax.ppermute(e, 'col', shift(w))  7.39 us
    ppermute x2, waiting for transfers between devices, body(): lists[name[0]].append(lax.ppermute(chosen[name[0]], 'col', across))  4.89 us
    unnamed x6, local copies, waits for them, and re-layouts  3.79 us
    ppermute x2, starting transfers between devices, body(): lists[name[0]].append(lax.ppermute(chosen[name[0]], 'col', across))  3.44 us
    ppermute x1, waiting for transfers between devices, body(): lax.ppermute(sums, 'layer', swap)  1.78 us
    ppermute x1, starting transfers between devices, body(): code = lax.ppermute(code, 'layer', swap)  1.55 us
    pallas_call x2, Pallas kernels, started(): pl.pallas_call(functools.partial(early_kernel, len(items), kept), out_sha...  1.52 us
  transfers between devices with their start and end apart: 19, of which 11 were waited for; matrix products, arithmetic and copies ran while one was open for 0% of the time, Pallas kernels for 5%

profile of v9, /device:TPU:0, one launch (start us, length us, event | category | flops | bytes accessed | tf_op | source)
XLA Modules:
  0.0 44.6 jit_solution(638004006227719288)
XLA Ops:
  0.0 0.9 %copy-done.1 = bf16[8,1,1,128,128]{4,3,2,1,0:T(8,128)(2,1)S(1)} copy-done((bf16[8,1,1,128,128]{4,3,2,1,0:T(8,128)(2,1)S(1)}, bf16[8,1,1,128,128]{4,3,2,1,0:T(8,128)(2,1)}, u32[]{:S(2)}) %copy-start.1) | copy-done | bytes 262168
  2.5 2.6 %collective-permute-start = (bf16[528,128]{1,0:T(8,128)(2,1)S(1)}, bf16[528,128]{1,0:T(8,128)(2,1)S(1)}, u32[]{:S(2)}, u32[]{:S(2)}) collective-permute-start(bf16[528,128]{1,0:T(8,128)(2,1)S(1)} %get-tuple-element.50.refs_0_), channel_id=1, source_target_pairs={{12,8},{8,4},{4,0},{0,2},{2,6},{6,10},{10,14},{14,12},{13,9},{9,5}... | collective-permute-start | bytes 405512 | tf_op jit(solution)/shard_map/ppermute | solution.py:258
  5.2 1.9 %collective-permute-start.5 = (bf16[528,128]{1,0:T(8,128)(2,1)S(1)}, bf16[528,128]{1,0:T(8,128)(2,1)S(1)}, u32[]{:S(2)}, u32[]{:S(2)}) collective-permute-start(bf16[528,128]{1,0:T(8,128)(2,1)S(1)} %get-tuple-element.47.refs_0_), channel_id=1, source_target_pairs={{12,8},{8,4},{4,0},{0,2},{2,6},{6,10},{10,14},{14,12},{13,9},{9,5}... | collective-permute-start | bytes 405512 | tf_op jit(solution)/shard_map/ppermute | solution.py:258
  7.2 2.2 %copy-done = bf16[1,4096,512]{2,1,0:T(8,128)(2,1)S(1)} copy-done((bf16[1,4096,512]{2,1,0:T(8,128)(2,1)S(1)}, bf16[1,4096,512]{2,1,0:T(8,128)(2,1)}, u32[]{:S(2)}) %copy-start) | copy-done | bytes 4194328
  9.7 1.8 %collective-permute-done.1.last_ref.refs_2_ = bf16[528,128]{1,0:T(8,128)(2,1)S(1)} collective-permute-done((bf16[528,128]{1,0:T(8,128)(2,1)S(1)}, bf16[528,128]{1,0:T(8,128)(2,1)S(1)}, u32[]{:S(2)}, u32[]{:S(2)}) %collective-permute-start.1) | collective-permute-done | bytes 135200 | tf_op jit(solution)/shard_map/ppermute | solution.py:258
  11.5 1.6 %collective-permute-start.2 = (bf16[528,128]{1,0:T(8,128)(2,1)S(1)}, bf16[528,128]{1,0:T(8,128)(2,1)S(1)}, u32[]{:S(2)}, u32[]{:S(2)}) collective-permute-start(bf16[528,128]{1,0:T(8,128)(2,1)S(1)} %collective-permute-done.first_ref.refs_1_), channel_id=1, source_target_pairs={{12,8},{8,4},{4,0},{0,2},{2,6},{6,10},{10,14},{14,12},{13,9},{9,5}... | collective-permute-start | bytes 405512 | tf_op jit(solution)/shard_map/ppermute | solution.py:258
  13.5 1.6 %collective-permute-start.11 = (bf16[528,128]{1,0:T(8,128)(2,1)S(1)}, bf16[528,128]{1,0:T(8,128)(2,1)S(1)}, u32[]{:S(2)}, u32[]{:S(2)}) collective-permute-start(bf16[528,128]{1,0:T(8,128)(2,1)S(1)} %collective-permute-done.5.first_ref.refs_1_), channel_id=1, source_target_pairs={{12,8},{8,4},{4,0},{0,2},{2,6},{6,10},{10,14},{14,12},{13,9},{9,5}... | collective-permute-start | bytes 405512 | tf_op jit(solution)/shard_map/ppermute | solution.py:258
  16.0 1.5 %collective-permute-done.2.refs_3_ = bf16[528,128]{1,0:T(8,128)(2,1)S(1)} collective-permute-done((bf16[528,128]{1,0:T(8,128)(2,1)S(1)}, bf16[528,128]{1,0:T(8,128)(2,1)S(1)}, u32[]{:S(2)}, u32[]{:S(2)}) %collective-permute-start.2) | collective-permute-done | bytes 135200 | tf_op jit(solution)/shard_map/ppermute | solution.py:258
  17.5 1.3 %collective-permute-done.3.refs_4_ = bf16[528,128]{1,0:T(8,128)(2,1)S(1)} collective-permute-done((bf16[528,128]{1,0:T(8,128)(2,1)S(1)}, bf16[528,128]{1,0:T(8,128)(2,1)S(1)}, u32[]{:S(2)}, u32[]{:S(2)}) %collective-permute-start.3) | collective-permute-done | bytes 135200 | tf_op jit(solution)/shard_map/ppermute | solution.py:258
  18.8 1.8 %collective-permute-start.10 = (bf16[528,128]{1,0:T(8,128)(2,1)S(1)}, bf16[528,128]{1,0:T(8,128)(2,1)S(1)}, u32[]{:S(2)}, u32[]{:S(2)}) collective-permute-start(bf16[528,128]{1,0:T(8,128)(2,1)S(1)} %shard_map.40), channel_id=1, source_target_pairs={{10,8},{6,4},{4,6},{8,10},{0,12},{12,0},{14,2},{2,14},{11,9},{7,5}... | collective-permute-start | bytes 405512 | tf_op jit(solution)/shard_map/ppermute | solution.py:255
  20.6 1.6 %collective-permute-start.8 = (bf16[528,128]{1,0:T(8,128)(2,1)S(1)}, bf16[528,128]{1,0:T(8,128)(2,1)S(1)}, u32[]{:S(2)}, u32[]{:S(2)}) collective-permute-start(bf16[528,128]{1,0:T(8,128)(2,1)S(1)} %collective-permute-done.2.refs_3_), channel_id=1, source_target_pairs={{12,8},{8,4},{4,0},{0,2},{2,6},{6,10},{10,14},{14,12},{13,9},{9,5}... | collective-permute-start | bytes 405512 | tf_op jit(solution)/shard_map/ppermute | solution.py:258
  23.4 2.4 %collective-permute-done.10.refs_2_ = bf16[528,128]{1,0:T(8,128)(2,1)S(1)} collective-permute-done((bf16[528,128]{1,0:T(8,128)(2,1)S(1)}, bf16[528,128]{1,0:T(8,128)(2,1)S(1)}, u32[]{:S(2)}, u32[]{:S(2)}) %collective-permute-start.10) | collective-permute-done | bytes 135200 | tf_op jit(solution)/shard_map/ppermute | solution.py:255
  25.8 1.3 %collective-permute-done.8.refs_0_ = bf16[528,128]{1,0:T(8,128)(2,1)S(1)} collective-permute-done((bf16[528,128]{1,0:T(8,128)(2,1)S(1)}, bf16[528,128]{1,0:T(8,128)(2,1)S(1)}, u32[]{:S(2)}, u32[]{:S(2)}) %collective-permute-start.8) | collective-permute-done | bytes 135200 | tf_op jit(solution)/shard_map/ppermute | solution.py:258
  27.2 1.0 %shard_map.44 = bf16[528,512]{1,0:T(8,128)(2,1)S(1)} custom-call(bf16[528,128]{1,0:T(8,128)(2,1)S(1)} %collective-permute-done.8.refs_0_, bf16[528,128]{1,0:T(8,128)(2,1)S(1)} %collective-permute-done.9.refs_1_, bf16[528,128]{1,0:T(8,128)(2,1)S(1)} %collective-permute-done.10.refs_2_, bf16[8192,512]{1,0:T(8,128)(2,1)S(1)} %shard_map.39.refs_5_.refs_3_, ...), custom_call_target="tpu_custom_call" | custom-call | tf_op jit(solution)/shard_map/pallas_call | solution.py:204
  28.2 1.6 %collective-permute-start.15 = (bf16[528,512]{1,0:T(8,128)(2,1)S(1)}, bf16[528,512]{1,0:T(8,128)(2,1)S(1)}, u32[]{:S(2)}, u32[]{:S(2)}) collective-permute-start(bf16[528,512]{1,0:T(8,128)(2,1)S(1)} %shard_map.44), channel_id=1, source_target_pairs={{0,1},{1,0},{2,3},{3,2},{4,5},{5,4},{6,7},{7,6},{8,9},{9,8},{10,11... | collective-permute-start | bytes 1622024 | tf_op jit(solution)/shard_map/ppermute | solution.py:249
  29.7 1.7 %collective-permute-start.7 = (bf16[528,128]{1,0:T(8,128)(2,1)S(1)}, bf16[528,128]{1,0:T(8,128)(2,1)S(1)}, u32[]{:S(2)}, u32[]{:S(2)}) collective-permute-start(bf16[528,128]{1,0:T(8,128)(2,1)S(1)} %shard_map.41), channel_id=1, source_target_pairs={{10,8},{6,4},{4,6},{8,10},{0,12},{12,0},{14,2},{2,14},{11,9},{7,5}... | collective-permute-start | bytes 405512 | tf_op jit(solution)/shard_map/ppermute | solution.py:255
  31.4 1.7 %collective-permute-start.13 = (bf16[528,128]{1,0:T(8,128)(2,1)S(1)}, bf16[528,128]{1,0:T(8,128)(2,1)S(1)}, u32[]{:S(2)}, u32[]{:S(2)}) collective-permute-start(bf16[528,128]{1,0:T(8,128)(2,1)S(1)} %collective-permute-done.11.refs_3_), channel_id=1, source_target_pairs={{12,8},{8,4},{4,0},{0,2},{2,6},{6,10},{10,14},{14,12},{13,9},{9,5}... | collective-permute-start | bytes 405512 | tf_op jit(solution)/shard_map/ppermute | solution.py:258
  34.2 2.5 %collective-permute-done.7.refs_0_ = bf16[528,128]{1,0:T(8,128)(2,1)S(1)} collective-permute-done((bf16[528,128]{1,0:T(8,128)(2,1)S(1)}, bf16[528,128]{1,0:T(8,128)(2,1)S(1)}, u32[]{:S(2)}, u32[]{:S(2)}) %collective-permute-start.7) | collective-permute-done | bytes 135200 | tf_op jit(solution)/shard_map/ppermute | solution.py:255
  36.7 1.2 %collective-permute-done.13.refs_1_ = bf16[528,128]{1,0:T(8,128)(2,1)S(1)} collective-permute-done((bf16[528,128]{1,0:T(8,128)(2,1)S(1)}, bf16[528,128]{1,0:T(8,128)(2,1)S(1)}, u32[]{:S(2)}, u32[]{:S(2)}) %collective-permute-start.13) | collective-permute-done | bytes 135200 | tf_op jit(solution)/shard_map/ppermute | solution.py:258
  38.1 0.9 %shard_map.45 = (f32[512,512]{1,0:T(8,128)S(1)}, f32[1,512]{1,0:T(1,128)S(1)}) custom-call(bf16[528,128]{1,0:T(8,128)(2,1)S(1)} %collective-permute-done.7.refs_0_, bf16[528,128]{1,0:T(8,128)(2,1)S(1)} %collective-permute-done.13.refs_1_, bf16[528,128]{1,0:T(8,128)(2,1)S(1)} %collective-permute-done.14.refs_2_, ...), custom_call_target="tpu_custom_call" | custom-call | tf_op jit(solution)/shard_map/pallas_call | solution.py:265
  39.1 1.4 %collective-permute-start.17 = (f32[1,512]{1,0:T(1,128)S(1)}, f32[1,512]{1,0:T(1,128)S(1)}, u32[]{:S(2)}, u32[]{:S(2)}) collective-permute-start(f32[1,512]{1,0:T(1,128)S(1)} %get-tuple-element.54), channel_id=1, source_target_pairs={{0,1},{1,0},{2,3},{3,2},{4,5},{5,4},{6,7},{7,6},{8,9},{9,8},{10,11... | collective-permute-start | bytes 6152 | tf_op jit(solution)/shard_map/ppermute | solution.py:276
  40.9 1.8 %collective-permute-done.17 = f32[1,512]{1,0:T(1,128)S(1)} collective-permute-done((f32[1,512]{1,0:T(1,128)S(1)}, f32[1,512]{1,0:T(1,128)S(1)}, u32[]{:S(2)}, u32[]{:S(2)}) %collective-permute-start.17) | collective-permute-done | bytes 2080 | tf_op jit(solution)/shard_map/ppermute | solution.py:276
  42.7 0.8 %collective-permute-done.18 = f32[1,512]{1,0:T(1,128)S(1)} collective-permute-done((f32[1,512]{1,0:T(1,128)S(1)}, f32[1,512]{1,0:T(1,128)S(1)}, u32[]{:S(2)}, u32[]{:S(2)}) %collective-permute-start.18) | collective-permute-done | bytes 2080 | tf_op jit(solution)/shard_map/ppermute | solution.py:276
  43.5 1.1 %broadcast_multiply_fusion = f32[512,512]{1,0:T(8,128)} fusion(f32[512,512]{1,0:T(8,128)S(1)} %get-tuple-element.53, f32[512]{0:T(512)S(1)} %bitcast.8), kind=kLoop, calls=%fused_computation | loop fusion | flops 262144 | bytes 2099200 | tf_op jit(solution)/shard_map/mul | solution.py:278
  (31 shorter events, 6.6 us)
Async XLA Ops:
  0.0 0.9 %copy-start.1 = (bf16[8,1,1,128,128]{4,3,2,1,0:T(8,128)(2,1)S(1)}, bf16[8,1,1,128,128]{4,3,2,1,0:T(8,128)(2,1)}, u32[]{:S(2)}) copy-start(bf16[8,1,1,128,128]{4,3,2,1,0:T(8,128)(2,1)} %param.4) | copy-start | bytes 786436
  1.0 0.7 %copy-start.2 = (s32[8,1,1]{0,2,1:T(1,128)S(1)}, s32[8,1,1]{0,2,1:T(1,128)}, u32[]{:S(2)}) copy-start(s32[8,1,1]{0,2,1:T(1,128)} %param.3) | copy-start | bytes 100
  1.9 13.8 %collective-permute-start.4 = (bf16[4096,512]{1,0:T(8,128)(2,1)}, bf16[4096,512]{1,0:T(8,128)(2,1)S(1)}, u32[]{:S(2)}, u32[]{:S(2)}) collective-permute-start(bf16[4096,512]{1,0:T(8,128)(2,1)} %bitcast.4), channel_id=1, source_target_pairs={{0,16},{16,0},{1,17},{17,1},{2,18},{18,2},{3,19},{19,3},{4,20},{20... | collective-permute-start | bytes 12582920 | tf_op jit(solution)/shard_map/ppermute | solution.py:243
  2.5 7.2 %collective-permute-start = (bf16[528,128]{1,0:T(8,128)(2,1)S(1)}, bf16[528,128]{1,0:T(8,128)(2,1)S(1)}, u32[]{:S(2)}, u32[]{:S(2)}) collective-permute-start(bf16[528,128]{1,0:T(8,128)(2,1)S(1)} %get-tuple-element.50.refs_0_), channel_id=1, source_target_pairs={{12,8},{8,4},{4,0},{0,2},{2,6},{6,10},{10,14},{14,12},{13,9},{9,5}... | collective-permute-start | bytes 405512 | tf_op jit(solution)/shard_map/ppermute | solution.py:258
  5.0 6.4 %collective-permute-start.1 = (bf16[528,128]{1,0:T(8,128)(2,1)S(1)}, bf16[528,128]{1,0:T(8,128)(2,1)S(1)}, u32[]{:S(2)}, u32[]{:S(2)}) collective-permute-start(bf16[528,128]{1,0:T(8,128)(2,1)S(1)} %get-tuple-element.50.refs_0_), channel_id=1, source_target_pairs={{12,14},{8,12},{4,8},{0,4},{2,0},{6,2},{10,6},{14,10},{13,15},{9,1... | collective-permute-start | bytes 405512 | tf_op jit(solution)/shard_map/ppermute | solution.py:258
  5.2 8.3 %collective-permute-start.5 = (bf16[528,128]{1,0:T(8,128)(2,1)S(1)}, bf16[528,128]{1,0:T(8,128)(2,1)S(1)}, u32[]{:S(2)}, u32[]{:S(2)}) collective-permute-start(bf16[528,128]{1,0:T(8,128)(2,1)S(1)} %get-tuple-element.47.refs_0_), channel_id=1, source_target_pairs={{12,8},{8,4},{4,0},{0,2},{2,6},{6,10},{10,14},{14,12},{13,9},{9,5}... | collective-permute-start | bytes 405512 | tf_op jit(solution)/shard_map/ppermute | solution.py:258
  7.1 8.1 %collective-permute-start.6 = (bf16[528,128]{1,0:T(8,128)(2,1)S(1)}, bf16[528,128]{1,0:T(8,128)(2,1)S(1)}, u32[]{:S(2)}, u32[]{:S(2)}) collective-permute-start(bf16[528,128]{1,0:T(8,128)(2,1)S(1)} %get-tuple-element.47.refs_0_), channel_id=1, source_target_pairs={{12,14},{8,12},{4,8},{0,4},{2,0},{6,2},{10,6},{14,10},{13,15},{9,1... | collective-permute-start | bytes 405512 | tf_op jit(solution)/shard_map/ppermute | solution.py:258
  7.2 2.2 %copy-start = (bf16[1,4096,512]{2,1,0:T(8,128)(2,1)S(1)}, bf16[1,4096,512]{2,1,0:T(8,128)(2,1)}, u32[]{:S(2)}) copy-start(bf16[1,4096,512]{2,1,0:T(8,128)(2,1)} %param.5) | copy-start | bytes 12582916
  11.5 6.1 %collective-permute-start.2 = (bf16[528,128]{1,0:T(8,128)(2,1)S(1)}, bf16[528,128]{1,0:T(8,128)(2,1)S(1)}, u32[]{:S(2)}, u32[]{:S(2)}) collective-permute-start(bf16[528,128]{1,0:T(8,128)(2,1)S(1)} %collective-permute-done.first_ref.refs_1_), channel_id=1, source_target_pairs={{12,8},{8,4},{4,0},{0,2},{2,6},{6,10},{10,14},{14,12},{13,9},{9,5}... | collective-permute-start | bytes 405512 | tf_op jit(solution)/shard_map/ppermute | solution.py:258
  13.1 5.8 %collective-permute-start.3 = (bf16[528,128]{1,0:T(8,128)(2,1)S(1)}, bf16[528,128]{1,0:T(8,128)(2,1)S(1)}, u32[]{:S(2)}, u32[]{:S(2)}) collective-permute-start(bf16[528,128]{1,0:T(8,128)(2,1)S(1)} %collective-permute-done.1.last_ref.refs_2_), channel_id=1, source_target_pairs={{12,14},{8,12},{4,8},{0,4},{2,0},{6,2},{10,6},{14,10},{13,15},{9,1... | collective-permute-start | bytes 405512 | tf_op jit(solution)/shard_map/ppermute | solution.py:258
  13.5 9.8 %collective-permute-start.11 = (bf16[528,128]{1,0:T(8,128)(2,1)S(1)}, bf16[528,128]{1,0:T(8,128)(2,1)S(1)}, u32[]{:S(2)}, u32[]{:S(2)}) collective-permute-start(bf16[528,128]{1,0:T(8,128)(2,1)S(1)} %collective-permute-done.5.first_ref.refs_1_), channel_id=1, source_target_pairs={{12,8},{8,4},{4,0},{0,2},{2,6},{6,10},{10,14},{14,12},{13,9},{9,5}... | collective-permute-start | bytes 405512 | tf_op jit(solution)/shard_map/ppermute | solution.py:258
  15.2 8.2 %collective-permute-start.12 = (bf16[528,128]{1,0:T(8,128)(2,1)S(1)}, bf16[528,128]{1,0:T(8,128)(2,1)S(1)}, u32[]{:S(2)}, u32[]{:S(2)}) collective-permute-start(bf16[528,128]{1,0:T(8,128)(2,1)S(1)} %collective-permute-done.6.last_ref.refs_2_), channel_id=1, source_target_pairs={{12,14},{8,12},{4,8},{0,4},{2,0},{6,2},{10,6},{14,10},{13,15},{9,1... | collective-permute-start | bytes 405512 | tf_op jit(solution)/shard_map/ppermute | solution.py:258
  18.8 7.0 %collective-permute-start.10 = (bf16[528,128]{1,0:T(8,128)(2,1)S(1)}, bf16[528,128]{1,0:T(8,128)(2,1)S(1)}, u32[]{:S(2)}, u32[]{:S(2)}) collective-permute-start(bf16[528,128]{1,0:T(8,128)(2,1)S(1)} %shard_map.40), channel_id=1, source_target_pairs={{10,8},{6,4},{4,6},{8,10},{0,12},{12,0},{14,2},{2,14},{11,9},{7,5}... | collective-permute-start | bytes 405512 | tf_op jit(solution)/shard_map/ppermute | solution.py:255
  20.6 6.5 %collective-permute-start.8 = (bf16[528,128]{1,0:T(8,128)(2,1)S(1)}, bf16[528,128]{1,0:T(8,128)(2,1)S(1)}, u32[]{:S(2)}, u32[]{:S(2)}) collective-permute-start(bf16[528,128]{1,0:T(8,128)(2,1)S(1)} %collective-permute-done.2.refs_3_), channel_id=1, source_target_pairs={{12,8},{8,4},{4,0},{0,2},{2,6},{6,10},{10,14},{14,12},{13,9},{9,5}... | collective-permute-start | bytes 405512 | tf_op jit(solution)/shard_map/ppermute | solution.py:258
  22.2 5.0 %collective-permute-start.9 = (bf16[528,128]{1,0:T(8,128)(2,1)S(1)}, bf16[528,128]{1,0:T(8,128)(2,1)S(1)}, u32[]{:S(2)}, u32[]{:S(2)}) collective-permute-start(bf16[528,128]{1,0:T(8,128)(2,1)S(1)} %collective-permute-done.3.refs_4_), channel_id=1, source_target_pairs={{12,14},{8,12},{4,8},{0,4},{2,0},{6,2},{10,6},{14,10},{13,15},{9,1... | collective-permute-start | bytes 405512 | tf_op jit(solution)/shard_map/ppermute | solution.py:258
  28.2 9.9 %collective-permute-start.15 = (bf16[528,512]{1,0:T(8,128)(2,1)S(1)}, bf16[528,512]{1,0:T(8,128)(2,1)S(1)}, u32[]{:S(2)}, u32[]{:S(2)}) collective-permute-start(bf16[528,512]{1,0:T(8,128)(2,1)S(1)} %shard_map.44), channel_id=1, source_target_pairs={{0,1},{1,0},{2,3},{3,2},{4,5},{5,4},{6,7},{7,6},{8,9},{9,8},{10,11... | collective-permute-start | bytes 1622024 | tf_op jit(solution)/shard_map/ppermute | solution.py:249
  29.7 7.0 %collective-permute-start.7 = (bf16[528,128]{1,0:T(8,128)(2,1)S(1)}, bf16[528,128]{1,0:T(8,128)(2,1)S(1)}, u32[]{:S(2)}, u32[]{:S(2)}) collective-permute-start(bf16[528,128]{1,0:T(8,128)(2,1)S(1)} %shard_map.41), channel_id=1, source_target_pairs={{10,8},{6,4},{4,6},{8,10},{0,12},{12,0},{14,2},{2,14},{11,9},{7,5}... | collective-permute-start | bytes 405512 | tf_op jit(solution)/shard_map/ppermute | solution.py:255
  31.4 6.5 %collective-permute-start.13 = (bf16[528,128]{1,0:T(8,128)(2,1)S(1)}, bf16[528,128]{1,0:T(8,128)(2,1)S(1)}, u32[]{:S(2)}, u32[]{:S(2)}) collective-permute-start(bf16[528,128]{1,0:T(8,128)(2,1)S(1)} %collective-permute-done.11.refs_3_), channel_id=1, source_target_pairs={{12,8},{8,4},{4,0},{0,2},{2,6},{6,10},{10,14},{14,12},{13,9},{9,5}... | collective-permute-start | bytes 405512 | tf_op jit(solution)/shard_map/ppermute | solution.py:258
  33.1 5.0 %collective-permute-start.14 = (bf16[528,128]{1,0:T(8,128)(2,1)S(1)}, bf16[528,128]{1,0:T(8,128)(2,1)S(1)}, u32[]{:S(2)}, u32[]{:S(2)}) collective-permute-start(bf16[528,128]{1,0:T(8,128)(2,1)S(1)} %collective-permute-done.12.refs_4_), channel_id=1, source_target_pairs={{12,14},{8,12},{4,8},{0,4},{2,0},{6,2},{10,6},{14,10},{13,15},{9,1... | collective-permute-start | bytes 405512 | tf_op jit(solution)/shard_map/ppermute | solution.py:258
  39.0 1.9 %collective-permute-start.16 = (f32[1,512]{1,0:T(1,128)S(1)}, f32[1,512]{1,0:T(1,128)S(1)}, u32[]{:S(2)}, u32[]{:S(2)}) collective-permute-start(f32[1,512]{1,0:T(1,128)S(1)} %get-tuple-element.54), channel_id=1, source_target_pairs={{0,16},{16,0},{1,17},{17,1},{2,18},{18,2},{3,19},{19,3},{4,20},{20... | collective-permute-start | bytes 6152 | tf_op jit(solution)/shard_map/ppermute | solution.py:276
  39.1 3.7 %collective-permute-start.17 = (f32[1,512]{1,0:T(1,128)S(1)}, f32[1,512]{1,0:T(1,128)S(1)}, u32[]{:S(2)}, u32[]{:S(2)}) collective-permute-start(f32[1,512]{1,0:T(1,128)S(1)} %get-tuple-element.54), channel_id=1, source_target_pairs={{0,1},{1,0},{2,3},{3,2},{4,5},{5,4},{6,7},{7,6},{8,9},{9,8},{10,11... | collective-permute-start | bytes 6152 | tf_op jit(solution)/shard_map/ppermute | solution.py:276
  40.5 3.0 %collective-permute-start.18 = (f32[1,512]{1,0:T(1,128)S(1)}, f32[1,512]{1,0:T(1,128)S(1)}, u32[]{:S(2)}, u32[]{:S(2)}) collective-permute-start(f32[1,512]{1,0:T(1,128)S(1)} %get-tuple-element.54), channel_id=1, source_target_pairs={{0,17},{1,16},{16,1},{17,0},{2,19},{3,18},{18,3},{19,2},{4,21},{5,... | collective-permute-start | bytes 6152 | tf_op jit(solution)/shard_map/ppermute | solution.py:276
